TPU v7x, 512 devices: a whole 4x4x16 slice. The times are simulated.
512 devices in a mesh: dp: 32 (over y_lo, z), fsdp: 16 (over y_hi, x, core).
Axes of the slice: x: 4, y: 4 (y_hi: 2, y_lo: 2; y = y_hi * 2 + y_lo), z: 16, core: 2. Of those that a mesh axis runs over, the one named last changes fastest.
Arguments:
- policy_out: bfloat16 [640, 2560], P('fsdp'), may hold values from -0.25 to 0.25
- frozen_out: bfloat16 [640, 2560], P('fsdp'), may hold values from -0.25 to 0.25
- qkv_current: bfloat16 [131072, 896], P(('dp', 'fsdp')), may hold values from -8.125 to 8.125
- segment_current: int32 [131072], P(('dp', 'fsdp')), may hold values from 0 to 15, as said below
- grad_output: bfloat16 [131072, 2560], P(('dp', 'fsdp')), may hold values from -6 to 6
- query_key_value_next: bfloat16 [131072, 896], P(('dp', 'fsdp')), may hold values from -8.125 to 8.125
- document_next: int32 [131072], P(('dp', 'fsdp')), may hold values from 0 to 15, as said below
- block_counts: int32 [32, 16], P('dp', 'fsdp'), may hold values from 0 to 2, as said below
- move_plan: int32 [32, 16, 5], P('dp', 'fsdp'), may hold values from 0 to 1, as said below
Outputs:
- qkv_gradient: bfloat16 [131072, 896], P(('dp', 'fsdp'))
- weight_grad: bfloat16 [640, 2560], P('fsdp')
- frozen_layer_output: bfloat16 [131072, 2560], P(('dp', 'fsdp'))
Inputs may be any that keep to these rules, and one draw needn't show every extreme that they name: `segment_current`: within each aligned block of 128 rows the ids start at 0, never fall, and change only at multiples of 8 rows. `document_next`: within each aligned block of 128 rows the ids start at 0, never fall, and change only at multiples of 8 rows. `block_counts`: A device's live blocks are its first slots. `move_plan`: of two partners at a step at most one sends; no device ever holds more than 2 or fewer than 0 live blocks.
All inputs are finite; a program needn't handle non-finite values.
Results may differ from a plain program's by a relative error of at most 0.019.
Values may be sent and summed in bfloat16 or wider, within the bound.
No kernel may reach another device: no remote copies, remote signals or barrier semaphores. Data moves between devices by JAX's collectives and lax.ppermute only.
A program may use at most 64 MiB of HBM per device.

v0:
```python
import math

import jax
import jax.numpy as jnp
from jax import lax
from jax.sharding import PartitionSpec as P

HD = 128
HQ = 5
ALIGNED_ROWS = 128
SLOT_NUMBER = 2


masked_score = -1e30


def as_sent(shard):
    return jax.tree.map(lambda a: a.astype(jnp.bfloat16) if a.dtype == jnp.float32 else a, shard)


def from_partner(shard, axis, stride):
    return lax.ppermute(shard, axis, [(i, i ^ 1 << stride) for i in range(lax.axis_size(axis))])


def split_heads(qkv_rows):
    blocks = qkv_rows.shape[0] // ALIGNED_ROWS
    query_width = HQ * HD
    query_matrix = qkv_rows[:, :query_width].reshape(blocks, ALIGNED_ROWS, HQ, HD)
    key_matrix = qkv_rows[:, query_width : query_width + HD].reshape(blocks, ALIGNED_ROWS, HD)
    value_matrix = qkv_rows[:, query_width + HD :].reshape(blocks, ALIGNED_ROWS, HD)
    return (query_matrix, key_matrix, value_matrix)


def attend_over_blocks(qkv_rows, segment_ids):
    query_matrix, key_matrix, value_matrix = split_heads(qkv_rows)
    blocks = query_matrix.shape[0]
    scale_multiplier = 1.0 / math.sqrt(HD)
    score_matrix = (
        jnp.einsum("ofam,ozm->oafz", query_matrix, key_matrix, preferred_element_type=jnp.float32)
        * scale_multiplier
    )
    positions = jnp.arange(ALIGNED_ROWS)
    segment_block = segment_ids.reshape(blocks, ALIGNED_ROWS)
    allowed = (positions[:, None] >= positions[None, :])[None] & (
        segment_block[:, :, None] == segment_block[:, None, :]
    )
    score_matrix = jnp.where(allowed[:, None], score_matrix, masked_score)
    row_max = jnp.max(score_matrix, axis=-1, keepdims=True)
    exp_scores = jnp.exp(score_matrix - row_max)
    softmax_full = exp_scores / jnp.sum(exp_scores, axis=-1, keepdims=True)
    softmax_reduced = softmax_full.astype(jnp.bfloat16)
    output_rows = jnp.einsum(
        "gpsa,gan->gspn", softmax_reduced, value_matrix, preferred_element_type=jnp.float32
    )
    attention_map = output_rows.reshape(blocks * ALIGNED_ROWS, HQ * HD).astype(jnp.bfloat16)
    return (attention_map, softmax_full, softmax_reduced)


def attend_backward(qkv_rows, softmax_full, softmax_reduced, grad_attention):
    query_matrix, key_matrix, value_matrix = split_heads(qkv_rows)
    blocks = query_matrix.shape[0]
    scale_multiplier = 1.0 / math.sqrt(HD)
    output_gradient = grad_attention.reshape(blocks, ALIGNED_ROWS, HQ, HD)
    probability_gradient = jnp.einsum(
        "ofam,ozm->oafz", output_gradient, value_matrix, preferred_element_type=jnp.float32
    )
    centre = jnp.sum(softmax_full * probability_gradient, axis=-1, keepdims=True)
    score_gradient = softmax_full * (probability_gradient - centre)
    query_gradient = (
        jnp.einsum(
            "gpsa,gan->gspn",
            score_gradient,
            key_matrix.astype(jnp.float32),
            precision=lax.Precision.HIGHEST,
            preferred_element_type=jnp.float32,
        )
        * scale_multiplier
    )
    key_gradient = (
        jnp.einsum(
            "xzrl,xrzw->xlw",
            score_gradient,
            query_matrix.astype(jnp.float32),
            precision=lax.Precision.HIGHEST,
            preferred_element_type=jnp.float32,
        )
        * scale_multiplier
    )
    value_gradient = jnp.einsum(
        "xzrl,xrzw->xlw", softmax_reduced, output_gradient, preferred_element_type=jnp.float32
    )
    row_count = blocks * ALIGNED_ROWS
    joined = jnp.concatenate(
        [
            query_gradient.reshape(row_count, HQ * HD),
            key_gradient.reshape(row_count, HD),
            value_gradient.reshape(row_count, HD),
        ],
        axis=1,
    )
    return joined.astype(jnp.bfloat16)


def take_outgoing(slot_contents, top_start, send_count):
    slot_index = jnp.clip(top_start + 0, 0, slot_contents.shape[0] - 1).astype(jnp.int32)
    chosen_block = lax.dynamic_index_in_dim(slot_contents, slot_index, 0, keepdims=False)
    pieces = [jnp.where(0 < send_count, chosen_block, jnp.zeros_like(chosen_block))]
    return jnp.stack(pieces)


def place_incoming(slot_contents, incoming, top_start, recv_count):
    slot_ids = jnp.arange(slot_contents.shape[0])
    hit_mask = (slot_ids == top_start + 0) & (0 < recv_count)
    hit_mask = hit_mask.reshape((-1,) + (1,) * (slot_contents.ndim - 1))
    slot_contents = jnp.where(hit_mask, incoming[0][None], slot_contents)
    return slot_contents


def body(
    policy_out,
    frozen_out,
    qkv_current,
    segment_current,
    grad_output,
    query_key_value_next,
    document_next,
    block_counts,
    move_plan,
):
    fsdp_count = lax.axis_size("fsdp")
    group_count = lax.axis_size("dp")
    contract_last = (((1,), (1,)), ((), ()))
    grad_attention = lax.dot_general(
        grad_output,
        lax.all_gather(policy_out, "fsdp", axis=0, tiled=True),
        contract_last,
        preferred_element_type=jnp.float32,
    ).astype(jnp.bfloat16)
    frozen_complete = lax.all_gather(frozen_out, "fsdp", axis=0, tiled=True)
    attention_map, softmax_full, softmax_reduced = attend_over_blocks(qkv_current, segment_current)
    qkv_gradient = attend_backward(qkv_current, softmax_full, softmax_reduced, grad_attention)
    group_part = lax.psum_scatter(
        lax.dot_general(
            attention_map, grad_output, (((0,), (0,)), ((), ())), preferred_element_type=jnp.float32
        ).astype(jnp.bfloat16),
        "fsdp",
        scatter_dimension=0,
        tiled=True,
    ).astype(jnp.float32)
    scale_total = 1.0 / (group_count * fsdp_count)
    total_grad = lax.psum(group_part, "dp")
    weight_grad = (total_grad * scale_total).astype(jnp.bfloat16)
    slot_contents = query_key_value_next.reshape(
        SLOT_NUMBER, ALIGNED_ROWS, query_key_value_next.shape[1]
    )
    slot_documents = document_next.reshape(SLOT_NUMBER, ALIGNED_ROWS)
    live_tally_count = block_counts[0, 0]
    plan_row = move_plan[0, 0]
    levels = group_count.bit_length() - 1
    empty_rows = jnp.zeros((SLOT_NUMBER, ALIGNED_ROWS, frozen_complete.shape[1]), jnp.bfloat16)
    for level in range(levels):
        send_count = plan_row[level]
        top_start = live_tally_count - send_count
        out_data = take_outgoing(slot_contents, top_start, send_count)
        out_segments = take_outgoing(slot_documents, top_start, send_count)
        in_data, in_segments, in_count = (
            from_partner(out_data, "dp", level),
            from_partner(as_sent(out_segments), "dp", level).astype(out_segments.dtype),
            from_partner(send_count.reshape(1), "dp", level),
        )
        slot_contents = place_incoming(slot_contents, in_data, top_start, in_count[0])
        slot_documents = place_incoming(slot_documents, in_segments, top_start, in_count[0])
        live_tally_count = top_start + in_count[0]

    def frozen_block(slot_index, result_list):
        block_rows = lax.dynamic_index_in_dim(slot_contents, slot_index, 0, keepdims=False)
        block_ids = lax.dynamic_index_in_dim(slot_documents, slot_index, 0, keepdims=False)
        block_attention = attend_over_blocks(block_rows, block_ids)[0]
        product = jnp.dot(
            block_attention, frozen_complete, preferred_element_type=jnp.float32
        ).astype(jnp.bfloat16)
        return lax.dynamic_update_index_in_dim(result_list, product, slot_index, 0)

    result_list = lax.fori_loop(0, live_tally_count, frozen_block, empty_rows)
    frozen_layer_output = result_list.reshape(SLOT_NUMBER * ALIGNED_ROWS, frozen_complete.shape[1])
    return (qkv_gradient, weight_grad, frozen_layer_output)


def solution(mesh):
    return jax.shard_map(
        body,
        mesh=mesh,
        in_specs=(
            P("fsdp", None),
            P("fsdp", None),
            P(("dp", "fsdp"), None),
            P(("dp", "fsdp")),
            P(("dp", "fsdp"), None),
            P(("dp", "fsdp"), None),
            P(("dp", "fsdp")),
            P("dp", "fsdp"),
            P("dp", "fsdp", None),
        ),
        out_specs=(P(("dp", "fsdp"), None), P("fsdp", None), P(("dp", "fsdp"), None)),
        check_vma=False,
    )
```

profile of v0, /device:TPU:24, one launch (start us, length us, event | category | flops | bytes accessed | tf_op | source)
XLA Modules:
  0.0 297.1 jit_solution(7654348215393901867)
XLA Ops:
  7.2 1.0 fusion.43
  8.2 1.0 slice.52
  9.3 0.4 reshape.246
  9.8 1.2 fusion.45
  11.0 0.6 fusion.14
  11.6 1.0 copy.33
  12.6 2.8 convolution_convert_fusion.2
  15.5 0.7 all-gather.3.cloned.1.call-update
  16.9 0.7 fusion.44
  18.7 3.8 %collective-permute-start.5 = (bf16[1,128,896]{2,1,0:T(8,128)(2,1)S(1)}, bf16[1,128,896]{2,1,0:T(8,128)(2,1)S(1)}, u32[]{:S(2)}, u32[]{:S(2)}) collective-permute-start(bf16[1,128,896]{2,1,0:T(8,128)(2,1)S(1)} %dynamic-slice_select_fusion.4), channel_id=1, source_target_pairs={{0,16},{16,0},{32,48},{48,32},{64,80},{80,64},{96,112},{112,96},{1... | collective-permute-start | bytes 688136 | tf_op jit(solution)/shard_map/ppermute | solution.py:22
  22.6 2.0 collective-permute-start
  24.6 5.2 %collective-permute-start.1 = (s32[1]{0:T(128)}, s32[1]{0:T(128)}, u32[]{:S(2)}, u32[]{:S(2)}) collective-permute-start(s32[1]{0:T(128)} %bitcast.36), channel_id=1, source_target_pairs={{0,32},{16,48},{32,0},{48,16},{64,96},{80,112},{96,64},{112,80},{1... | collective-permute-start | bytes 20 | tf_op jit(solution)/shard_map/ppermute | solution.py:22
  29.8 9.1 %collective-permute-start.2 = (s32[1]{0:T(128)}, s32[1]{0:T(128)}, u32[]{:S(2)}, u32[]{:S(2)}) collective-permute-start(s32[1]{0:T(128)} %bitcast.39), channel_id=1, source_target_pairs={{0,64},{16,80},{32,96},{48,112},{64,0},{80,16},{96,32},{112,48},{1... | collective-permute-start | bytes 20 | tf_op jit(solution)/shard_map/ppermute | solution.py:22
  38.9 9.1 %collective-permute-start.3 = (s32[1]{0:T(128)}, s32[1]{0:T(128)}, u32[]{:S(2)}, u32[]{:S(2)}) collective-permute-start(s32[1]{0:T(128)} %bitcast.42), channel_id=1, source_target_pairs={{0,128},{16,144},{32,160},{48,176},{64,192},{80,208},{96,224},{112... | collective-permute-start | bytes 20 | tf_op jit(solution)/shard_map/ppermute | solution.py:22
  50.5 2.7 collective-permute-start.4
  55.1 2.9 collective-permute-start.10
  64.3 3.3 %collective-permute-start.11 = (s32[1,128]{1,0:T(1,128)S(1)}, s32[1,128]{1,0:T(1,128)S(1)}, u32[]{:S(2)}, u32[]{:S(2)}) collective-permute-start(s32[1,128]{1,0:T(1,128)S(1)} %broadcast_select_fusion.11), channel_id=1, source_target_pairs={{0,32},{16,48},{32,0},{48,16},{64,96},{80,112},{96,64},{112,80},{1... | collective-permute-start | bytes 1544 | tf_op jit(solution)/shard_map/ppermute | solution.py:22
  67.8 3.4 %collective-permute-start.6 = (bf16[1,128,896]{2,1,0:T(8,128)(2,1)S(1)}, bf16[1,128,896]{2,1,0:T(8,128)(2,1)S(1)}, u32[]{:S(2)}, u32[]{:S(2)}) collective-permute-start(bf16[1,128,896]{2,1,0:T(8,128)(2,1)S(1)} %dynamic-slice_select_fusion.3), channel_id=1, source_target_pairs={{0,32},{16,48},{32,0},{48,16},{64,96},{80,112},{96,64},{112,80},{1... | collective-permute-start | bytes 688136 | tf_op jit(solution)/shard_map/ppermute | solution.py:22
  71.3 5.5 %collective-permute-start.12 = (s32[1,128]{1,0:T(1,128)S(1)}, s32[1,128]{1,0:T(1,128)S(1)}, u32[]{:S(2)}, u32[]{:S(2)}) collective-permute-start(s32[1,128]{1,0:T(1,128)S(1)} %broadcast_select_fusion.12), channel_id=1, source_target_pairs={{0,64},{16,80},{32,96},{48,112},{64,0},{80,16},{96,32},{112,48},{1... | collective-permute-start | bytes 1544 | tf_op jit(solution)/shard_map/ppermute | solution.py:22
  76.8 3.9 %collective-permute-done.6 = bf16[1,128,896]{2,1,0:T(8,128)(2,1)S(1)} collective-permute-done((bf16[1,128,896]{2,1,0:T(8,128)(2,1)S(1)}, bf16[1,128,896]{2,1,0:T(8,128)(2,1)S(1)}, u32[]{:S(2)}, u32[]{:S(2)}) %collective-permute-start.6) | collective-permute-done | bytes 229408 | tf_op jit(solution)/shard_map/ppermute | solution.py:22
  80.8 5.5 %collective-permute-start.7 = (bf16[1,128,896]{2,1,0:T(8,128)(2,1)S(1)}, bf16[1,128,896]{2,1,0:T(8,128)(2,1)S(1)}, u32[]{:S(2)}, u32[]{:S(2)}) collective-permute-start(bf16[1,128,896]{2,1,0:T(8,128)(2,1)S(1)} %dynamic-slice_select_fusion.2), channel_id=1, source_target_pairs={{0,64},{16,80},{32,96},{48,112},{64,0},{80,16},{96,32},{112,48},{1... | collective-permute-start | bytes 688136 | tf_op jit(solution)/shard_map/ppermute | solution.py:22
  86.4 2.2 collective-permute-start.13
  88.6 18.0 %collective-permute-done.7 = bf16[1,128,896]{2,1,0:T(8,128)(2,1)S(1)} collective-permute-done((bf16[1,128,896]{2,1,0:T(8,128)(2,1)S(1)}, bf16[1,128,896]{2,1,0:T(8,128)(2,1)S(1)}, u32[]{:S(2)}, u32[]{:S(2)}) %collective-permute-start.7) | collective-permute-done | bytes 229408 | tf_op jit(solution)/shard_map/ppermute | solution.py:22
  106.8 5.3 %collective-permute-start.8 = (bf16[1,128,896]{2,1,0:T(8,128)(2,1)S(1)}, bf16[1,128,896]{2,1,0:T(8,128)(2,1)S(1)}, u32[]{:S(2)}, u32[]{:S(2)}) collective-permute-start(bf16[1,128,896]{2,1,0:T(8,128)(2,1)S(1)} %dynamic-slice_select_fusion.1), channel_id=1, source_target_pairs={{0,128},{16,144},{32,160},{48,176},{64,192},{80,208},{96,224},{112... | collective-permute-start | bytes 688136 | tf_op jit(solution)/shard_map/ppermute | solution.py:22
  112.2 3.2 %collective-permute-start.14 = (s32[1,128]{1,0:T(1,128)S(1)}, s32[1,128]{1,0:T(1,128)S(1)}, u32[]{:S(2)}, u32[]{:S(2)}) collective-permute-start(s32[1,128]{1,0:T(1,128)S(1)} %broadcast_select_fusion.14), channel_id=1, source_target_pairs={{0,256},{16,272},{32,288},{48,304},{64,320},{80,336},{96,352},{112... | collective-permute-start | bytes 1544 | tf_op jit(solution)/shard_map/ppermute | solution.py:22
  115.4 17.2 %collective-permute-done.8 = bf16[1,128,896]{2,1,0:T(8,128)(2,1)S(1)} collective-permute-done((bf16[1,128,896]{2,1,0:T(8,128)(2,1)S(1)}, bf16[1,128,896]{2,1,0:T(8,128)(2,1)S(1)}, u32[]{:S(2)}, u32[]{:S(2)}) %collective-permute-start.8) | collective-permute-done | bytes 229408 | tf_op jit(solution)/shard_map/ppermute | solution.py:22
  132.6 0.2 broadcast_select_fusion.3
  132.8 3.2 %collective-permute-start.9 = (bf16[1,128,896]{2,1,0:T(8,128)(2,1)S(1)}, bf16[1,128,896]{2,1,0:T(8,128)(2,1)S(1)}, u32[]{:S(2)}, u32[]{:S(2)}) collective-permute-start(bf16[1,128,896]{2,1,0:T(8,128)(2,1)S(1)} %dynamic-slice_select_fusion), channel_id=1, source_target_pairs={{0,256},{16,272},{32,288},{48,304},{64,320},{80,336},{96,352},{112... | collective-permute-start | bytes 688136 | tf_op jit(solution)/shard_map/ppermute | solution.py:22
  136.6 7.2 %collective-permute-done.9 = bf16[1,128,896]{2,1,0:T(8,128)(2,1)S(1)} collective-permute-done((bf16[1,128,896]{2,1,0:T(8,128)(2,1)S(1)}, bf16[1,128,896]{2,1,0:T(8,128)(2,1)S(1)}, u32[]{:S(2)}, u32[]{:S(2)}) %collective-permute-start.9) | collective-permute-done | bytes 229408 | tf_op jit(solution)/shard_map/ppermute | solution.py:22
  143.8 0.2 broadcast_select_fusion.4
  144.1 126.2 %all-reduce.1 = f32[40,2560]{1,0:T(8,128)S(1)} all-reduce(bf16[40,2560]{1,0:T(8,128)(2,1)} %reduce-scatter.2.cloned.1.call-done), channel_id=1, replica_groups=mesh['dp'=32,'fsdp'=16] {'dp'}, use_global_device_ids=true, to_apply=%region_4.5 | all-reduce | flops 102400 | bytes 614400 | tf_op jit(solution)/shard_map/psum | solution.py:151
  270.3 0.7 multiply_convert_fusion
  271.0 3.2 %convolution_convert_fusion.3 = bf16[256,640]{1,0:T(8,128)(2,1)S(1)} fusion(bf16[256,2560]{1,0:T(8,128)(2,1)S(1)} %copy-done, bf16[640,2560]{1,0:T(8,128)(2,1)} %all-gather.3.cloned.1.call-done), kind=kOutput, calls=%fused_computation.27 | convolution fusion | flops 839024640 | bytes 4915200 | tf_op jit(solution)/shard_map/dot_general | solution.py:133
  274.2 0.4 reshape.247
  274.6 1.1 fusion.18
  275.8 1.4 multiply_reduce_fusion
  277.3 0.7 fusion.15
  278.0 0.5 fusion.17
  278.5 1.1 broadcast_in_dim.178
  279.7 8.6 %while.10 = (s32[]{:T(128)}, bf16[2,128,2560]{2,1,0:T(8,128)(2,1)}, s32[]{:T(128)}, bf16[2,128,896]{2,1,0:T(8,128)(2,1)S(1)}, s32[2,128]{1,0:T(2,128)S(1)}, /*in...) while((s32[]{:T(128)}, bf16[2,128,2560]{2,1,0:T(8,128)(2,1)}, s32[]{:T(128)}, ...), condition=%wide.region_8.9_spmd, body=%wide.region_5.8_spmd.sunk | while | flops 462486272 | bytes 6636683 | solution.py:184
  280.0 0.2 fusion.75
  280.3 0.2 convolution_convert_fusion.6
  280.5 3.5 %fusion.77 = bf16[2,128,2560]{2,1,0:T(8,128)(2,1)} fusion(bf16[2,128,2560]{2,1,0:T(8,128)(2,1)} %get-tuple-element.117, s32[]{:T(128)S(6)} %select_n.252, bf16[128,640]{0,1:T(8,128)(2,1)S(1)} %bitcast.179, bf16[640,2560]{1,0:T(8,128)(2,1)} %get-tuple-element.130), kind=kOutput, calls=%fused_computation.2.clone.1 | convolution fusion | flops 419758080 | bytes 4096004 | tf_op jit(solution)/shard_map/while/body/dot_general | solution.py:179
  284.3 0.2 fusion.75
  284.6 0.2 convolution_convert_fusion.6
  284.8 3.5 %fusion.77 = bf16[2,128,2560]{2,1,0:T(8,128)(2,1)} fusion(bf16[2,128,2560]{2,1,0:T(8,128)(2,1)} %get-tuple-element.117, s32[]{:T(128)S(6)} %select_n.252, bf16[128,640]{0,1:T(8,128)(2,1)S(1)} %bitcast.179, bf16[640,2560]{1,0:T(8,128)(2,1)} %get-tuple-element.130), kind=kOutput, calls=%fused_computation.2.clone.1 | convolution fusion | flops 419758080 | bytes 4096004 | tf_op jit(solution)/shard_map/while/body/dot_general | solution.py:179
  288.3 1.0 copy.27
  289.6 1.0 copy.34
  (86 shorter events, 2.4 us)
Async XLA Ops:
  7.2 5.5 %copy-start = (bf16[256,2560]{1,0:T(8,128)(2,1)S(1)}, bf16[256,2560]{1,0:T(8,128)(2,1)}, u32[]{:S(2)}) copy-start(bf16[256,2560]{1,0:T(8,128)(2,1)} %param.15) | copy-start | bytes 3932164
  7.2 2.5 copy-start.11
  7.2 136.9 %reduce-scatter.2.cloned.1.call-start = ((), (), s32[]{:S(2)}) async-start(), calls=%async_computation.2 | async-start | bytes 3481600 | tf_op jit(solution)/shard_map/reduce_scatter | solution.py:142
  8.2 2.8 copy-start.5
  8.2 2.8 copy-start.7
  9.7 1.9 copy-start.2
  15.4 1.5 copy-start.10
  15.4 3.3 %copy-start.1 = (bf16[256,896]{1,0:T(8,128)(2,1)S(1)}, bf16[256,896]{1,0:T(8,128)(2,1)}, u32[]{:S(2)}) copy-start(bf16[256,896]{1,0:T(8,128)(2,1)} %param.16) | copy-start | bytes 1376260
  15.4 35.1 %copy-start.9 = (s32[256]{0:T(256)S(1)}, s32[256]{0:T(256)}, u32[]{:S(2)}) copy-start(s32[256]{0:T(256)} %param.17) | copy-start | bytes 3076
  15.4 255.6 %all-gather.3.cloned.1.call-start = ((), (), s32[]{:S(2)}) async-start(), calls=%async_computation.1 | async-start | bytes 3481600 | tf_op jit(solution)/shard_map/all_gather | solution.py:135
  16.2 262.3 %all-gather.5.cloned.1.call-start = ((), (), s32[]{:S(2)}) async-start(), calls=%async_computation.3 | async-start | bytes 3481600 | tf_op jit(solution)/shard_map/all_gather | solution.py:139
  18.7 48.9 %collective-permute-start.5 = (bf16[1,128,896]{2,1,0:T(8,128)(2,1)S(1)}, bf16[1,128,896]{2,1,0:T(8,128)(2,1)S(1)}, u32[]{:S(2)}, u32[]{:S(2)}) collective-permute-start(bf16[1,128,896]{2,1,0:T(8,128)(2,1)S(1)} %dynamic-slice_select_fusion.4), channel_id=1, source_target_pairs={{0,16},{16,0},{32,48},{48,32},{64,80},{80,64},{96,112},{112,96},{1... | collective-permute-start | bytes 688136 | tf_op jit(solution)/shard_map/ppermute | solution.py:22
  22.6 28.0 %collective-permute-start = (s32[1]{0:T(128)}, s32[1]{0:T(128)}, u32[]{:S(2)}, u32[]{:S(2)}) collective-permute-start(s32[1]{0:T(128)} %bitcast.33), channel_id=1, source_target_pairs={{0,16},{16,0},{32,48},{48,32},{64,80},{80,64},{96,112},{112,96},{1... | collective-permute-start | bytes 20 | tf_op jit(solution)/shard_map/ppermute | solution.py:22
  24.6 30.5 %collective-permute-start.1 = (s32[1]{0:T(128)}, s32[1]{0:T(128)}, u32[]{:S(2)}, u32[]{:S(2)}) collective-permute-start(s32[1]{0:T(128)} %bitcast.36), channel_id=1, source_target_pairs={{0,32},{16,48},{32,0},{48,16},{64,96},{80,112},{96,64},{112,80},{1... | collective-permute-start | bytes 20 | tf_op jit(solution)/shard_map/ppermute | solution.py:22
  29.8 30.2 %collective-permute-start.2 = (s32[1]{0:T(128)}, s32[1]{0:T(128)}, u32[]{:S(2)}, u32[]{:S(2)}) collective-permute-start(s32[1]{0:T(128)} %bitcast.39), channel_id=1, source_target_pairs={{0,64},{16,80},{32,96},{48,112},{64,0},{80,16},{96,32},{112,48},{1... | collective-permute-start | bytes 20 | tf_op jit(solution)/shard_map/ppermute | solution.py:22
  38.9 22.9 %collective-permute-start.3 = (s32[1]{0:T(128)}, s32[1]{0:T(128)}, u32[]{:S(2)}, u32[]{:S(2)}) collective-permute-start(s32[1]{0:T(128)} %bitcast.42), channel_id=1, source_target_pairs={{0,128},{16,144},{32,160},{48,176},{64,192},{80,208},{96,224},{112... | collective-permute-start | bytes 20 | tf_op jit(solution)/shard_map/ppermute | solution.py:22
  50.5 13.1 %collective-permute-start.4 = (s32[1]{0:T(128)}, s32[1]{0:T(128)}, u32[]{:S(2)}, u32[]{:S(2)}) collective-permute-start(s32[1]{0:T(128)} %bitcast.45), channel_id=1, source_target_pairs={{0,256},{16,272},{32,288},{48,304},{64,320},{80,336},{96,352},{112... | collective-permute-start | bytes 20 | tf_op jit(solution)/shard_map/ppermute | solution.py:22
  55.1 9.1 %collective-permute-start.10 = (s32[1,128]{1,0:T(1,128)S(1)}, s32[1,128]{1,0:T(1,128)S(1)}, u32[]{:S(2)}, u32[]{:S(2)}) collective-permute-start(s32[1,128]{1,0:T(1,128)S(1)} %broadcast_select_fusion.10), channel_id=1, source_target_pairs={{0,16},{16,0},{32,48},{48,32},{64,80},{80,64},{96,112},{112,96},{1... | collective-permute-start | bytes 1544 | tf_op jit(solution)/shard_map/ppermute | solution.py:22
  64.3 6.9 %collective-permute-start.11 = (s32[1,128]{1,0:T(1,128)S(1)}, s32[1,128]{1,0:T(1,128)S(1)}, u32[]{:S(2)}, u32[]{:S(2)}) collective-permute-start(s32[1,128]{1,0:T(1,128)S(1)} %broadcast_select_fusion.11), channel_id=1, source_target_pairs={{0,32},{16,48},{32,0},{48,16},{64,96},{80,112},{96,64},{112,80},{1... | collective-permute-start | bytes 1544 | tf_op jit(solution)/shard_map/ppermute | solution.py:22
  67.8 12.8 %collective-permute-start.6 = (bf16[1,128,896]{2,1,0:T(8,128)(2,1)S(1)}, bf16[1,128,896]{2,1,0:T(8,128)(2,1)S(1)}, u32[]{:S(2)}, u32[]{:S(2)}) collective-permute-start(bf16[1,128,896]{2,1,0:T(8,128)(2,1)S(1)} %dynamic-slice_select_fusion.3), channel_id=1, source_target_pairs={{0,32},{16,48},{32,0},{48,16},{64,96},{80,112},{96,64},{112,80},{1... | collective-permute-start | bytes 688136 | tf_op jit(solution)/shard_map/ppermute | solution.py:22
  71.3 15.0 %collective-permute-start.12 = (s32[1,128]{1,0:T(1,128)S(1)}, s32[1,128]{1,0:T(1,128)S(1)}, u32[]{:S(2)}, u32[]{:S(2)}) collective-permute-start(s32[1,128]{1,0:T(1,128)S(1)} %broadcast_select_fusion.12), channel_id=1, source_target_pairs={{0,64},{16,80},{32,96},{48,112},{64,0},{80,16},{96,32},{112,48},{1... | collective-permute-start | bytes 1544 | tf_op jit(solution)/shard_map/ppermute | solution.py:22
  80.8 25.8 %collective-permute-start.7 = (bf16[1,128,896]{2,1,0:T(8,128)(2,1)S(1)}, bf16[1,128,896]{2,1,0:T(8,128)(2,1)S(1)}, u32[]{:S(2)}, u32[]{:S(2)}) collective-permute-start(bf16[1,128,896]{2,1,0:T(8,128)(2,1)S(1)} %dynamic-slice_select_fusion.2), channel_id=1, source_target_pairs={{0,64},{16,80},{32,96},{48,112},{64,0},{80,16},{96,32},{112,48},{1... | collective-permute-start | bytes 688136 | tf_op jit(solution)/shard_map/ppermute | solution.py:22
  86.4 25.7 %collective-permute-start.13 = (s32[1,128]{1,0:T(1,128)S(1)}, s32[1,128]{1,0:T(1,128)S(1)}, u32[]{:S(2)}, u32[]{:S(2)}) collective-permute-start(s32[1,128]{1,0:T(1,128)S(1)} %broadcast_select_fusion.13), channel_id=1, source_target_pairs={{0,128},{16,144},{32,160},{48,176},{64,192},{80,208},{96,224},{112... | collective-permute-start | bytes 1544 | tf_op jit(solution)/shard_map/ppermute | solution.py:22
  106.8 25.8 %collective-permute-start.8 = (bf16[1,128,896]{2,1,0:T(8,128)(2,1)S(1)}, bf16[1,128,896]{2,1,0:T(8,128)(2,1)S(1)}, u32[]{:S(2)}, u32[]{:S(2)}) collective-permute-start(bf16[1,128,896]{2,1,0:T(8,128)(2,1)S(1)} %dynamic-slice_select_fusion.1), channel_id=1, source_target_pairs={{0,128},{16,144},{32,160},{48,176},{64,192},{80,208},{96,224},{112... | collective-permute-start | bytes 688136 | tf_op jit(solution)/shard_map/ppermute | solution.py:22
  112.2 24.4 %collective-permute-start.14 = (s32[1,128]{1,0:T(1,128)S(1)}, s32[1,128]{1,0:T(1,128)S(1)}, u32[]{:S(2)}, u32[]{:S(2)}) collective-permute-start(s32[1,128]{1,0:T(1,128)S(1)} %broadcast_select_fusion.14), channel_id=1, source_target_pairs={{0,256},{16,272},{32,288},{48,304},{64,320},{80,336},{96,352},{112... | collective-permute-start | bytes 1544 | tf_op jit(solution)/shard_map/ppermute | solution.py:22
  132.8 11.1 %collective-permute-start.9 = (bf16[1,128,896]{2,1,0:T(8,128)(2,1)S(1)}, bf16[1,128,896]{2,1,0:T(8,128)(2,1)S(1)}, u32[]{:S(2)}, u32[]{:S(2)}) collective-permute-start(bf16[1,128,896]{2,1,0:T(8,128)(2,1)S(1)} %dynamic-slice_select_fusion), channel_id=1, source_target_pairs={{0,256},{16,272},{32,288},{48,304},{64,320},{80,336},{96,352},{112... | collective-permute-start | bytes 688136 | tf_op jit(solution)/shard_map/ppermute | solution.py:22
  271.0 3.6 %copy-start.3 = (bf16[2,128,5,128]{3,2,1,0:T(8,128)(2,1)S(1)}, bf16[2,128,5,128]{3,2,1,0:T(8,128)(2,1)}, u32[]{:S(2)}) copy-start(bf16[2,128,5,128]{3,2,1,0:T(8,128)(2,1)} %copy-done.2) | copy-start | bytes 983044
  271.0 3.6 %copy-start.6 = (bf16[256,128]{1,0:T(8,128)(2,1)S(1)}, bf16[256,128]{1,0:T(8,128)(2,1)}, u32[]{:S(2)}) copy-start(bf16[256,128]{1,0:T(8,128)(2,1)} %copy-done.5) | copy-start | bytes 196612
  274.6 1.2 copy-start.8
  275.8 1.4 copy-start.12
  288.3 1.2 copy-start.4
Sparse Core Ops, SparseCore 0:
  15.5 102.2 reduce-scatter.1
  121.7 67.6 all-gather.2
  193.2 66.4 all-gather.4
where the time goes:
time: 298 us; the launch traced here: 297 us
  blocking collectives  126 us (42%)
  starting transfers between devices  66.4 us (22%)
  waiting for transfers between devices  47.1 us (16%)
  between operations  27.1 us (9%)
  matrix products  19.3 us (6%)
  local copies, waits for them, and re-layouts  8.28 us (3%)
    psum x1, blocking collectives, body(): total_grad = lax.psum(group_part, 'dp')  126 us
    ppermute x15, starting transfers between devices, from_partner(): lax.ppermute(shard, axis, [(i, i ^ 1 << stride) for i in range(lax.axis_s...  66.3 us
    ppermute x15, waiting for transfers between devices, from_partner(): lax.ppermute(shard, axis, [(i, i ^ 1 << stride) for i in range(lax.axis_s...  46.3 us
    dot_general x2, matrix products, frozen_block(): jnp.dot(block_attention, frozen_complete, preferred_element_type=jnp.floa...  6.95 us
  transfers between devices with their start and end apart: 18, of which 4 were waited for; matrix products, arithmetic and copies ran while one was open for 3% of the time, Pallas kernels for 0%

commit v1 on v0

v1 whole, which is shorter than its diff:
```python
import math

import jax
import jax.numpy as jnp
from jax import lax
from jax.experimental import pallas as pl
from jax.experimental.pallas import tpu as pltpu
from jax.sharding import PartitionSpec as P

HD = 128
HQ = 5
ALIGNED_ROWS = 128
SLOT_NUMBER = 2
QW = HQ * HD
QKV = (HQ + 2) * HD
D = 2560
SCALE = 1.0 / math.sqrt(HD)
MASKED = -1e30
VMEM = 48 * 1024 * 1024

NN = (((1,), (0,)), ((), ()))
NT = (((1,), (1,)), ((), ()))
TN = (((0,), (0,)), ((), ()))


def dot(a, b, dims):
    return lax.dot_general(a, b, dims, preferred_element_type=jnp.float32)


def block_probs(x_ref, rows, allowed, h):
    q = x_ref[rows, h * HD : (h + 1) * HD]
    k = x_ref[rows, QW : QW + HD]
    s = jnp.where(allowed, dot(q, k, NT) * SCALE, MASKED)
    e = jnp.exp(s - jnp.max(s, axis=-1, keepdims=True))
    return e / jnp.sum(e, axis=-1, keepdims=True)


def allowed_pairs(seg_ref, b):
    key_seg = jnp.broadcast_to(seg_ref[b : b + 1, :].astype(jnp.float32), (ALIGNED_ROWS, ALIGNED_ROWS))
    query_pos = lax.broadcasted_iota(jnp.int32, key_seg.shape, 0)
    key_pos = lax.broadcasted_iota(jnp.int32, key_seg.shape, 1)
    return (query_pos >= key_pos) & (key_seg == key_seg.T)


def forward_kernel(cur_ref, cur_seg_ref, nxt_ref, nxt_seg_ref, order_ref, cur_out, nxt_out, prob_out, attn_ref):
    for b in range(2):
        rows = slice(b * ALIGNED_ROWS, (b + 1) * ALIGNED_ROWS)
        allowed = allowed_pairs(cur_seg_ref, b)
        for h in range(HQ):
            p = block_probs(cur_ref, rows, allowed, h)
            prob_out[h, rows, :] = p
            v = cur_ref[rows, QW + HD :]
            attn_ref[rows, h * HD : (h + 1) * HD] = dot(p.astype(jnp.bfloat16), v, NN).astype(jnp.bfloat16)
    cur_out[...] = dot(attn_ref[...], order_ref[...], NN).astype(jnp.bfloat16)
    for b in range(2):
        rows = slice(b * ALIGNED_ROWS, (b + 1) * ALIGNED_ROWS)
        allowed = allowed_pairs(nxt_seg_ref, b)
        for h in range(HQ):
            p = block_probs(nxt_ref, rows, allowed, h)
            v = nxt_ref[rows, QW + HD :]
            nxt_out[rows, h * HD : (h + 1) * HD] = dot(p.astype(jnp.bfloat16), v, NN).astype(jnp.bfloat16)


def forward_attention(qkv_current, segment_current, qkv_next, document_next, order):
    rows = qkv_current.shape[0]
    return pl.pallas_call(
        forward_kernel,
        out_shape=(
            jax.ShapeDtypeStruct((rows, QW), jnp.bfloat16),
            jax.ShapeDtypeStruct((rows, QW), jnp.bfloat16),
            jax.ShapeDtypeStruct((HQ, rows, HD), jnp.float32),
        ),
        scratch_shapes=[pltpu.VMEM((rows, QW), jnp.bfloat16)],
        compiler_params=pltpu.CompilerParams(vmem_limit_bytes=VMEM),
        cost_estimate=pl.CostEstimate(flops=10**9, bytes_accessed=3 * 10**6, transcendentals=10**6),
        name="forward_attention",
    )(qkv_current, segment_current, qkv_next, document_next, order)


def backward_kernel(x_ref, prob_ref, g_ref, w_ref, out_ref, dk_ref, dv_ref):
    h = pl.program_id(0)

    @pl.when(h == 0)
    def _():
        dk_ref[...] = jnp.zeros_like(dk_ref)
        dv_ref[...] = jnp.zeros_like(dv_ref)

    columns = pl.ds(pl.multiple_of(h * HD, HD), HD)
    grad_attention = dot(g_ref[...], w_ref[...], NT).astype(jnp.bfloat16)
    for b in range(2):
        rows = slice(b * ALIGNED_ROWS, (b + 1) * ALIGNED_ROWS)
        ga = grad_attention[rows]
        q = x_ref[rows, columns]
        k = x_ref[rows, QW : QW + HD]
        v = x_ref[rows, QW + HD :]
        p = prob_ref[rows, :]
        dp = dot(ga, v, NT)
        ds = p * (dp - jnp.sum(p * dp, axis=-1, keepdims=True))
        high = ds.astype(jnp.bfloat16)
        low = (ds - high.astype(jnp.float32)).astype(jnp.bfloat16)
        out_ref[rows, columns] = ((dot(high, k, NN) + dot(low, k, NN)) * SCALE).astype(jnp.bfloat16)
        dk_ref[rows, :] += dot(high, q, TN) + dot(low, q, TN)
        dv_ref[rows, :] += dot(p.astype(jnp.bfloat16), ga, TN)

    @pl.when(h == HQ - 1)
    def _():
        out_ref[:, QW : QW + HD] = (dk_ref[...] * SCALE).astype(jnp.bfloat16)
        out_ref[:, QW + HD :] = dv_ref[...].astype(jnp.bfloat16)


def backward_attention(qkv_current, probs, grad_output, weights):
    rows = qkv_current.shape[0]
    return pl.pallas_call(
        backward_kernel,
        grid=(HQ,),
        in_specs=[
            pl.BlockSpec((rows, QKV), lambda h: (0, 0)),
            pl.BlockSpec((None, rows, HD), lambda h: (h, 0, 0)),
            pl.BlockSpec((rows, D), lambda h: (0, 0)),
            pl.BlockSpec((HD, D), lambda h: (h, 0)),
        ],
        out_specs=pl.BlockSpec((rows, QKV), lambda h: (0, 0)),
        out_shape=jax.ShapeDtypeStruct((rows, QKV), jnp.bfloat16),
        scratch_shapes=[pltpu.VMEM((rows, HD), jnp.float32), pltpu.VMEM((rows, HD), jnp.float32)],
        compiler_params=pltpu.CompilerParams(vmem_limit_bytes=VMEM),
        cost_estimate=pl.CostEstimate(flops=2 * 10**9, bytes_accessed=6 * 10**6, transcendentals=0),
        name="backward_attention",
    )(qkv_current, probs, grad_output, weights)


def frozen_kernel(live_ref, a_ref, w_ref, out_ref):
    rows = lax.broadcasted_iota(jnp.int32, out_ref.shape, 0)
    product = dot(a_ref[...], w_ref[...], NN)
    out_ref[...] = jnp.where(rows < live_ref[0] * ALIGNED_ROWS, product, 0.0).astype(jnp.bfloat16)


def frozen_projection(live, attention, weights):
    rows = attention.shape[0]
    width = 512
    return pl.pallas_call(
        frozen_kernel,
        grid=(D // width,),
        in_specs=[
            pl.BlockSpec(memory_space=pltpu.SMEM),
            pl.BlockSpec((rows, QW), lambda i: (0, 0)),
            pl.BlockSpec((QW, width), lambda i: (0, D // width + i)),
        ],
        out_specs=pl.BlockSpec((rows, width), lambda i: (0, i)),
        out_shape=jax.ShapeDtypeStruct((rows, D), jnp.bfloat16),
        compiler_params=pltpu.CompilerParams(vmem_limit_bytes=VMEM),
        cost_estimate=pl.CostEstimate(flops=10**9, bytes_accessed=5 * 10**6, transcendentals=0),
        name="frozen_projection",
    )(live, attention, weights)


N_DP = 32
N_FSDP = 16


def fsdp_pairs(flip, x_step):
    def target(j):
        j ^= flip
        return (j & 9) | (((j >> 1 & 3) + x_step) % 4 << 1)

    return [(j, target(j)) for j in range(N_FSDP)]


def all_pairs(dp_flip, fsdp_flip):
    return [
        (d * N_FSDP + j, (d ^ dp_flip) * N_FSDP + (j ^ fsdp_flip)) for d in range(N_DP) for j in range(N_FSDP)
    ]


def swap(a, dp_flip, fsdp_flip=0):
    return lax.ppermute(a, ("dp", "fsdp"), all_pairs(dp_flip, fsdp_flip))


def add(*terms):
    return sum(t.astype(jnp.float32) for t in terms).astype(jnp.bfloat16)


def leaving_order(me):
    rows = QW // N_FSDP
    natural = jnp.arange(QW, dtype=jnp.int32)
    j, k = natural // rows, natural % rows
    flip = j ^ me
    place = (flip & 1) * 8 + (((j >> 1) - (me >> 1)) & 3) * 2 + (flip >> 3)
    return (natural[None, :] == (place * rows + k)[:, None]).astype(jnp.bfloat16)


def reduce_weight_grad(attention, grad_output, y_lo, z_lo):
    half = QW // 2
    terms = dot(attention[:, half:], grad_output, TN).astype(jnp.bfloat16)
    other = lax.ppermute(terms, "fsdp", fsdp_pairs(1, 0))
    total = add(dot(attention[:, :half], grad_output, TN).astype(jnp.bfloat16), other)
    chunks = total.reshape(4, half // 4, D)
    total = add(chunks[0], *(lax.ppermute(chunks[s], "fsdp", fsdp_pairs(0, s)) for s in (1, 2, 3)))
    own, far = total[: half // 8], total[half // 8 :]

    def halves(a, flag):
        left, right = jnp.split(a, 2, axis=1)
        return jnp.where(flag, right, left), jnp.where(flag, left, right)

    own_keep, own_give = halves(own, y_lo == 1)
    far_keep, far_give = halves(far, y_lo == 1)
    total = add(own_keep, swap(own_give, 16), swap(far_keep, 0, 8), swap(far_give, 16, 8))
    keep, give = halves(total, z_lo == 1)
    total = add(keep, swap(give, 1))
    total = add(total, swap(total, 2))
    total = add(total, swap(total, 4))
    total = total.astype(jnp.float32) + swap(total, 8).astype(jnp.float32)
    total = (total * (1.0 / (N_DP * N_FSDP))).astype(jnp.bfloat16)

    def joined(a, b, flag):
        return jnp.where(flag, jnp.concatenate([b, a], axis=1), jnp.concatenate([a, b], axis=1))

    near = joined(total, swap(total, 1), z_lo == 1)
    away = joined(swap(total, 16), swap(total, 17), z_lo == 1)
    return joined(near, away, y_lo == 1)


def move_blocks(attention, live, plan):
    slots = attention.reshape(SLOT_NUMBER, ALIGNED_ROWS, QW)
    for level in range(N_DP.bit_length() - 1):
        count = plan[level]
        top = live - count
        block = jnp.where(top >= 1, slots[1], slots[0])
        flag = jnp.full((16, QW), count, jnp.bfloat16)
        arrived = swap(jnp.concatenate([block, flag], axis=0), 1 << level)
        received = arrived[ALIGNED_ROWS, 0].astype(jnp.int32)
        block = arrived[:ALIGNED_ROWS]
        slots = jnp.stack(
            [jnp.where((received > 0) & (top == s), block, slots[s]) for s in range(SLOT_NUMBER)]
        )
        live = top + received
    return slots.reshape(SLOT_NUMBER * ALIGNED_ROWS, QW), live


def body(
    policy_out,
    frozen_out,
    qkv_current,
    segment_current,
    grad_output,
    query_key_value_next,
    document_next,
    block_counts,
    move_plan,
):
    me = lax.axis_index("fsdp")
    group = lax.axis_index("dp")
    weights = lax.all_gather(
        jnp.concatenate([policy_out, frozen_out], axis=1), "fsdp", axis=0, tiled=True
    )
    attention, next_attention, probs = forward_attention(
        qkv_current,
        segment_current.reshape(2, ALIGNED_ROWS),
        query_key_value_next,
        document_next.reshape(SLOT_NUMBER, ALIGNED_ROWS),
        leaving_order(me),
    )
    weight_grad = reduce_weight_grad(attention, grad_output, group >> 4, group & 1)
    moved, live = move_blocks(next_attention, block_counts[0, 0], move_plan[0, 0])
    qkv_gradient = backward_attention(qkv_current, probs, grad_output, weights)
    frozen_layer_output = frozen_projection(live.reshape(1), moved, weights)
    return (qkv_gradient, weight_grad, frozen_layer_output)


def solution(mesh):
    return jax.shard_map(
        body,
        mesh=mesh,
        in_specs=(
            P("fsdp", None),
            P("fsdp", None),
            P(("dp", "fsdp"), None),
            P(("dp", "fsdp")),
            P(("dp", "fsdp"), None),
            P(("dp", "fsdp"), None),
            P(("dp", "fsdp")),
            P("dp", "fsdp"),
            P("dp", "fsdp", None),
        ),
        out_specs=(P(("dp", "fsdp"), None), P("fsdp", None), P(("dp", "fsdp"), None)),
        check_vma=False,
    )
```

time: 298 us -> 201 us (0.67)
  blocking collectives: 126 us -> 0 us
  Pallas kernels: 0 us -> 20.1 us
  matrix products: 19.3 us -> 4 us
  waiting for transfers between devices: 47.1 us -> 62.4 us
  starting transfers between devices: 66.4 us -> 75.1 us
  other arithmetic: 2.55 us -> 6.87 us
    psum x1 -> x0, blocking collectives: 126 us -> none  [body(): total_grad = lax.psum(group_part, 'dp')]
    pallas_call x0 -> x3, Pallas kernels: none -> 20.1 us  [the longest x1 8.51 us: backward_attention(): pl.pallas_call(backward_kernel, grid=(HQ,), in_specs=[pl.BlockSpec((rows,...]
    ppermute x15 -> x19, waiting for transfers between devices: 46.3 us -> 62.4 us  [the longest x15 62.4 us: swap(): return lax.ppermute(a, ('dp', 'fsdp'), all_pairs(dp_flip, fsdp_flip))]
    dot_general x13 -> x2, matrix products: 18.1 us -> 4 us  [dot(): return lax.dot_general(a, b, dims, preferred_element_type=jnp.float32)]
    ppermute x15 -> x19, starting transfers between devices: 66.3 us -> 75 us  [the longest x15 62.4 us: swap(): return lax.ppermute(a, ('dp', 'fsdp'), all_pairs(dp_flip, fsdp_flip))]
  transfers between devices with their start and end apart: 18 -> 20, of which waited for: 4 -> 9; matrix products, arithmetic and copies ran while one was open for 3% -> 7% of each run, Pallas kernels for 0% -> 3%
where the time goes in v1:
time: 201 us; the launch traced here: 199 us
  starting transfers between devices  75.1 us (37%)
  waiting for transfers between devices  62.4 us (31%)
  between operations  25 us (12%)
  Pallas kernels  20.1 us (10%)
  other arithmetic  6.87 us (3%)
  local copies, waits for them, and re-layouts  5.85 us (3%)
  matrix products  4 us (2%)
    ppermute x15, waiting for transfers between devices, swap(): return lax.ppermute(a, ('dp', 'fsdp'), all_pairs(dp_flip, fsdp_flip))  62.4 us
    ppermute x15, starting transfers between devices, swap(): return lax.ppermute(a, ('dp', 'fsdp'), all_pairs(dp_flip, fsdp_flip))  62.4 us
    ppermute x3, starting transfers between devices, reduce_weight_grad(): lax.ppermute(chunks[s], 'fsdp', fsdp_pairs(0, s))  10.8 us
    pallas_call x1, Pallas kernels, backward_attention(): pl.pallas_call(backward_kernel, grid=(HQ,), in_specs=[pl.BlockSpec((rows,...  8.51 us
    pallas_call x1, Pallas kernels, forward_attention(): pl.pallas_call(forward_kernel, out_shape=(jax.ShapeDtypeStruct((rows, QW)...  6.27 us
    pallas_call x1, Pallas kernels, frozen_projection(): pl.pallas_call(frozen_kernel, grid=(D // width,), in_specs=[pl.BlockSpec(...  5.34 us
  transfers between devices with their start and end apart: 20, of which 9 were waited for; matrix products, arithmetic and copies ran while one was open for 7% of the time, Pallas kernels for 3%

profile of v1, /device:TPU:24, one launch (start us, length us, event | category | flops | bytes accessed | tf_op | source)
XLA Modules:
  0.0 199.3 jit_solution(12270074843452732850)
XLA Ops:
  7.3 1.9 pad_maximum_fusion
  9.2 0.2 fusion.1.order_ref
  9.4 6.3 %forward_attention.1 = (bf16[256,640]{1,0:T(8,128)(2,1)S(1)}, bf16[256,640]{1,0:T(8,128)(2,1)S(1)}, f32[5,256,128]{2,1,0:T(8,128)S(1)}) custom-call(bf16[256,896]{1,0:T(8,128)(2,1)S(1)} %copy-done.1, s32[2,128]{1,0:T(2,128)S(1)} %bitcast.28, bf16[256,896]{1,0:T(8,128)(2,1)S(1)} %copy-done.2, s32[2,128]{1,0:T(2,128)S(1)} %bitcast.29, ...), custom_call_target="tpu_custom_call" | custom-call | flops 1000000000 | bytes 3000000 | tf_op jit(solution)/shard_map/forward_attention/pallas_call | solution.py:66
  15.7 2.0 convolution_convert_fusion
  17.7 1.9 collective-permute-start
  20.3 0.6 fusion.15
  22.3 3.8 %collective-permute-start.14 = (bf16[144,640]{1,0:T(8,128)(2,1)S(1)}, bf16[144,640]{1,0:T(8,128)(2,1)}, u32[]{:S(2)}, u32[]{:S(2)}) collective-permute-start(bf16[144,640]{1,0:T(8,128)(2,1)S(1)} %concatenate.43), channel_id=1, source_target_pairs={{0,16},{1,17},{2,18},{3,19},{4,20},{5,21},{6,22},{7,23},{8,24},{9,... | collective-permute-start | bytes 552968 | tf_op jit(solution)/shard_map/ppermute | solution.py:175
  26.8 4.8 %collective-permute-done.14 = bf16[144,640]{1,0:T(8,128)(2,1)} collective-permute-done((bf16[144,640]{1,0:T(8,128)(2,1)S(1)}, bf16[144,640]{1,0:T(8,128)(2,1)}, u32[]{:S(2)}, u32[]{:S(2)}) %collective-permute-start.14) | collective-permute-done | bytes 184352 | tf_op jit(solution)/shard_map/ppermute | solution.py:175
  31.5 1.1 slice.115
  34.0 1.0 broadcast_select_fusion.11
  34.9 0.7 concatenate.44
  35.6 5.2 %collective-permute-start.15 = (bf16[144,640]{1,0:T(8,128)(2,1)}, bf16[144,640]{1,0:T(8,128)(2,1)S(1)}, u32[]{:S(2)}, u32[]{:S(2)}) collective-permute-start(bf16[144,640]{1,0:T(8,128)(2,1)} %concatenate.44), channel_id=1, source_target_pairs={{0,32},{1,33},{2,34},{3,35},{4,36},{5,37},{6,38},{7,39},{8,40},{9,... | collective-permute-start | bytes 552968 | tf_op jit(solution)/shard_map/ppermute | solution.py:175
  41.5 8.1 %collective-permute-done.15 = bf16[144,640]{1,0:T(8,128)(2,1)S(1)} collective-permute-done((bf16[144,640]{1,0:T(8,128)(2,1)}, bf16[144,640]{1,0:T(8,128)(2,1)S(1)}, u32[]{:S(2)}, u32[]{:S(2)}) %collective-permute-start.15) | collective-permute-done | bytes 184352 | tf_op jit(solution)/shard_map/ppermute | solution.py:175
  49.6 0.6 slice.117
  51.5 2.0 %add_convert_fusion = bf16[320,2560]{1,0:T(8,128)(2,1)S(1)} fusion(bf16[320,2560]{1,0:T(8,128)(2,1)} %collective-permute-done, bf16[256,2560]{1,0:T(8,128)(2,1)S(1)} %copy-done, bf16[256,640]{1,0:T(8,128)(2,1)S(1)} %get-tuple-element.7), kind=kOutput, calls=%fused_computation.3 | convolution fusion | flops 423526400 | bytes 4784128 | tf_op jit(solution)/shard_map/dot_general | solution.py:27
  53.6 1.1 fusion.14
  54.7 3.4 %collective-permute-start.1 = (bf16[80,2560]{1,0:T(8,128)(2,1)}, bf16[80,2560]{1,0:T(8,128)(2,1)}, u32[]{:S(2)}, u32[]{:S(2)}) collective-permute-start(bf16[80,2560]{1,0:T(8,128)(2,1)} %get-tuple-element.15), channel_id=1, source_target_pairs={{0,2},{1,3},{2,4},{3,5},{4,6},{5,7},{6,0},{7,1},{8,10},{9,11},{10,... | collective-permute-start | bytes 1228808 | tf_op jit(solution)/shard_map/ppermute | solution.py:197
  58.1 3.7 %collective-permute-start.3 = (bf16[80,2560]{1,0:T(8,128)(2,1)}, bf16[80,2560]{1,0:T(8,128)(2,1)}, u32[]{:S(2)}, u32[]{:S(2)}) collective-permute-start(bf16[80,2560]{1,0:T(8,128)(2,1)} %get-tuple-element.16), channel_id=1, source_target_pairs={{0,6},{1,7},{2,0},{3,1},{4,2},{5,3},{6,4},{7,5},{8,14},{9,15},{10,... | collective-permute-start | bytes 1228808 | tf_op jit(solution)/shard_map/ppermute | solution.py:197
  61.8 3.7 %collective-permute-start.2 = (bf16[80,2560]{1,0:T(8,128)(2,1)}, bf16[80,2560]{1,0:T(8,128)(2,1)}, u32[]{:S(2)}, u32[]{:S(2)}) collective-permute-start(bf16[80,2560]{1,0:T(8,128)(2,1)} %get-tuple-element.17), channel_id=1, source_target_pairs={{0,4},{1,5},{2,6},{3,7},{4,0},{5,1},{6,2},{7,3},{8,12},{9,13},{10,... | collective-permute-start | bytes 1228808 | tf_op jit(solution)/shard_map/ppermute | solution.py:197
  65.6 9.1 %collective-permute-start.16 = (bf16[144,640]{1,0:T(8,128)(2,1)S(1)}, bf16[144,640]{1,0:T(8,128)(2,1)S(1)}, u32[]{:S(2)}, u32[]{:S(2)}) collective-permute-start(bf16[144,640]{1,0:T(8,128)(2,1)S(1)} %concatenate.45), channel_id=1, source_target_pairs={{0,64},{1,65},{2,66},{3,67},{4,68},{5,69},{6,70},{7,71},{8,72},{9,... | collective-permute-start | bytes 552968 | tf_op jit(solution)/shard_map/ppermute | solution.py:175
  75.4 13.5 %collective-permute-done.16 = bf16[144,640]{1,0:T(8,128)(2,1)S(1)} collective-permute-done((bf16[144,640]{1,0:T(8,128)(2,1)S(1)}, bf16[144,640]{1,0:T(8,128)(2,1)S(1)}, u32[]{:S(2)}, u32[]{:S(2)}) %collective-permute-start.16) | collective-permute-done | bytes 184352 | tf_op jit(solution)/shard_map/ppermute | solution.py:175
  88.9 0.5 slice.119
  90.7 1.6 add_convert_fusion.1
  92.4 2.7 %collective-permute-start.4 = (bf16[40,1280]{1,0:T(8,128)(2,1)S(1)}, bf16[40,1280]{1,0:T(8,128)(2,1)S(1)}, u32[]{:S(2)}, u32[]{:S(2)}) collective-permute-start(bf16[40,1280]{1,0:T(8,128)(2,1)S(1)} %get-tuple-element.18), channel_id=1, source_target_pairs={{0,256},{1,257},{2,258},{3,259},{4,260},{5,261},{6,262},{7,263},{8... | collective-permute-start | bytes 307208 | tf_op jit(solution)/shard_map/ppermute | solution.py:175
  95.1 4.7 %collective-permute-start.5 = (bf16[40,1280]{1,0:T(8,128)(2,1)S(1)}, bf16[40,1280]{1,0:T(8,128)(2,1)S(1)}, u32[]{:S(2)}, u32[]{:S(2)}) collective-permute-start(bf16[40,1280]{1,0:T(8,128)(2,1)S(1)} %get-tuple-element.19), channel_id=1, source_target_pairs={{0,8},{1,9},{2,10},{3,11},{4,12},{5,13},{6,14},{7,15},{8,0},{9,1},... | collective-permute-start | bytes 307208 | tf_op jit(solution)/shard_map/ppermute | solution.py:175
  99.8 3.0 %collective-permute-start.6 = (bf16[40,1280]{1,0:T(8,128)(2,1)S(1)}, bf16[40,1280]{1,0:T(8,128)(2,1)S(1)}, u32[]{:S(2)}, u32[]{:S(2)}) collective-permute-start(bf16[40,1280]{1,0:T(8,128)(2,1)S(1)} %get-tuple-element.20), channel_id=1, source_target_pairs={{0,264},{1,265},{2,266},{3,267},{4,268},{5,269},{6,270},{7,271},{8... | collective-permute-start | bytes 307208 | tf_op jit(solution)/shard_map/ppermute | solution.py:175
  102.8 1.0 broadcast_select_fusion.5
  103.9 13.1 %collective-permute-start.17 = (bf16[144,640]{1,0:T(8,128)(2,1)S(1)}, bf16[144,640]{1,0:T(8,128)(2,1)S(1)}, u32[]{:S(2)}, u32[]{:S(2)}) collective-permute-start(bf16[144,640]{1,0:T(8,128)(2,1)S(1)} %concatenate.46), channel_id=1, source_target_pairs={{0,128},{1,129},{2,130},{3,131},{4,132},{5,133},{6,134},{7,135},{8... | collective-permute-start | bytes 552968 | tf_op jit(solution)/shard_map/ppermute | solution.py:175
  117.0 0.1 add_convert_fusion.2
  117.1 1.9 collective-permute-start.7
  119.6 13.3 %collective-permute-done.17 = bf16[144,640]{1,0:T(8,128)(2,1)S(1)} collective-permute-done((bf16[144,640]{1,0:T(8,128)(2,1)S(1)}, bf16[144,640]{1,0:T(8,128)(2,1)S(1)}, u32[]{:S(2)}, u32[]{:S(2)}) %collective-permute-start.17) | collective-permute-done | bytes 184352 | tf_op jit(solution)/shard_map/ppermute | solution.py:175
  133.0 0.5 slice.121
  134.8 1.9 collective-permute-start.8
  136.8 1.9 collective-permute-start.18
  138.7 3.0 %collective-permute-done.8 = bf16[40,640]{1,0:T(8,128)(2,1)S(1)} collective-permute-done((bf16[40,640]{1,0:T(8,128)(2,1)S(1)}, bf16[40,640]{1,0:T(8,128)(2,1)S(1)}, u32[]{:S(2)}, u32[]{:S(2)}) %collective-permute-start.8) | collective-permute-done | bytes 51232 | tf_op jit(solution)/shard_map/ppermute | solution.py:175
  141.7 1.9 collective-permute-start.9
  143.7 0.6 collective-permute-done.18
  144.2 0.5 slice.123
  145.4 6.2 %collective-permute-done.9 = bf16[40,640]{1,0:T(8,128)(2,1)S(1)} collective-permute-done((bf16[40,640]{1,0:T(8,128)(2,1)S(1)}, bf16[40,640]{1,0:T(8,128)(2,1)S(1)}, u32[]{:S(2)}, u32[]{:S(2)}) %collective-permute-start.9) | collective-permute-done | bytes 51232 | tf_op jit(solution)/shard_map/ppermute | solution.py:175
  151.7 3.9 %collective-permute-start.10 = (bf16[40,640]{1,0:T(8,128)(2,1)S(1)}, bf16[40,640]{1,0:T(8,128)(2,1)S(1)}, u32[]{:S(2)}, u32[]{:S(2)}) collective-permute-start(bf16[40,640]{1,0:T(8,128)(2,1)S(1)} %add_convert_fusion.3), channel_id=1, source_target_pairs={{0,128},{1,129},{2,130},{3,131},{4,132},{5,133},{6,134},{7,135},{8... | collective-permute-start | bytes 153608 | tf_op jit(solution)/shard_map/ppermute | solution.py:175
  155.6 10.9 %collective-permute-done.10 = bf16[40,640]{1,0:T(8,128)(2,1)S(1)} collective-permute-done((bf16[40,640]{1,0:T(8,128)(2,1)S(1)}, bf16[40,640]{1,0:T(8,128)(2,1)S(1)}, u32[]{:S(2)}, u32[]{:S(2)}) %collective-permute-start.10) | collective-permute-done | bytes 51232 | tf_op jit(solution)/shard_map/ppermute | solution.py:175
  166.5 1.9 collective-permute-start.13
  168.5 1.9 collective-permute-start.12
  170.4 5.4 %collective-permute-start.11 = (bf16[40,640]{1,0:T(8,128)(2,1)S(1)}, bf16[40,640]{1,0:T(8,128)(2,1)S(1)}, u32[]{:S(2)}, u32[]{:S(2)}) collective-permute-start(bf16[40,640]{1,0:T(8,128)(2,1)S(1)} %multiply_convert_fusion), channel_id=1, source_target_pairs={{0,272},{1,273},{2,274},{3,275},{4,276},{5,277},{6,278},{7,279},{8... | collective-permute-start | bytes 153608 | tf_op jit(solution)/shard_map/ppermute | solution.py:175
  175.9 2.0 %collective-permute-done.11 = bf16[40,640]{1,0:T(8,128)(2,1)S(1)} collective-permute-done((bf16[40,640]{1,0:T(8,128)(2,1)S(1)}, bf16[40,640]{1,0:T(8,128)(2,1)S(1)}, u32[]{:S(2)}, u32[]{:S(2)}) %collective-permute-start.11) | collective-permute-done | bytes 51232 | tf_op jit(solution)/shard_map/ppermute | solution.py:175
  177.9 0.7 maximum_select_fusion
  178.7 8.5 %backward_attention.1 = bf16[256,896]{1,0:T(8,128)(2,1)} custom-call(bf16[256,896]{1,0:T(8,128)(2,1)S(1)} %copy-done.1, f32[5,256,128]{2,1,0:T(8,128)S(1)} %get-tuple-element.6.prob_ref, bf16[256,2560]{1,0:T(8,128)(2,1)S(1)} %copy-done, bf16[640,5120]{1,0:T(8,128)(2,1)} %all-gather.2.cloned.1.call-done.w_ref), custom_call_target="tpu_custom_call" | custom-call | flops 2000000000 | bytes 6000000 | tf_op jit(solution)/shard_map/backward_attention/pallas_call | solution.py:113
  187.2 5.3 %frozen_projection.1 = bf16[256,2560]{1,0:T(8,128)(2,1)} custom-call(s32[1]{0:T(128)} %bitcast.17.live_ref, bf16[256,640]{1,0:T(8,128)(2,1)S(1)} %bitcast.27, bf16[640,5120]{1,0:T(8,128)(2,1)} %all-gather.2.cloned.1.call-done.w_ref), custom_call_target="tpu_custom_call" | custom-call | flops 1000000000 | bytes 5000000 | tf_op jit(solution)/shard_map/frozen_projection/pallas_call | solution.py:140
  (51 shorter events, 0.6 us)
Async XLA Ops:
  7.2 2.2 %copy-start.1 = (bf16[256,896]{1,0:T(8,128)(2,1)S(1)}, bf16[256,896]{1,0:T(8,128)(2,1)}, u32[]{:S(2)}) copy-start(bf16[256,896]{1,0:T(8,128)(2,1)} %x_ref.1) | copy-start | bytes 1376260
  7.2 2.2 %copy-start.4 = (s32[256]{0:T(256)S(1)}, s32[256]{0:T(256)}, u32[]{:S(2)}) copy-start(s32[256]{0:T(256)} %param.15) | copy-start | bytes 3076
  7.2 2.2 %copy-start.2 = (bf16[256,896]{1,0:T(8,128)(2,1)S(1)}, bf16[256,896]{1,0:T(8,128)(2,1)}, u32[]{:S(2)}) copy-start(bf16[256,896]{1,0:T(8,128)(2,1)} %nxt_ref.1) | copy-start | bytes 1376260
  7.2 2.2 %copy-start.3 = (s32[256]{0:T(256)S(1)}, s32[256]{0:T(256)}, u32[]{:S(2)}) copy-start(s32[256]{0:T(256)} %param.12) | copy-start | bytes 3076
  7.2 171.4 %all-gather.2.cloned.1.call-start = ((), (), s32[]{:S(2)}) async-start(), calls=%async_computation | async-start | bytes 6963200 | tf_op jit(solution)/shard_map/all_gather | solution.py:252
  9.4 6.3 %copy-start = (bf16[256,2560]{1,0:T(8,128)(2,1)S(1)}, bf16[256,2560]{1,0:T(8,128)(2,1)}, u32[]{:S(2)}) copy-start(bf16[256,2560]{1,0:T(8,128)(2,1)} %g_ref.1) | copy-start | bytes 3932164
  15.7 4.5 %copy-start.9 = (s32[1,1,5]{2,1,0:T(1,128)S(1)}, s32[1,1,5]{2,1,0:T(1,128)}, u32[]{:S(2)}) copy-start(s32[1,1,5]{2,1,0:T(1,128)} %param.17) | copy-start | bytes 64
  17.7 33.8 %collective-permute-start = (bf16[320,2560]{1,0:T(8,128)(2,1)}, bf16[320,2560]{1,0:T(8,128)(2,1)}, u32[]{:S(2)}, u32[]{:S(2)}) collective-permute-start(bf16[320,2560]{1,0:T(8,128)(2,1)} %convolution_convert_fusion), channel_id=1, source_target_pairs={{0,1},{1,0},{2,3},{3,2},{4,5},{5,4},{6,7},{7,6},{8,9},{9,8},{10,11... | collective-permute-start | bytes 4915208 | tf_op jit(solution)/shard_map/ppermute | solution.py:194
  22.3 9.2 %collective-permute-start.14 = (bf16[144,640]{1,0:T(8,128)(2,1)S(1)}, bf16[144,640]{1,0:T(8,128)(2,1)}, u32[]{:S(2)}, u32[]{:S(2)}) collective-permute-start(bf16[144,640]{1,0:T(8,128)(2,1)S(1)} %concatenate.43), channel_id=1, source_target_pairs={{0,16},{1,17},{2,18},{3,19},{4,20},{5,21},{6,22},{7,23},{8,24},{9,... | collective-permute-start | bytes 552968 | tf_op jit(solution)/shard_map/ppermute | solution.py:175
  35.6 14.0 %collective-permute-start.15 = (bf16[144,640]{1,0:T(8,128)(2,1)}, bf16[144,640]{1,0:T(8,128)(2,1)S(1)}, u32[]{:S(2)}, u32[]{:S(2)}) collective-permute-start(bf16[144,640]{1,0:T(8,128)(2,1)} %concatenate.44), channel_id=1, source_target_pairs={{0,32},{1,33},{2,34},{3,35},{4,36},{5,37},{6,38},{7,39},{8,40},{9,... | collective-permute-start | bytes 552968 | tf_op jit(solution)/shard_map/ppermute | solution.py:175
  49.6 16.0 %copy-start.6 = (bf16[144,640]{1,0:T(8,128)(2,1)}, bf16[144,640]{1,0:T(8,128)(2,1)S(1)}, u32[]{:S(2)}) copy-start(bf16[144,640]{1,0:T(8,128)(2,1)S(1)} %collective-permute-done.15) | copy-start | bytes 552964
  53.6 12.0 %copy-start.5 = (bf16[320,2560]{1,0:T(8,128)(2,1)}, bf16[320,2560]{1,0:T(8,128)(2,1)S(1)}, u32[]{:S(2)}) copy-start(bf16[320,2560]{1,0:T(8,128)(2,1)S(1)} %add_convert_fusion) | copy-start | bytes 4915204
  54.7 35.9 %collective-permute-start.1 = (bf16[80,2560]{1,0:T(8,128)(2,1)}, bf16[80,2560]{1,0:T(8,128)(2,1)}, u32[]{:S(2)}, u32[]{:S(2)}) collective-permute-start(bf16[80,2560]{1,0:T(8,128)(2,1)} %get-tuple-element.15), channel_id=1, source_target_pairs={{0,2},{1,3},{2,4},{3,5},{4,6},{5,7},{6,0},{7,1},{8,10},{9,11},{10,... | collective-permute-start | bytes 1228808 | tf_op jit(solution)/shard_map/ppermute | solution.py:197
  58.1 32.5 %collective-permute-start.3 = (bf16[80,2560]{1,0:T(8,128)(2,1)}, bf16[80,2560]{1,0:T(8,128)(2,1)}, u32[]{:S(2)}, u32[]{:S(2)}) collective-permute-start(bf16[80,2560]{1,0:T(8,128)(2,1)} %get-tuple-element.16), channel_id=1, source_target_pairs={{0,6},{1,7},{2,0},{3,1},{4,2},{5,3},{6,4},{7,5},{8,14},{9,15},{10,... | collective-permute-start | bytes 1228808 | tf_op jit(solution)/shard_map/ppermute | solution.py:197
  61.8 28.9 %collective-permute-start.2 = (bf16[80,2560]{1,0:T(8,128)(2,1)}, bf16[80,2560]{1,0:T(8,128)(2,1)}, u32[]{:S(2)}, u32[]{:S(2)}) collective-permute-start(bf16[80,2560]{1,0:T(8,128)(2,1)} %get-tuple-element.17), channel_id=1, source_target_pairs={{0,4},{1,5},{2,6},{3,7},{4,0},{5,1},{6,2},{7,3},{8,12},{9,13},{10,... | collective-permute-start | bytes 1228808 | tf_op jit(solution)/shard_map/ppermute | solution.py:197
  65.6 23.3 %collective-permute-start.16 = (bf16[144,640]{1,0:T(8,128)(2,1)S(1)}, bf16[144,640]{1,0:T(8,128)(2,1)S(1)}, u32[]{:S(2)}, u32[]{:S(2)}) collective-permute-start(bf16[144,640]{1,0:T(8,128)(2,1)S(1)} %concatenate.45), channel_id=1, source_target_pairs={{0,64},{1,65},{2,66},{3,67},{4,68},{5,69},{6,70},{7,71},{8,72},{9,... | collective-permute-start | bytes 552968 | tf_op jit(solution)/shard_map/ppermute | solution.py:175
  88.9 10.9 %copy-start.8 = (bf16[144,640]{1,0:T(8,128)(2,1)}, bf16[144,640]{1,0:T(8,128)(2,1)S(1)}, u32[]{:S(2)}) copy-start(bf16[144,640]{1,0:T(8,128)(2,1)S(1)} %collective-permute-done.16) | copy-start | bytes 552964
  90.7 12.2 %copy-start.7 = (bf16[144,640]{1,0:T(8,128)(2,1)S(1)}, bf16[144,640]{1,0:T(8,128)(2,1)}, u32[]{:S(2)}) copy-start(bf16[144,640]{1,0:T(8,128)(2,1)} %copy-done.6) | copy-start | bytes 552964
  92.4 24.6 %collective-permute-start.4 = (bf16[40,1280]{1,0:T(8,128)(2,1)S(1)}, bf16[40,1280]{1,0:T(8,128)(2,1)S(1)}, u32[]{:S(2)}, u32[]{:S(2)}) collective-permute-start(bf16[40,1280]{1,0:T(8,128)(2,1)S(1)} %get-tuple-element.18), channel_id=1, source_target_pairs={{0,256},{1,257},{2,258},{3,259},{4,260},{5,261},{6,262},{7,263},{8... | collective-permute-start | bytes 307208 | tf_op jit(solution)/shard_map/ppermute | solution.py:175
  95.1 21.9 %collective-permute-start.5 = (bf16[40,1280]{1,0:T(8,128)(2,1)S(1)}, bf16[40,1280]{1,0:T(8,128)(2,1)S(1)}, u32[]{:S(2)}, u32[]{:S(2)}) collective-permute-start(bf16[40,1280]{1,0:T(8,128)(2,1)S(1)} %get-tuple-element.19), channel_id=1, source_target_pairs={{0,8},{1,9},{2,10},{3,11},{4,12},{5,13},{6,14},{7,15},{8,0},{9,1},... | collective-permute-start | bytes 307208 | tf_op jit(solution)/shard_map/ppermute | solution.py:175
  99.8 17.2 %collective-permute-start.6 = (bf16[40,1280]{1,0:T(8,128)(2,1)S(1)}, bf16[40,1280]{1,0:T(8,128)(2,1)S(1)}, u32[]{:S(2)}, u32[]{:S(2)}) collective-permute-start(bf16[40,1280]{1,0:T(8,128)(2,1)S(1)} %get-tuple-element.20), channel_id=1, source_target_pairs={{0,264},{1,265},{2,266},{3,267},{4,268},{5,269},{6,270},{7,271},{8... | collective-permute-start | bytes 307208 | tf_op jit(solution)/shard_map/ppermute | solution.py:175
  103.9 29.1 %collective-permute-start.17 = (bf16[144,640]{1,0:T(8,128)(2,1)S(1)}, bf16[144,640]{1,0:T(8,128)(2,1)S(1)}, u32[]{:S(2)}, u32[]{:S(2)}) collective-permute-start(bf16[144,640]{1,0:T(8,128)(2,1)S(1)} %concatenate.46), channel_id=1, source_target_pairs={{0,128},{1,129},{2,130},{3,131},{4,132},{5,133},{6,134},{7,135},{8... | collective-permute-start | bytes 552968 | tf_op jit(solution)/shard_map/ppermute | solution.py:175
  117.1 17.7 %collective-permute-start.7 = (bf16[40,640]{1,0:T(8,128)(2,1)S(1)}, bf16[40,640]{1,0:T(8,128)(2,1)S(1)}, u32[]{:S(2)}, u32[]{:S(2)}) collective-permute-start(bf16[40,640]{1,0:T(8,128)(2,1)S(1)} %broadcast_select_fusion.16), channel_id=1, source_target_pairs={{0,16},{1,17},{2,18},{3,19},{4,20},{5,21},{6,22},{7,23},{8,24},{9,... | collective-permute-start | bytes 153608 | tf_op jit(solution)/shard_map/ppermute | solution.py:175
  134.8 6.9 %collective-permute-start.8 = (bf16[40,640]{1,0:T(8,128)(2,1)S(1)}, bf16[40,640]{1,0:T(8,128)(2,1)S(1)}, u32[]{:S(2)}, u32[]{:S(2)}) collective-permute-start(bf16[40,640]{1,0:T(8,128)(2,1)S(1)} %add_convert_fusion.5), channel_id=1, source_target_pairs={{0,32},{1,33},{2,34},{3,35},{4,36},{5,37},{6,38},{7,39},{8,40},{9,... | collective-permute-start | bytes 153608 | tf_op jit(solution)/shard_map/ppermute | solution.py:175
  136.8 7.4 %collective-permute-start.18 = (bf16[144,640]{1,0:T(8,128)(2,1)S(1)}, bf16[144,640]{1,0:T(8,128)(2,1)S(1)}, u32[]{:S(2)}, u32[]{:S(2)}) collective-permute-start(bf16[144,640]{1,0:T(8,128)(2,1)S(1)} %concatenate.47), channel_id=1, source_target_pairs={{0,256},{1,257},{2,258},{3,259},{4,260},{5,261},{6,262},{7,263},{8... | collective-permute-start | bytes 552968 | tf_op jit(solution)/shard_map/ppermute | solution.py:175
  141.7 9.9 %collective-permute-start.9 = (bf16[40,640]{1,0:T(8,128)(2,1)S(1)}, bf16[40,640]{1,0:T(8,128)(2,1)S(1)}, u32[]{:S(2)}, u32[]{:S(2)}) collective-permute-start(bf16[40,640]{1,0:T(8,128)(2,1)S(1)} %add_convert_fusion.4), channel_id=1, source_target_pairs={{0,64},{1,65},{2,66},{3,67},{4,68},{5,69},{6,70},{7,71},{8,72},{9,... | collective-permute-start | bytes 153608 | tf_op jit(solution)/shard_map/ppermute | solution.py:175
  151.7 14.8 %collective-permute-start.10 = (bf16[40,640]{1,0:T(8,128)(2,1)S(1)}, bf16[40,640]{1,0:T(8,128)(2,1)S(1)}, u32[]{:S(2)}, u32[]{:S(2)}) collective-permute-start(bf16[40,640]{1,0:T(8,128)(2,1)S(1)} %add_convert_fusion.3), channel_id=1, source_target_pairs={{0,128},{1,129},{2,130},{3,131},{4,132},{5,133},{6,134},{7,135},{8... | collective-permute-start | bytes 153608 | tf_op jit(solution)/shard_map/ppermute | solution.py:175
  166.5 9.3 %collective-permute-start.13 = (bf16[40,640]{1,0:T(8,128)(2,1)S(1)}, bf16[40,640]{1,0:T(8,128)(2,1)S(1)}, u32[]{:S(2)}, u32[]{:S(2)}) collective-permute-start(bf16[40,640]{1,0:T(8,128)(2,1)S(1)} %multiply_convert_fusion), channel_id=1, source_target_pairs={{0,16},{1,17},{2,18},{3,19},{4,20},{5,21},{6,22},{7,23},{8,24},{9,... | collective-permute-start | bytes 153608 | tf_op jit(solution)/shard_map/ppermute | solution.py:175
  168.5 7.4 %collective-permute-start.12 = (bf16[40,640]{1,0:T(8,128)(2,1)S(1)}, bf16[40,640]{1,0:T(8,128)(2,1)S(1)}, u32[]{:S(2)}, u32[]{:S(2)}) collective-permute-start(bf16[40,640]{1,0:T(8,128)(2,1)S(1)} %multiply_convert_fusion), channel_id=1, source_target_pairs={{0,256},{1,257},{2,258},{3,259},{4,260},{5,261},{6,262},{7,263},{8... | collective-permute-start | bytes 153608 | tf_op jit(solution)/shard_map/ppermute | solution.py:175
  170.4 7.5 %collective-permute-start.11 = (bf16[40,640]{1,0:T(8,128)(2,1)S(1)}, bf16[40,640]{1,0:T(8,128)(2,1)S(1)}, u32[]{:S(2)}, u32[]{:S(2)}) collective-permute-start(bf16[40,640]{1,0:T(8,128)(2,1)S(1)} %multiply_convert_fusion), channel_id=1, source_target_pairs={{0,272},{1,273},{2,274},{3,275},{4,276},{5,277},{6,278},{7,279},{8... | collective-permute-start | bytes 153608 | tf_op jit(solution)/shard_map/ppermute | solution.py:175
Sparse Core Ops, SparseCore 0:
  11.9 83.3 all-gather.1

commit v2 on v1

v2 whole, which is shorter than its diff:
```python
import functools
import math

import jax
import jax.numpy as jnp
from jax import lax
from jax.experimental import pallas as pl
from jax.experimental.pallas import tpu as pltpu
from jax.sharding import PartitionSpec as P

HD = 128
HQ = 5
ALIGNED_ROWS = 128
SLOT_NUMBER = 2
QW = HQ * HD
QKV = (HQ + 2) * HD
D = 2560
SCALE = 1.0 / math.sqrt(HD)
MASKED = -1e30
ABSENT = 1024.0
COSTS = {f"move_step_{level}": (flops * 10**9, 0) for level, flops in ((1, 4), (2, 4), (3, 16), (4, 8))}
N_DP = 32
N_FSDP = 16
VMEM = 20 * 1024 * 1024

NN = (((1,), (0,)), ((), ()))
NT = (((1,), (1,)), ((), ()))
TN = (((0,), (0,)), ((), ()))


def dot(a, b, dims):
    return lax.dot_general(a, b, dims, preferred_element_type=jnp.float32)


def block_probs(x_ref, rows, allowed, h):
    q = x_ref[rows, h * HD : (h + 1) * HD]
    k = x_ref[rows, QW : QW + HD]
    s = jnp.where(allowed, dot(q, k, NT) * SCALE, MASKED)
    e = jnp.exp(s - jnp.max(s, axis=-1, keepdims=True))
    return e / jnp.sum(e, axis=-1, keepdims=True)


def allowed_pairs(seg_ref, b):
    key_seg = jnp.broadcast_to(seg_ref[b : b + 1, :].astype(jnp.float32), (ALIGNED_ROWS, ALIGNED_ROWS))
    query_pos = lax.broadcasted_iota(jnp.int32, key_seg.shape, 0)
    key_pos = lax.broadcasted_iota(jnp.int32, key_seg.shape, 1)
    return (query_pos >= key_pos) & (key_seg == key_seg.T)


def call(kernel, out_shape, scratch=(), cost=(10**8, 10**6), name=None, **specs):
    flops, moved = COSTS.get(name, cost)
    return pl.pallas_call(
        kernel,
        out_shape=out_shape,
        scratch_shapes=list(scratch),
        compiler_params=pltpu.CompilerParams(vmem_limit_bytes=VMEM),
        cost_estimate=pl.CostEstimate(flops=flops, bytes_accessed=moved, transcendentals=0),
        name=name,
        **specs,
    )


def bf16(*shape):
    return jax.ShapeDtypeStruct(shape, jnp.bfloat16)


LIVE, PLAN = 0, 1


def column_blocks(ref):
    return [slice(i, i + HD) for i in range(0, ref.shape[-1], HD)]


def attend(x_ref, seg_ref, out_ref, prob_ref=None):
    for b in range(2):
        rows = slice(b * ALIGNED_ROWS, (b + 1) * ALIGNED_ROWS)
        allowed = allowed_pairs(seg_ref, b)
        for h in range(HQ):
            p = block_probs(x_ref, rows, allowed, h)
            if prob_ref is not None:
                prob_ref[h, rows, :] = p
            v = x_ref[rows, QW + HD :]
            out_ref[rows, h * HD : (h + 1) * HD] = dot(p.astype(jnp.bfloat16), v, NN).astype(jnp.bfloat16)


def move(level, live, table_ref, slots_ref, block_ref, arrived_ref=None, slots_out=None):
    square = (ALIGNED_ROWS, HD)
    slot_rows = slice(0, ALIGNED_ROWS), slice(ALIGNED_ROWS, 2 * ALIGNED_ROWS)
    if arrived_ref is not None:
        top = live - table_ref[PLAN + level - 1 : PLAN + level, :]
        present = (arrived_ref[0:1, 0:HD].astype(jnp.float32) < ABSENT / 2).astype(jnp.int32)
        live = top + present
        place = jnp.where(present == 1, top, -1)
    if block_ref is not None:
        count = table_ref[PLAN + level : PLAN + level + 1, :]
        leaving = jnp.broadcast_to(jnp.where(count > 0, jnp.maximum(live - count, 0), -1), square)
    for columns in column_blocks(slots_ref):
        slots = [slots_ref[rows, columns] for rows in slot_rows]
        if arrived_ref is not None:
            arrived = arrived_ref[:, columns]
            for s in range(SLOT_NUMBER):
                slots[s] = jnp.where(jnp.broadcast_to(place, square) == s, arrived, slots[s])
                slots_out[slot_rows[s], columns] = slots[s]
        if block_ref is not None:
            block = jnp.where(leaving == 0, slots[0], jnp.full(square, ABSENT, jnp.bfloat16))
            block_ref[:, columns] = jnp.where(leaving == 1, slots[1], block)
    return live


def next_kernel(table_ref, x_ref, seg_ref, out_ref, block_ref):
    attend(x_ref, seg_ref, out_ref)
    move(0, table_ref[LIVE : LIVE + 1, :], table_ref, out_ref, block_ref)


def next_attention(table, qkv, segments):
    rows = qkv.shape[0]
    return call(next_kernel, (bf16(rows, QW), bf16(ALIGNED_ROWS, QW)), name="next_attention")(table, qkv, segments)


def move_kernel(level, table_ref, live_ref, slots_ref, arrived_ref, slots_out, live_out, block_ref):
    live_out[...] = move(level, live_ref[...], table_ref, slots_ref, block_ref, arrived_ref, slots_out)


def move_step(level, table, live, slots, block):
    arrived = swap(block, 1 << (level - 1))
    return call(
        functools.partial(move_kernel, level),
        (bf16(*slots.shape), jax.ShapeDtypeStruct((1, HD), jnp.int32), bf16(*block.shape)),
        name=f"move_step_{level}",
    )(table, live, slots, arrived)


def current_kernel(x_ref, seg_ref, order_ref, keep_ref, send_ref, prob_ref, attn_ref):
    attend(x_ref, seg_ref, attn_ref, prob_ref)
    ordered = dot(attn_ref[...], order_ref[...], NN).astype(jnp.bfloat16)
    keep_ref[...] = ordered[:, : QW // 2]
    send_ref[...] = ordered[:, QW // 2 :]


def current_attention(qkv, segments, order):
    rows = qkv.shape[0]
    return call(
        current_kernel,
        (bf16(rows, QW // 2), bf16(rows, QW // 2), jax.ShapeDtypeStruct((HQ, rows, HD), jnp.float32)),
        [pltpu.VMEM((rows, QW), jnp.bfloat16)],
        name="current_attention",
    )(qkv, segments, order)


def grad_attention_kernel(g_ref, w_ref, out_ref):
    out_ref[...] = dot(g_ref[...], w_ref[...], NT).astype(jnp.bfloat16)


def grad_attention(grad_output, weights):
    rows = grad_output.shape[0]
    return call(
        grad_attention_kernel,
        bf16(rows, QW),
        name="grad_attention",
        cost=(10**9, 5 * 10**6),
        grid=(HQ,),
        in_specs=[pl.BlockSpec((rows, D), lambda i: (0, 0)), pl.BlockSpec((HD, D), lambda i: (i, 0))],
        out_specs=pl.BlockSpec((rows, HD), lambda i: (0, i)),
    )(grad_output, weights)


def backward_kernel(x_ref, prob_ref, ga_ref, out_ref):
    for b in range(2):
        rows = slice(b * ALIGNED_ROWS, (b + 1) * ALIGNED_ROWS)
        k = x_ref[rows, QW : QW + HD]
        v = x_ref[rows, QW + HD :]
        dk = jnp.zeros((ALIGNED_ROWS, HD), jnp.float32)
        dv = jnp.zeros((ALIGNED_ROWS, HD), jnp.float32)
        for h in range(HQ):
            head = slice(h * HD, (h + 1) * HD)
            ga = ga_ref[rows, head]
            q = x_ref[rows, head]
            p = prob_ref[h, rows, :]
            dp = dot(ga, v, NT)
            ds = p * (dp - jnp.sum(p * dp, axis=-1, keepdims=True))
            high = ds.astype(jnp.bfloat16)
            low = (ds - high.astype(jnp.float32)).astype(jnp.bfloat16)
            out_ref[rows, head] = ((dot(high, k, NN) + dot(low, k, NN)) * SCALE).astype(jnp.bfloat16)
            dk += dot(high, q, TN) + dot(low, q, TN)
            dv += dot(p.astype(jnp.bfloat16), ga, TN)
        out_ref[rows, QW : QW + HD] = (dk * SCALE).astype(jnp.bfloat16)
        out_ref[rows, QW + HD :] = dv.astype(jnp.bfloat16)


def frozen_kernel(level, table_ref, live_ref, slots_ref, arrived_ref, w_ref, out_ref, moved_ref):
    @pl.when(pl.program_id(0) == 0)
    def _():
        live = move(level, live_ref[...], table_ref, slots_ref, None, arrived_ref, moved_ref)
        for columns in column_blocks(moved_ref):
            for s in range(SLOT_NUMBER):
                rows = slice(s * ALIGNED_ROWS, (s + 1) * ALIGNED_ROWS)
                block = moved_ref[rows, columns]
                dead = jnp.broadcast_to(live, block.shape) <= s
                moved_ref[rows, columns] = jnp.where(dead, jnp.zeros_like(block), block)

    out_ref[...] = dot(moved_ref[...], w_ref[...], NN).astype(jnp.bfloat16)


def frozen_projection(table, live, slots, arrived, weights):
    rows = slots.shape[0]
    width = 512

    def whole(a):
        return pl.BlockSpec(a.shape, lambda i: (0, 0))

    return call(
        functools.partial(frozen_kernel, N_DP.bit_length() - 1),
        bf16(rows, D),
        [pltpu.VMEM((rows, QW), jnp.bfloat16)],
        (10**9, 5 * 10**6),
        "frozen_projection",
        grid=(D // width,),
        in_specs=[whole(a) for a in (table, live, slots, arrived)]
        + [pl.BlockSpec((QW, width), lambda i: (0, D // width + i))],
        out_specs=pl.BlockSpec((rows, width), lambda i: (0, i)),
    )(table, live, slots, arrived, weights)


def terms_kernel(a_ref, g_ref, out_ref):
    for i in range(0, D, 512):
        columns = slice(i, i + 512)
        out_ref[:, columns] = dot(a_ref[...], g_ref[:, columns], TN).astype(jnp.bfloat16)


def terms_to_send(attention, grad_output):
    return call(terms_kernel, bf16(QW // 2, D), name="terms_to_send")(attention, grad_output)


def terms_with_kernel(a_ref, g_ref, other_ref, out_ref):
    rows = QW // N_FSDP
    for i in range(0, D, 512):
        columns = slice(i, i + 512)
        total = dot(a_ref[...], g_ref[:, columns], TN) + other_ref[:, columns].astype(jnp.float32)
        for j in range(out_ref.shape[0]):
            out_ref[j, :, columns] = total[j * rows : (j + 1) * rows].astype(jnp.bfloat16)


def terms_with_other_core(attention, grad_output, other):
    return call(terms_with_kernel, bf16(N_FSDP // 2, QW // N_FSDP, D), name="terms_with_other_core")(
        attention, grad_output, other
    )


PEERS = 8
TILES = [(i, j) for i in range(0, QW // N_FSDP, 8) for j in range(0, D, HD)]
SHARE = -(-len(TILES) // PEERS)
SHARE_ROWS = -(-SHARE * 8 // 16) * 16


def group_sum_kernel(parts_ref, out_ref):
    shares = [[] for _ in range(PEERS)]
    for n, (i, j) in enumerate(TILES):
        if i == 0:
            columns = sum(parts_ref[p, :, j : j + HD].astype(jnp.float32) for p in range(parts_ref.shape[0]))
            for r in range(0, columns.shape[0], 8):
                at = TILES.index((r, j))
                shares[at // SHARE].append((at % SHARE, columns[r : r + 8]))
    for k, share in enumerate(shares):
        tiles = [tile for _, tile in sorted(share, key=lambda pair: pair[0])]
        tiles += [jnp.zeros_like(tiles[0])] * (SHARE_ROWS // 8 - len(tiles))
        out_ref[k] = jnp.concatenate(tiles, axis=0).astype(jnp.bfloat16)


def group_sum(parts):
    return call(group_sum_kernel, bf16(PEERS, SHARE_ROWS, HD), name="group_sum")(parts)


def share_sum_kernel(parts_ref, out_ref):
    out_ref[...] = sum(parts_ref[p].astype(jnp.float32) for p in range(PEERS)).astype(jnp.bfloat16)


def share_sum(parts):
    return call(share_sum_kernel, bf16(SHARE_ROWS, HD), name="share_sum")(parts)


def mean_kernel(total_ref, other_ref, out_ref):
    total = total_ref[...].astype(jnp.float32) + other_ref[...].astype(jnp.float32)
    mean = (total * (1.0 / (N_DP * N_FSDP))).astype(jnp.bfloat16)
    for p in range(PEERS):
        out_ref[p] = mean


def mean_for_all(total, other):
    return call(mean_kernel, bf16(PEERS, SHARE_ROWS, HD), name="mean_for_all")(total, other)


def join_kernel(shares_ref, out_ref):
    shares = [shares_ref[k].astype(jnp.float32) for k in range(PEERS)]
    for j in range(0, D, HD):
        tiles = []
        for i in range(0, QW // N_FSDP, 8):
            n = TILES.index((i, j))
            row = n % SHARE * 8
            tiles.append(shares[n // SHARE][row : row + 8])
        out_ref[:, j : j + HD] = jnp.concatenate(tiles, axis=0).astype(jnp.bfloat16)


def join(shares):
    return call(join_kernel, bf16(QW // N_FSDP, D), name="join")(shares)


def side_by_side_kernel(left, right, out_ref):
    out_ref[:, :D] = left[...]
    out_ref[:, D:] = right[...]


def gather_weights(policy_out, frozen_out):
    own = call(side_by_side_kernel, bf16(policy_out.shape[0], 2 * D), name="side_by_side")(policy_out, frozen_out)
    return lax.all_gather(own, "fsdp", axis=0, tiled=True)


def fsdp_pairs(flip, x_step):
    def target(j):
        j ^= flip
        return (j & 9) | (((j >> 1 & 3) + x_step) % 4 << 1)

    return [(j, target(j)) for j in range(N_FSDP)]


def all_pairs(dp_flip, fsdp_flip):
    return [
        (d * N_FSDP + j, (d ^ dp_flip) * N_FSDP + (j ^ fsdp_flip)) for d in range(N_DP) for j in range(N_FSDP)
    ]


def swap(a, dp_flip, fsdp_flip=0):
    return lax.ppermute(a, ("dp", "fsdp"), all_pairs(dp_flip, fsdp_flip))


def add(*terms):
    return sum(t.astype(jnp.float32) for t in terms).astype(jnp.bfloat16)


def after(a, *others):
    return lax.optimization_barrier((a, *others))[0]


def sum_order(me):
    rows = QW // N_FSDP
    natural = jnp.arange(QW, dtype=jnp.int32)
    j, k = natural // rows, natural % rows
    place = ((j ^ me) & 1) * (N_FSDP // 2) + (j >> 1)
    return (natural[None, :] == (place * rows + k)[:, None]).astype(jnp.bfloat16)


def body(
    policy_out,
    frozen_out,
    qkv_current,
    segment_current,
    grad_output,
    query_key_value_next,
    document_next,
    block_counts,
    move_plan,
):
    me = lax.axis_index("fsdp")
    group = lax.axis_index("dp")
    numbers = jnp.concatenate([block_counts.reshape(1), move_plan.reshape(5), jnp.zeros((2,), jnp.int32)])
    table = jnp.broadcast_to(numbers[:, None], (8, HD))
    same_core = [[j for j in range(N_FSDP) if j & 1 == core] for core in range(2)]
    near = [[y * 16 + 4 * q + z for y in range(2) for z in range(4)] for q in range(4)]

    slots, block = next_attention(table, query_key_value_next, document_next.reshape(SLOT_NUMBER, ALIGNED_ROWS))
    live = table[LIVE : LIVE + 1]
    weights = gather_weights(after(policy_out, slots), frozen_out)
    keep_half, send_half, probs = current_attention(
        after(qkv_current, slots), segment_current.reshape(2, ALIGNED_ROWS), sum_order(me)
    )
    slots, live, block = move_step(1, table, live, slots, block)
    other = lax.ppermute(terms_to_send(after(send_half, live), grad_output), "fsdp", fsdp_pairs(1, 0))
    slots, live, block = move_step(2, table, live, slots, block)
    parts = terms_with_other_core(keep_half, grad_output, other)
    parts = lax.all_to_all(after(parts, live), "fsdp", 0, 0, axis_index_groups=same_core)
    slots, live, block = move_step(3, table, live, slots, block)
    shares = group_sum(after(parts, live))
    shares = lax.all_to_all(shares, "dp", 0, 0, axis_index_groups=near)
    slots, live, block = move_step(4, table, live, slots, block)
    total = share_sum(after(shares, live))
    total = add(total, swap(total, 4))
    block = swap(block, 16)
    shares = mean_for_all(after(total, block), swap(total, 8))
    shares = lax.all_to_all(shares, "dp", 0, 0, axis_index_groups=near)
    gradient = grad_attention(grad_output, weights)
    qkv_gradient = call(backward_kernel, bf16(*qkv_current.shape), name="backward_attention", cost=(10**9, 2 * 10**6))(
        qkv_current, probs, gradient
    )
    frozen_layer_output = frozen_projection(table, live, slots, block, weights)
    weight_grad = join(after(shares, qkv_gradient, frozen_layer_output))
    return (qkv_gradient, weight_grad, frozen_layer_output)


def solution(mesh):
    return jax.shard_map(
        body,
        mesh=mesh,
        in_specs=(
            P("fsdp", None),
            P("fsdp", None),
            P(("dp", "fsdp"), None),
            P(("dp", "fsdp")),
            P(("dp", "fsdp"), None),
            P(("dp", "fsdp"), None),
            P(("dp", "fsdp")),
            P("dp", "fsdp"),
            P("dp", "fsdp", None),
        ),
        out_specs=(P(("dp", "fsdp"), None), P("fsdp", None), P(("dp", "fsdp"), None)),
        check_vma=False,
    )
```

time: 201 us -> 154 us (0.77)
  waiting for transfers between devices: 62.4 us -> 34.3 us
  starting transfers between devices: 75.1 us -> 63.7 us
  between operations: 25 us -> 14.9 us
  local copies, waits for them, and re-layouts: 5.85 us -> 13.2 us
  other arithmetic: 6.87 us -> 0.97 us
  matrix products: 4 us -> 0 us
  Pallas kernels: 20.1 us -> 24.1 us
    ppermute x15 -> x7, waiting for transfers between devices: 62.4 us -> 28.2 us  [swap(): return lax.ppermute(a, ('dp', 'fsdp'), all_pairs(dp_flip, fsdp_flip))]
    ppermute x15 -> x7, starting transfers between devices: 62.4 us -> 43.9 us  [swap(): return lax.ppermute(a, ('dp', 'fsdp'), all_pairs(dp_flip, fsdp_flip))]
    all_to_all x0 -> x3, starting transfers between devices: none -> 17.8 us  [the longest x2 10.5 us: body(): shares = lax.all_to_all(shares, 'dp', 0, 0, axis_index_groups=near)]
    unnamed x20 -> x32, local copies, waits for them, and re-layouts: 0.05 us -> 13.2 us
    ppermute x4 -> x1, starting transfers between devices: 12.7 us -> 1.92 us  [body(): lax.ppermute(terms_to_send(after(send_half, live), grad_output), 'fsdp',...]
    all_to_all x0 -> x3, waiting for transfers between devices: none -> 6.05 us  [the longest x1 4.31 us: body(): lax.all_to_all(after(parts, live), 'fsdp', 0, 0, axis_index_groups=same_c...]
    slice x7 -> x0, local copies, waits for them, and re-layouts: 5.05 us -> none  [the longest x5 3.29 us: move_blocks(): received = arrived[ALIGNED_ROWS, 0].astype(jnp.int32)]
    dot_general x2 -> x0, matrix products: 4 us -> none  [dot(): return lax.dot_general(a, b, dims, preferred_element_type=jnp.float32)]
  transfers between devices with their start and end apart: 20 -> 12, of which waited for: 9 -> 7; matrix products, arithmetic and copies ran while one was open for 7% -> 0% of each run, Pallas kernels for 3% -> 13%
where the time goes in v2:
time: 154 us; the launch traced here: 151 us
  starting transfers between devices  63.7 us (41%)
  waiting for transfers between devices  34.3 us (22%)
  Pallas kernels  24.1 us (16%)
  between operations  14.9 us (10%)
  local copies, waits for them, and re-layouts  13.2 us (9%)
    ppermute x7, starting transfers between devices, swap(): return lax.ppermute(a, ('dp', 'fsdp'), all_pairs(dp_flip, fsdp_flip))  43.9 us
    ppermute x7, waiting for transfers between devices, swap(): return lax.ppermute(a, ('dp', 'fsdp'), all_pairs(dp_flip, fsdp_flip))  28.2 us
    unnamed x32, local copies, waits for them, and re-layouts  13.2 us
    all_to_all x2, starting transfers between devices, body(): shares = lax.all_to_all(shares, 'dp', 0, 0, axis_index_groups=near)  10.5 us
    all_to_all x1, starting transfers between devices, body(): lax.all_to_all(after(parts, live), 'fsdp', 0, 0, axis_index_groups=same_c...  7.26 us
    all_to_all x1, waiting for transfers between devices, body(): lax.all_to_all(after(parts, live), 'fsdp', 0, 0, axis_index_groups=same_c...  4.31 us
    pallas_call x4, Pallas kernels, move_step(): call(functools.partial(move_kernel, level), (bf16(*slots.shape), jax.Shap...  3.57 us
    pallas_call x1, Pallas kernels, current_attention(): call(current_kernel, (bf16(rows, QW // 2), bf16(rows, QW // 2), jax.Shape...  3.51 us
  transfers between devices with their start and end apart: 12, of which 7 were waited for; matrix products, arithmetic and copies ran while one was open for 0% of the time, Pallas kernels for 13%

profile of v2, /device:TPU:24, one launch (start us, length us, event | category | flops | bytes accessed | tf_op | source)
XLA Modules:
  0.0 151.1 jit_solution(15206546579424405919)
XLA Ops:
  7.9 0.7 pad_add_fusion
  8.6 0.1 broadcast_in_dim.4.table_ref
  8.7 1.0 copy-done.4
  9.7 0.7 copy-done.8
  10.4 3.3 %next_attention.1 = (bf16[256,640]{1,0:T(8,128)(2,1)S(1)}, bf16[128,640]{1,0:T(8,128)(2,1)S(1)}) custom-call(s32[8,128]{1,0:T(8,128)S(1)} %broadcast_in_dim.4.table_ref, bf16[256,896]{1,0:T(8,128)(2,1)S(1)} %copy-done.4, s32[2,128]{1,0:T(2,128)S(1)} %bitcast.7), custom_call_target="tpu_custom_call" | custom-call | flops 100000000 | bytes 1000000 | tf_op jit(solution)/shard_map/next_attention/pallas_call | solution.py:117
  13.7 0.9 copy-done.6
  14.7 0.9 copy-done.7
  15.6 0.8 side_by_side.1
  16.4 3.8 %collective-permute-start = (bf16[128,640]{1,0:T(8,128)(2,1)S(1)}, bf16[128,640]{1,0:T(8,128)(2,1)S(1)}, u32[]{:S(2)}, u32[]{:S(2)}) collective-permute-start(bf16[128,640]{1,0:T(8,128)(2,1)S(1)} %get-tuple-element.34), channel_id=1, source_target_pairs={{0,16},{1,17},{2,18},{3,19},{4,20},{5,21},{6,22},{7,23},{8,24},{9,... | collective-permute-start | bytes 491528 | tf_op jit(solution)/shard_map/ppermute | solution.py:332
  20.2 0.2 fusion.order_ref
  20.5 3.5 %current_attention.1 = (bf16[256,320]{1,0:T(8,128)(2,1)S(1)}, bf16[256,320]{1,0:T(8,128)(2,1)S(1)}, f32[5,256,128]{2,1,0:T(8,128)S(1)}) custom-call(bf16[256,896]{1,0:T(8,128)(2,1)S(1)} %copy-done.5, s32[2,128]{1,0:T(2,128)S(1)} %bitcast.8, bf16[640,640]{1,0:T(8,128)(2,1)S(1)} %fusion.order_ref), custom_call_target="tpu_custom_call" | custom-call | flops 100000000 | bytes 1000000 | tf_op jit(solution)/shard_map/current_attention/pallas_call | solution.py:142
  24.0 0.8 copy-done.10
  24.8 0.1 move_step_1.1
  24.9 1.2 copy-done.2
  26.2 0.6 terms_to_send.1
  26.8 1.9 %collective-permute-start.1 = (bf16[320,2560]{1,0:T(8,128)(2,1)S(1)}, bf16[320,2560]{1,0:T(8,128)(2,1)S(1)}, u32[]{:S(2)}, u32[]{:S(2)}) collective-permute-start(bf16[320,2560]{1,0:T(8,128)(2,1)S(1)} %terms_to_send.1), channel_id=1, source_target_pairs={{0,1},{1,0},{2,3},{3,2},{4,5},{5,4},{6,7},{7,6},{8,9},{9,8},{10,11... | collective-permute-start | bytes 4915208 | tf_op jit(solution)/shard_map/ppermute | solution.py:376
  28.7 5.2 %collective-permute-start.2 = (bf16[128,640]{1,0:T(8,128)(2,1)S(1)}, bf16[128,640]{1,0:T(8,128)(2,1)S(1)}, u32[]{:S(2)}, u32[]{:S(2)}) collective-permute-start(bf16[128,640]{1,0:T(8,128)(2,1)S(1)} %get-tuple-element.38), channel_id=1, source_target_pairs={{0,32},{1,33},{2,34},{3,35},{4,36},{5,37},{6,38},{7,39},{8,40},{9,... | collective-permute-start | bytes 491528 | tf_op jit(solution)/shard_map/ppermute | solution.py:332
  33.9 8.4 %collective-permute-done.2.arrived_ref = bf16[128,640]{1,0:T(8,128)(2,1)S(1)} collective-permute-done((bf16[128,640]{1,0:T(8,128)(2,1)S(1)}, bf16[128,640]{1,0:T(8,128)(2,1)S(1)}, u32[]{:S(2)}, u32[]{:S(2)}) %collective-permute-start.2) | collective-permute-done | bytes 163872 | tf_op jit(solution)/shard_map/ppermute | solution.py:332
  42.2 0.8 move_step_2.1
  43.0 0.7 copy-done.12
  43.8 9.1 %collective-permute-start.3 = (bf16[128,640]{1,0:T(8,128)(2,1)}, bf16[128,640]{1,0:T(8,128)(2,1)}, u32[]{:S(2)}, u32[]{:S(2)}) collective-permute-start(bf16[128,640]{1,0:T(8,128)(2,1)} %get-tuple-element.42), channel_id=1, source_target_pairs={{0,64},{1,65},{2,66},{3,67},{4,68},{5,69},{6,70},{7,71},{8,72},{9,... | collective-permute-start | bytes 491528 | tf_op jit(solution)/shard_map/ppermute | solution.py:332
  52.9 0.6 terms_with_other_core.1
  53.5 1.3 copy-done.3
  54.8 7.3 %all-to-all-start = ((bf16[8,40,2560]{2,1,0:T(8,128)(2,1)}), bf16[8,40,2560]{2,1,0:T(8,128)(2,1)S(1)}, u32[]{:S(2)}, u32[]{:S(2)}) async-start(bf16[8,40,2560]{2,1,0:T(8,128)(2,1)} %copy-done.3), calls=%async_computation | async-start | bytes 3276800 | tf_op jit(solution)/shard_map/all_to_all | solution.py:379
  62.0 4.9 %collective-permute-done.3.arrived_ref = bf16[128,640]{1,0:T(8,128)(2,1)} collective-permute-done((bf16[128,640]{1,0:T(8,128)(2,1)}, bf16[128,640]{1,0:T(8,128)(2,1)}, u32[]{:S(2)}, u32[]{:S(2)}) %collective-permute-start.3) | collective-permute-done | bytes 163872 | tf_op jit(solution)/shard_map/ppermute | solution.py:332
  67.0 1.0 copy-done.13
  67.9 1.7 %move_step_3.1 = (bf16[256,640]{1,0:T(8,128)(2,1)S(1)}, s32[1,128]{1,0:T(1,128)S(1)}, bf16[128,640]{1,0:T(8,128)(2,1)}) custom-call(s32[8,128]{1,0:T(8,128)S(1)} %broadcast_in_dim.4.table_ref, s32[1,128]{1,0:T(1,128)S(1)} %get-tuple-element.39.live_ref, bf16[256,640]{1,0:T(8,128)(2,1)S(1)} %copy-done.13, bf16[128,640]{1,0:T(8,128)(2,1)} %collective-permute-done.3.arrived_ref), custom_call_target="tpu_custom_call" | custom-call | flops 16000000000 | tf_op jit(solution)/shard_map/move_step_3/pallas_call | solution.py:126
  69.6 0.7 copy-done.14
  70.4 12.3 %collective-permute-start.4 = (bf16[128,640]{1,0:T(8,128)(2,1)}, bf16[128,640]{1,0:T(8,128)(2,1)}, u32[]{:S(2)}, u32[]{:S(2)}) collective-permute-start(bf16[128,640]{1,0:T(8,128)(2,1)} %get-tuple-element.46), channel_id=1, source_target_pairs={{0,128},{1,129},{2,130},{3,131},{4,132},{5,133},{6,134},{7,135},{8... | collective-permute-start | bytes 491528 | tf_op jit(solution)/shard_map/ppermute | solution.py:332
  82.7 4.3 %all-to-all-done.parts_ref = bf16[8,40,2560]{2,1,0:T(8,128)(2,1)S(1)} async-done(((bf16[8,40,2560]{2,1,0:T(8,128)(2,1)}), bf16[8,40,2560]{2,1,0:T(8,128)(2,1)S(1)}, u32[]{:S(2)}, u32[]{:S(2)}) %all-to-all-start) | async-done | bytes 1638432 | tf_op jit(solution)/shard_map/all_to_all | solution.py:379
  87.0 0.9 group_sum.1
  87.9 6.1 %all-to-all-start.1 = ((bf16[8,112,128]{2,1,0:T(8,128)(2,1)}), bf16[8,112,128]{2,1,0:T(8,128)(2,1)S(1)}, u32[]{:S(2)}, u32[]{:S(2)}) async-start(bf16[8,112,128]{2,1,0:T(8,128)(2,1)} %group_sum.1), calls=%async_computation.1 | async-start | bytes 458752 | tf_op jit(solution)/shard_map/all_to_all | solution.py:382
  94.0 4.0 %collective-permute-done.4.arrived_ref = bf16[128,640]{1,0:T(8,128)(2,1)} collective-permute-done((bf16[128,640]{1,0:T(8,128)(2,1)}, bf16[128,640]{1,0:T(8,128)(2,1)}, u32[]{:S(2)}, u32[]{:S(2)}) %collective-permute-start.4) | collective-permute-done | bytes 163872 | tf_op jit(solution)/shard_map/ppermute | solution.py:332
  98.0 1.0 copy-done.15
  98.9 1.0 move_step_4.1
  100.0 1.7 %all-to-all-done.1.parts_ref = bf16[8,112,128]{2,1,0:T(8,128)(2,1)S(1)} async-done(((bf16[8,112,128]{2,1,0:T(8,128)(2,1)}), bf16[8,112,128]{2,1,0:T(8,128)(2,1)S(1)}, u32[]{:S(2)}, u32[]{:S(2)}) %all-to-all-start.1) | async-done | bytes 229408 | tf_op jit(solution)/shard_map/all_to_all | solution.py:382
  101.7 1.9 %collective-permute-start.5 = (bf16[112,128]{1,0:T(8,128)(2,1)S(1)}, bf16[112,128]{1,0:T(8,128)(2,1)S(1)}, u32[]{:S(2)}, u32[]{:S(2)}) collective-permute-start(bf16[112,128]{1,0:T(8,128)(2,1)S(1)} %share_sum.1), channel_id=1, source_target_pairs={{0,64},{1,65},{2,66},{3,67},{4,68},{5,69},{6,70},{7,71},{8,72},{9,... | collective-permute-start | bytes 86024 | tf_op jit(solution)/shard_map/ppermute | solution.py:332
  103.7 3.4 %collective-permute-start.6 = (bf16[128,640]{1,0:T(8,128)(2,1)S(1)}, bf16[128,640]{1,0:T(8,128)(2,1)S(1)}, u32[]{:S(2)}, u32[]{:S(2)}) collective-permute-start(bf16[128,640]{1,0:T(8,128)(2,1)S(1)} %get-tuple-element.49), channel_id=1, source_target_pairs={{0,256},{1,257},{2,258},{3,259},{4,260},{5,261},{6,262},{7,263},{8... | collective-permute-start | bytes 491528 | tf_op jit(solution)/shard_map/ppermute | solution.py:332
  107.0 4.7 %collective-permute-done.5 = bf16[112,128]{1,0:T(8,128)(2,1)S(1)} collective-permute-done((bf16[112,128]{1,0:T(8,128)(2,1)S(1)}, bf16[112,128]{1,0:T(8,128)(2,1)S(1)}, u32[]{:S(2)}, u32[]{:S(2)}) %collective-permute-start.5) | collective-permute-done | bytes 28704 | tf_op jit(solution)/shard_map/ppermute | solution.py:332
  111.7 8.2 %collective-permute-start.7 = (bf16[112,128]{1,0:T(8,128)(2,1)S(1)}, bf16[112,128]{1,0:T(8,128)(2,1)S(1)}, u32[]{:S(2)}, u32[]{:S(2)}) collective-permute-start(bf16[112,128]{1,0:T(8,128)(2,1)S(1)} %add_convert_fusion.total_ref), channel_id=1, source_target_pairs={{0,128},{1,129},{2,130},{3,131},{4,132},{5,133},{6,134},{7,135},{8... | collective-permute-start | bytes 86024 | tf_op jit(solution)/shard_map/ppermute | solution.py:332
  120.0 6.2 %collective-permute-done.7.other_ref = bf16[112,128]{1,0:T(8,128)(2,1)S(1)} collective-permute-done((bf16[112,128]{1,0:T(8,128)(2,1)S(1)}, bf16[112,128]{1,0:T(8,128)(2,1)S(1)}, u32[]{:S(2)}, u32[]{:S(2)}) %collective-permute-start.7) | collective-permute-done | bytes 28704 | tf_op jit(solution)/shard_map/ppermute | solution.py:332
  126.2 0.7 mean_for_all.1
  127.0 4.5 %all-to-all-start.2 = ((bf16[8,112,128]{2,1,0:T(8,128)(2,1)}), bf16[8,112,128]{2,1,0:T(8,128)(2,1)S(1)}, u32[]{:S(2)}, u32[]{:S(2)}) async-start(bf16[8,112,128]{2,1,0:T(8,128)(2,1)} %mean_for_all.1), calls=%async_computation.2 | async-start | bytes 458752 | tf_op jit(solution)/shard_map/all_to_all | solution.py:388
  131.4 2.9 %copy-done = bf16[640,5120]{1,0:T(8,128)(2,1)S(1)} copy-done((bf16[640,5120]{1,0:T(8,128)(2,1)S(1)}, bf16[640,5120]{1,0:T(8,128)(2,1)}, u32[]{:S(2)}) %copy-start) | copy-done | bytes 6553624
  134.3 2.8 %grad_attention.1.ga_ref = bf16[256,640]{1,0:T(8,128)(2,1)S(1)} custom-call(bf16[256,2560]{1,0:T(8,128)(2,1)S(1)} %copy-done.2, bf16[640,5120]{1,0:T(8,128)(2,1)S(1)} %copy-done), custom_call_target="tpu_custom_call" | custom-call | flops 1000000000 | bytes 5000000 | tf_op jit(solution)/shard_map/grad_attention/pallas_call | solution.py:156
  137.1 3.0 %backward_attention.1 = bf16[256,896]{1,0:T(8,128)(2,1)} custom-call(bf16[256,896]{1,0:T(8,128)(2,1)S(1)} %copy-done.5, f32[5,256,128]{2,1,0:T(8,128)S(1)} %copy-done.11, bf16[256,640]{1,0:T(8,128)(2,1)S(1)} %grad_attention.1.ga_ref), custom_call_target="tpu_custom_call" | custom-call | flops 1000000000 | bytes 2000000 | tf_op jit(solution)/shard_map/backward_attention/pallas_call | solution.py:390
  140.1 3.5 %frozen_projection.1 = bf16[256,2560]{1,0:T(8,128)(2,1)} custom-call(s32[8,128]{1,0:T(8,128)S(1)} %broadcast_in_dim.4.table_ref, s32[1,128]{1,0:T(1,128)S(1)} %get-tuple-element.47.live_ref, bf16[256,640]{1,0:T(8,128)(2,1)S(1)} %get-tuple-element.51.slots_ref, bf16[128,640]{1,0:T(8,128)(2,1)S(1)} %collective-permute-done.6.arrived_ref, ...), custom_call_target="tpu_custom_call" | custom-call | flops 1000000000 | bytes 5000000 | tf_op jit(solution)/shard_map/frozen_projection/pallas_call | solution.py:211
  143.6 0.7 join.1
  (32 shorter events, 0.2 us)
Async XLA Ops:
  7.2 13.3 %copy-start.9 = (s32[256]{0:T(256)S(1)}, s32[256]{0:T(256)}, u32[]{:S(2)}) copy-start(s32[256]{0:T(256)} %param.12) | copy-start | bytes 3076
  7.2 124.2 %all-gather.2.cloned.1.call-start = ((), (), s32[]{:S(2)}) async-start(), calls=%async_computation.3 | async-start | bytes 6963200 | tf_op jit(solution)/shard_map/all_gather | solution.py:314
  8.7 1.0 copy-start.4
  9.7 0.7 copy-start.8
  10.4 10.1 %copy-start.5 = (bf16[256,896]{1,0:T(8,128)(2,1)S(1)}, bf16[256,896]{1,0:T(8,128)(2,1)}, u32[]{:S(2)}) copy-start(bf16[256,896]{1,0:T(8,128)(2,1)} %x_ref.4) | copy-start | bytes 1376260
  13.7 0.9 copy-start.6
  14.7 0.9 copy-start.7
  16.4 8.4 %collective-permute-start = (bf16[128,640]{1,0:T(8,128)(2,1)S(1)}, bf16[128,640]{1,0:T(8,128)(2,1)S(1)}, u32[]{:S(2)}, u32[]{:S(2)}) collective-permute-start(bf16[128,640]{1,0:T(8,128)(2,1)S(1)} %get-tuple-element.34), channel_id=1, source_target_pairs={{0,16},{1,17},{2,18},{3,19},{4,20},{5,21},{6,22},{7,23},{8,24},{9,... | collective-permute-start | bytes 491528 | tf_op jit(solution)/shard_map/ppermute | solution.py:332
  24.0 0.8 copy-start.10
  24.8 1.3 copy-start.2
  26.8 26.1 %collective-permute-start.1 = (bf16[320,2560]{1,0:T(8,128)(2,1)S(1)}, bf16[320,2560]{1,0:T(8,128)(2,1)S(1)}, u32[]{:S(2)}, u32[]{:S(2)}) collective-permute-start(bf16[320,2560]{1,0:T(8,128)(2,1)S(1)} %terms_to_send.1), channel_id=1, source_target_pairs={{0,1},{1,0},{2,3},{3,2},{4,5},{5,4},{6,7},{7,6},{8,9},{9,8},{10,11... | collective-permute-start | bytes 4915208 | tf_op jit(solution)/shard_map/ppermute | solution.py:376
  28.7 13.5 %collective-permute-start.2 = (bf16[128,640]{1,0:T(8,128)(2,1)S(1)}, bf16[128,640]{1,0:T(8,128)(2,1)S(1)}, u32[]{:S(2)}, u32[]{:S(2)}) collective-permute-start(bf16[128,640]{1,0:T(8,128)(2,1)S(1)} %get-tuple-element.38), channel_id=1, source_target_pairs={{0,32},{1,33},{2,34},{3,35},{4,36},{5,37},{6,38},{7,39},{8,40},{9,... | collective-permute-start | bytes 491528 | tf_op jit(solution)/shard_map/ppermute | solution.py:332
  43.0 0.7 copy-start.12
  43.8 23.2 %collective-permute-start.3 = (bf16[128,640]{1,0:T(8,128)(2,1)}, bf16[128,640]{1,0:T(8,128)(2,1)}, u32[]{:S(2)}, u32[]{:S(2)}) collective-permute-start(bf16[128,640]{1,0:T(8,128)(2,1)} %get-tuple-element.42), channel_id=1, source_target_pairs={{0,64},{1,65},{2,66},{3,67},{4,68},{5,69},{6,70},{7,71},{8,72},{9,... | collective-permute-start | bytes 491528 | tf_op jit(solution)/shard_map/ppermute | solution.py:332
  53.5 1.3 copy-start.3
  54.8 32.2 %all-to-all-start = ((bf16[8,40,2560]{2,1,0:T(8,128)(2,1)}), bf16[8,40,2560]{2,1,0:T(8,128)(2,1)S(1)}, u32[]{:S(2)}, u32[]{:S(2)}) async-start(bf16[8,40,2560]{2,1,0:T(8,128)(2,1)} %copy-done.3), calls=%async_computation | async-start | bytes 3276800 | tf_op jit(solution)/shard_map/all_to_all | solution.py:379
  67.0 1.0 copy-start.13
  69.6 0.7 copy-start.14
  70.4 27.6 %collective-permute-start.4 = (bf16[128,640]{1,0:T(8,128)(2,1)}, bf16[128,640]{1,0:T(8,128)(2,1)}, u32[]{:S(2)}, u32[]{:S(2)}) collective-permute-start(bf16[128,640]{1,0:T(8,128)(2,1)} %get-tuple-element.46), channel_id=1, source_target_pairs={{0,128},{1,129},{2,130},{3,131},{4,132},{5,133},{6,134},{7,135},{8... | collective-permute-start | bytes 491528 | tf_op jit(solution)/shard_map/ppermute | solution.py:332
  87.9 13.8 %all-to-all-start.1 = ((bf16[8,112,128]{2,1,0:T(8,128)(2,1)}), bf16[8,112,128]{2,1,0:T(8,128)(2,1)S(1)}, u32[]{:S(2)}, u32[]{:S(2)}) async-start(bf16[8,112,128]{2,1,0:T(8,128)(2,1)} %group_sum.1), calls=%async_computation.1 | async-start | bytes 458752 | tf_op jit(solution)/shard_map/all_to_all | solution.py:382
  98.0 1.0 copy-start.15
  101.7 10.0 %collective-permute-start.5 = (bf16[112,128]{1,0:T(8,128)(2,1)S(1)}, bf16[112,128]{1,0:T(8,128)(2,1)S(1)}, u32[]{:S(2)}, u32[]{:S(2)}) collective-permute-start(bf16[112,128]{1,0:T(8,128)(2,1)S(1)} %share_sum.1), channel_id=1, source_target_pairs={{0,64},{1,65},{2,66},{3,67},{4,68},{5,69},{6,70},{7,71},{8,72},{9,... | collective-permute-start | bytes 86024 | tf_op jit(solution)/shard_map/ppermute | solution.py:332
  103.7 16.3 %collective-permute-start.6 = (bf16[128,640]{1,0:T(8,128)(2,1)S(1)}, bf16[128,640]{1,0:T(8,128)(2,1)S(1)}, u32[]{:S(2)}, u32[]{:S(2)}) collective-permute-start(bf16[128,640]{1,0:T(8,128)(2,1)S(1)} %get-tuple-element.49), channel_id=1, source_target_pairs={{0,256},{1,257},{2,258},{3,259},{4,260},{5,261},{6,262},{7,263},{8... | collective-permute-start | bytes 491528 | tf_op jit(solution)/shard_map/ppermute | solution.py:332
  111.7 14.5 %collective-permute-start.7 = (bf16[112,128]{1,0:T(8,128)(2,1)S(1)}, bf16[112,128]{1,0:T(8,128)(2,1)S(1)}, u32[]{:S(2)}, u32[]{:S(2)}) collective-permute-start(bf16[112,128]{1,0:T(8,128)(2,1)S(1)} %add_convert_fusion.total_ref), channel_id=1, source_target_pairs={{0,128},{1,129},{2,130},{3,131},{4,132},{5,133},{6,134},{7,135},{8... | collective-permute-start | bytes 86024 | tf_op jit(solution)/shard_map/ppermute | solution.py:332
  127.0 16.6 %all-to-all-start.2 = ((bf16[8,112,128]{2,1,0:T(8,128)(2,1)}), bf16[8,112,128]{2,1,0:T(8,128)(2,1)S(1)}, u32[]{:S(2)}, u32[]{:S(2)}) async-start(bf16[8,112,128]{2,1,0:T(8,128)(2,1)} %mean_for_all.1), calls=%async_computation.2 | async-start | bytes 458752 | tf_op jit(solution)/shard_map/all_to_all | solution.py:388
  131.4 2.9 %copy-start = (bf16[640,5120]{1,0:T(8,128)(2,1)S(1)}, bf16[640,5120]{1,0:T(8,128)(2,1)}, u32[]{:S(2)}) copy-start(bf16[640,5120]{1,0:T(8,128)(2,1)} %all-gather.2.cloned.1.call-done.w_ref) | copy-start | bytes 19660804
  134.3 2.8 %copy-start.11 = (f32[5,256,128]{2,1,0:T(8,128)S(1)}, f32[5,256,128]{2,1,0:T(8,128)}, u32[]{:S(2)}) copy-start(f32[5,256,128]{2,1,0:T(8,128)} %copy-done.10) | copy-start | bytes 1966084
  134.3 5.8 %copy-start.1 = (bf16[640,5120]{1,0:T(8,128)(2,1)S(1)}, bf16[640,5120]{1,0:T(8,128)(2,1)}, u32[]{:S(2)}) copy-start(bf16[640,5120]{1,0:T(8,128)(2,1)} %all-gather.2.cloned.1.call-done.w_ref) | copy-start | bytes 19660804
Sparse Core Ops, SparseCore 0:
  16.5 94.0 all-gather.1

commit v3 on v2

v3 whole, which is shorter than its diff:
```python
import functools
import math

import jax
import jax.numpy as jnp
from jax import lax
from jax.experimental import pallas as pl
from jax.experimental.pallas import tpu as pltpu
from jax.sharding import PartitionSpec as P

HD = 128
HQ = 5
ALIGNED_ROWS = 128
SLOT_NUMBER = 2
QW = HQ * HD
QKV = (HQ + 2) * HD
D = 2560
SCALE = 1.0 / math.sqrt(HD)
MASKED = -1e30
ABSENT = 1024.0
COSTS = {
    name: (flops * 10**9, 0)
    for name, flops in (("move_step_1", 4), ("move_step_2", 14), ("move_step_3", 20), ("move_step_4", 16), ("outputs", 20))
}
N_DP = 32
N_FSDP = 16
VMEM = 20 * 1024 * 1024
VMEM_FROM_HBM = 58 * 1024 * 1024
FROM_HBM = ("outputs", "side_by_side", "next_attention", "move_step_1", "move_step_2", "move_step_3", "move_step_4")

NN = (((1,), (0,)), ((), ()))
NT = (((1,), (1,)), ((), ()))
TN = (((0,), (0,)), ((), ()))


def dot(a, b, dims):
    return lax.dot_general(a, b, dims, preferred_element_type=jnp.float32)


def stacked_heads(x_ref, rows):
    return jnp.concatenate([x_ref[rows, h * HD : (h + 1) * HD] for h in range(HQ)], axis=0)


def block_probs(x_ref, rows, allowed):
    s = dot(stacked_heads(x_ref, rows), x_ref[rows, QW : QW + HD], NT) * SCALE
    s = jnp.where(jnp.concatenate([allowed] * HQ, axis=0), s, MASKED)
    e = jnp.exp(s - jnp.max(s, axis=-1, keepdims=True))
    return e * (1.0 / jnp.sum(e, axis=-1, keepdims=True))


def allowed_pairs(seg_ref, b):
    key_seg = jnp.broadcast_to(seg_ref[b : b + 1, :].astype(jnp.float32), (ALIGNED_ROWS, ALIGNED_ROWS))
    query_pos = lax.broadcasted_iota(jnp.int32, key_seg.shape, 0)
    key_pos = lax.broadcasted_iota(jnp.int32, key_seg.shape, 1)
    return (query_pos >= key_pos) & (key_seg == key_seg.T)


def call(kernel, out_shape, scratch=(), cost=(10**8, 10**6), name=None, **specs):
    flops, moved = COSTS.get(name, cost)
    return pl.pallas_call(
        kernel,
        out_shape=out_shape,
        scratch_shapes=list(scratch),
        compiler_params=pltpu.CompilerParams(vmem_limit_bytes=VMEM_FROM_HBM if name in FROM_HBM else VMEM),
        cost_estimate=pl.CostEstimate(flops=flops, bytes_accessed=moved, transcendentals=0),
        name=name,
        **specs,
    )


def bf16(*shape):
    return jax.ShapeDtypeStruct(shape, jnp.bfloat16)


SMEM = pl.BlockSpec(memory_space=pltpu.SMEM)
WHOLE = pl.BlockSpec(memory_space=pltpu.VMEM)
ANY = pl.BlockSpec(memory_space=pl.ANY)


def attend(x_ref, seg_ref, out_ref, prob_ref=None):
    for b in range(2):
        rows = slice(b * ALIGNED_ROWS, (b + 1) * ALIGNED_ROWS)
        p = block_probs(x_ref, rows, allowed_pairs(seg_ref, b))
        if prob_ref is not None:
            prob_ref[b] = p
        out = dot(p.astype(jnp.bfloat16), x_ref[rows, QW + HD :], NN).astype(jnp.bfloat16)
        for h in range(HQ):
            out_ref[rows, h * HD : (h + 1) * HD] = out[h * ALIGNED_ROWS : (h + 1) * ALIGNED_ROWS]


def with_arrived(live, count, slots_ref, arrived_ref, slots_out):
    top = live - count
    present = (jnp.max(arrived_ref[0:16, 0:HD].astype(jnp.float32)) < ABSENT / 2).astype(jnp.int32)
    place = jnp.where(present == 1, top, -1)
    arrived = arrived_ref[...]
    for s in range(SLOT_NUMBER):
        rows = slice(s * ALIGNED_ROWS, (s + 1) * ALIGNED_ROWS)
        slots_out[rows, :] = jnp.where(place == s, arrived, slots_ref[rows, :])
    return top + present


def leaving_block(live, count, slots_ref):
    first, second = slots_ref[:ALIGNED_ROWS, :], slots_ref[ALIGNED_ROWS:, :]
    block = jnp.where(live - count >= 1, second, first)
    return jnp.where(count > 0, block, jnp.full_like(block, ABSENT))


def next_kernel(live_ref, plan_ref, x_ref, seg_ref, out_ref, block_ref):
    attend(x_ref, seg_ref, out_ref)
    block_ref[...] = leaving_block(live_ref[0, 0], plan_ref[0, 0, 0], out_ref)


def next_attention(live, plan, qkv, segments):
    rows = qkv.shape[0]
    return call(
        next_kernel,
        (bf16(rows, QW), bf16(ALIGNED_ROWS, QW)),
        name="next_attention",
        in_specs=[SMEM, SMEM, WHOLE, WHOLE],
    )(live, plan, qkv, segments)


def move_kernel(level, live_ref, plan_ref, slots_ref, arrived_ref, slots_out, live_out, block_ref):
    live = with_arrived(live_ref[0, 0], plan_ref[0, 0, level - 1], slots_ref, arrived_ref, slots_out)
    live_out[0, 0] = live
    block_ref[...] = leaving_block(live, plan_ref[0, 0, level], slots_out)


def move_step(level, plan, live, slots, block):
    arrived = swap(block, 1 << (level - 1))
    return call(
        functools.partial(move_kernel, level),
        (bf16(*slots.shape), jax.ShapeDtypeStruct(live.shape, jnp.int32), bf16(*block.shape)),
        name=f"move_step_{level}",
        in_specs=[SMEM, SMEM, WHOLE, WHOLE],
        out_specs=(WHOLE, SMEM, WHOLE),
    )(live, plan, slots, arrived)


def current_kernel(x_ref, seg_ref, order_ref, keep_ref, send_ref, prob_ref, attn_ref):
    attend(x_ref, seg_ref, attn_ref, prob_ref)
    ordered = dot(attn_ref[...], order_ref[...], NN).astype(jnp.bfloat16)
    keep_ref[...] = ordered[:, : QW // 2]
    send_ref[...] = ordered[:, QW // 2 :]


def current_attention(qkv, segments, order):
    rows = qkv.shape[0]
    return call(
        current_kernel,
        (bf16(rows, QW // 2), bf16(rows, QW // 2), jax.ShapeDtypeStruct((2, QW, HD), jnp.float32)),
        [pltpu.VMEM((rows, QW), jnp.bfloat16)],
        name="current_attention",
    )(qkv, segments, order)


POLICY_PARTS = (0, 256), (256, 512), (512, QW)
FROZEN_PARTS = (0, D // 2), (D // 2, D)


def outputs_kernel(
    level, live_ref, plan_ref, x_hbm, prob_hbm, g_hbm, slots_hbm, arrived_hbm, w_hbm, grad_hbm, frozen_hbm,
    x_ref, prob_ref, g_ref, slots_ref, arrived_ref, w_ref, ga_ref, grad_ref, moved_ref, frozen_ref, sems, out_sems,
):
    g_copy, x_copy, prob_copy, slots_copy, arrived_copy = (
        pltpu.make_async_copy(source, target, sems.at[i])
        for i, (source, target) in enumerate(
            ((g_hbm, g_ref), (x_hbm, x_ref), (prob_hbm, prob_ref), (slots_hbm, slots_ref), (arrived_hbm, arrived_ref))
        )
    )
    policy_copies = [
        pltpu.make_async_copy(w_hbm.at[pl.ds(i, j - i), pl.ds(0, D)], w_ref.at[pl.ds(i, j - i), pl.ds(0, D)], sems.at[5 + n])
        for n, (i, j) in enumerate(POLICY_PARTS)
    ]
    frozen_copies = [
        pltpu.make_async_copy(w_hbm.at[:, pl.ds(D + i, j - i)], w_ref.at[:, pl.ds(D + i, j - i)], sems.at[8 + n])
        for n, (i, j) in enumerate(FROZEN_PARTS)
    ]
    for copy in (g_copy, *policy_copies, x_copy, prob_copy, slots_copy, arrived_copy, *frozen_copies):
        copy.start()
    g_copy.wait()
    for copy, (i, j) in zip(policy_copies, POLICY_PARTS):
        copy.wait()
        ga_ref[:, i:j] = dot(g_ref[...], w_ref[i:j, :D], NT).astype(jnp.bfloat16)
    x_copy.wait()
    prob_copy.wait()
    for b in range(2):
        rows = slice(b * ALIGNED_ROWS, (b + 1) * ALIGNED_ROWS)
        q, ga = stacked_heads(x_ref, rows), stacked_heads(ga_ref, rows)
        k, v = x_ref[rows, QW : QW + HD], x_ref[rows, QW + HD :]
        p = prob_ref[b]
        dp = dot(ga, v, NT)
        ds = p * (dp - jnp.sum(p * dp, axis=-1, keepdims=True))
        high = ds.astype(jnp.bfloat16)
        low = (ds - high.astype(jnp.float32)).astype(jnp.bfloat16)
        dq = ((dot(high, k, NN) + dot(low, k, NN)) * SCALE).astype(jnp.bfloat16)
        for h in range(HQ):
            grad_ref[rows, h * HD : (h + 1) * HD] = dq[h * ALIGNED_ROWS : (h + 1) * ALIGNED_ROWS]
        grad_ref[rows, QW : QW + HD] = ((dot(high, q, TN) + dot(low, q, TN)) * SCALE).astype(jnp.bfloat16)
        grad_ref[rows, QW + HD :] = dot(p.astype(jnp.bfloat16), ga, TN).astype(jnp.bfloat16)
    grad_copy = pltpu.make_async_copy(grad_ref, grad_hbm, out_sems.at[0])
    grad_copy.start()
    slots_copy.wait()
    arrived_copy.wait()
    live = with_arrived(live_ref[0, 0], plan_ref[0, 0, level], slots_ref, arrived_ref, moved_ref)
    for s in range(SLOT_NUMBER):
        rows = slice(s * ALIGNED_ROWS, (s + 1) * ALIGNED_ROWS)
        block = moved_ref[rows, :]
        moved_ref[rows, :] = jnp.where(live > s, block, jnp.zeros_like(block))
    out_copies = []
    for n, (copy, (i, j)) in enumerate(zip(frozen_copies, FROZEN_PARTS)):
        copy.wait()
        frozen_ref[:, i:j] = dot(moved_ref[...], w_ref[:, D + i : D + j], NN).astype(jnp.bfloat16)
        out_copies.append(
            pltpu.make_async_copy(frozen_ref.at[:, pl.ds(i, j - i)], frozen_hbm.at[:, pl.ds(i, j - i)], out_sems.at[1 + n])
        )
        out_copies[-1].start()
    for copy in (grad_copy, *out_copies):
        copy.wait()


def outputs(level, live, plan, qkv, probs, grad_output, slots, arrived, weights):
    rows = qkv.shape[0]
    inputs = (qkv, probs, grad_output, slots, arrived, weights)
    return call(
        functools.partial(outputs_kernel, level),
        (bf16(*qkv.shape), bf16(rows, D)),
        [pltpu.VMEM(a.shape, a.dtype) for a in inputs]
        + [pltpu.VMEM((rows, QW), jnp.bfloat16), pltpu.VMEM(qkv.shape, jnp.bfloat16)]
        + [pltpu.VMEM((rows, QW), jnp.bfloat16), pltpu.VMEM((rows, D), jnp.bfloat16)]
        + [pltpu.SemaphoreType.DMA((10,)), pltpu.SemaphoreType.DMA((3,))],
        (3 * 10**9, 10**7),
        "outputs",
        in_specs=[SMEM, SMEM] + [ANY] * len(inputs),
        out_specs=(ANY, ANY),
    )(live, plan, *inputs)


def terms_kernel(a_ref, g_ref, out_ref):
    for i in range(0, D, 512):
        columns = slice(i, i + 512)
        out_ref[:, columns] = dot(a_ref[...], g_ref[:, columns], TN).astype(jnp.bfloat16)


def terms_to_send(attention, grad_output):
    return call(terms_kernel, bf16(QW // 2, D), name="terms_to_send")(attention, grad_output)


def terms_with_kernel(a_ref, g_ref, other_ref, out_ref):
    rows = QW // N_FSDP
    for i in range(0, D, 512):
        columns = slice(i, i + 512)
        total = dot(a_ref[...], g_ref[:, columns], TN) + other_ref[:, columns].astype(jnp.float32)
        for j in range(out_ref.shape[0]):
            out_ref[j, :, columns] = total[j * rows : (j + 1) * rows].astype(jnp.bfloat16)


def terms_with_other_core(attention, grad_output, other):
    return call(terms_with_kernel, bf16(N_FSDP // 2, QW // N_FSDP, D), name="terms_with_other_core")(
        attention, grad_output, other
    )


PEERS = 8
TILES = [(i, j) for i in range(0, QW // N_FSDP, 8) for j in range(0, D, HD)]
SHARE = -(-len(TILES) // PEERS)
SHARE_ROWS = -(-SHARE * 8 // 16) * 16


def group_sum_kernel(parts_ref, out_ref):
    shares = [[] for _ in range(PEERS)]
    for n, (i, j) in enumerate(TILES):
        if i == 0:
            columns = sum(parts_ref[p, :, j : j + HD].astype(jnp.float32) for p in range(parts_ref.shape[0]))
            for r in range(0, columns.shape[0], 8):
                at = TILES.index((r, j))
                shares[at // SHARE].append((at % SHARE, columns[r : r + 8]))
    for k, share in enumerate(shares):
        tiles = [tile for _, tile in sorted(share, key=lambda pair: pair[0])]
        tiles += [jnp.zeros_like(tiles[0])] * (SHARE_ROWS // 8 - len(tiles))
        out_ref[k] = jnp.concatenate(tiles, axis=0).astype(jnp.bfloat16)


def group_sum(parts):
    return call(group_sum_kernel, bf16(PEERS, SHARE_ROWS, HD), name="group_sum")(parts)


def spread_sum_kernel(scale, parts_ref, out_ref):
    total = sum(parts_ref[p].astype(jnp.float32) for p in range(parts_ref.shape[0]))
    total = (total * scale).astype(jnp.bfloat16)
    for p in range(out_ref.shape[0]):
        out_ref[p] = total


def spread_sum(parts, peers, scale, name):
    return call(functools.partial(spread_sum_kernel, scale), bf16(peers, SHARE_ROWS, HD), name=name)(parts)


def join_kernel(shares_ref, out_ref):
    shares = [shares_ref[k].astype(jnp.float32) for k in range(PEERS)]
    for j in range(0, D, HD):
        tiles = []
        for i in range(0, QW // N_FSDP, 8):
            n = TILES.index((i, j))
            row = n % SHARE * 8
            tiles.append(shares[n // SHARE][row : row + 8])
        out_ref[:, j : j + HD] = jnp.concatenate(tiles, axis=0).astype(jnp.bfloat16)


def join(shares):
    return call(join_kernel, bf16(QW // N_FSDP, D), name="join")(shares)


def side_by_side_kernel(left, right, out_ref):
    out_ref[:, :D] = left[...]
    out_ref[:, D:] = right[...]


def side_by_side(left, right):
    return call(side_by_side_kernel, bf16(left.shape[0], 2 * D), name="side_by_side")(left, right)


def fsdp_pairs(flip, x_step):
    def target(j):
        j ^= flip
        return (j & 9) | (((j >> 1 & 3) + x_step) % 4 << 1)

    return [(j, target(j)) for j in range(N_FSDP)]


def all_pairs(dp_flip, fsdp_flip):
    return [
        (d * N_FSDP + j, (d ^ dp_flip) * N_FSDP + (j ^ fsdp_flip)) for d in range(N_DP) for j in range(N_FSDP)
    ]


def swap(a, dp_flip, fsdp_flip=0):
    return lax.ppermute(a, ("dp", "fsdp"), all_pairs(dp_flip, fsdp_flip))


def add(*terms):
    return sum(t.astype(jnp.float32) for t in terms).astype(jnp.bfloat16)


def after(a, *others):
    return lax.optimization_barrier((a, *others))[0]


def sum_order(me):
    rows = QW // N_FSDP
    natural = jnp.arange(QW, dtype=jnp.int32)
    j, k = natural // rows, natural % rows
    place = ((j ^ me) & 1) * (N_FSDP // 2) + (j >> 1)
    return (natural[None, :] == (place * rows + k)[:, None]).astype(jnp.bfloat16)


def body(
    policy_out,
    frozen_out,
    qkv_current,
    segment_current,
    grad_output,
    query_key_value_next,
    document_next,
    block_counts,
    move_plan,
):
    me = lax.axis_index("fsdp")
    group = lax.axis_index("dp")
    same_core = [[j for j in range(N_FSDP) if j & 1 == core] for core in range(2)]
    near = [[y * 16 + 4 * q + z for y in range(2) for z in range(4)] for q in range(4)]
    far = [[y * 16 + 4 * q + z for q in range(4)] for y in range(2) for z in range(4)]

    own = side_by_side(policy_out, frozen_out)
    weights = lax.all_gather(own, "fsdp", axis=0, tiled=True)
    live, plan = block_counts, move_plan
    slots, block = next_attention(
        live, plan, after(query_key_value_next, own), document_next.reshape(SLOT_NUMBER, ALIGNED_ROWS)
    )
    keep_half, send_half, probs = current_attention(
        after(qkv_current, slots), segment_current.reshape(2, ALIGNED_ROWS), sum_order(me)
    )
    slots, live, block = move_step(1, plan, live, slots, block)
    other = lax.ppermute(terms_to_send(after(send_half, live), grad_output), "fsdp", fsdp_pairs(1, 0))
    parts = terms_with_other_core(keep_half, grad_output, other)
    parts = lax.all_to_all(parts, "fsdp", 0, 0, axis_index_groups=same_core)
    slots, live, block = move_step(2, plan, live, slots, block)
    shares = group_sum(after(parts, live))
    shares = lax.all_to_all(shares, "dp", 0, 0, axis_index_groups=near)
    slots, live, block = move_step(3, plan, live, slots, block)
    shares = spread_sum(after(shares, live), len(far[0]), 1.0, "near_sum")
    shares = lax.all_to_all(shares, "dp", 0, 0, axis_index_groups=far)
    shares = spread_sum(shares, PEERS, 1.0 / (N_DP * N_FSDP), "mean")
    shares = lax.all_to_all(shares, "dp", 0, 0, axis_index_groups=near)
    slots, live, block = move_step(4, plan, live, slots, block)
    block = swap(block, 16)
    qkv_gradient, frozen_layer_output = outputs(
        4, live, plan, qkv_current, probs, grad_output, slots, block, weights
    )
    weight_grad = join(after(shares, qkv_gradient))
    return (qkv_gradient, weight_grad, frozen_layer_output)


def solution(mesh):
    return jax.shard_map(
        body,
        mesh=mesh,
        in_specs=(
            P("fsdp", None),
            P("fsdp", None),
            P(("dp", "fsdp"), None),
            P(("dp", "fsdp")),
            P(("dp", "fsdp"), None),
            P(("dp", "fsdp"), None),
            P(("dp", "fsdp")),
            P("dp", "fsdp"),
            P("dp", "fsdp", None),
        ),
        out_specs=(P(("dp", "fsdp"), None), P("fsdp", None), P(("dp", "fsdp"), None)),
        check_vma=False,
    )
```

time: 154 us -> 137 us (0.89)
  local copies, waits for them, and re-layouts: 13.2 us -> 3.32 us
  starting transfers between devices: 63.7 us -> 56.8 us
  Pallas kernels: 24.1 us -> 31 us
  waiting for transfers between devices: 34.3 us -> 28.7 us
    ppermute x7 -> x5, waiting for transfers between devices: 28.2 us -> 2.7 us  [swap(): return lax.ppermute(a, ('dp', 'fsdp'), all_pairs(dp_flip, fsdp_flip))]
    all_to_all x1 -> x2, waiting for transfers between devices: 4.31 us -> 26 us  [the longest x1 13.9 us: body(): shares = lax.all_to_all(shares, 'dp', 0, 0, axis_index_groups=far)]
    ppermute x7 -> x5, starting transfers between devices: 43.9 us -> 33.1 us  [swap(): return lax.ppermute(a, ('dp', 'fsdp'), all_pairs(dp_flip, fsdp_flip))]
    unnamed x32 -> x20, local copies, waits for them, and re-layouts: 13.2 us -> 3.32 us
    pallas_call x4, Pallas kernels: 3.57 us -> 9.83 us  [move_step(): call(functools.partial(move_kernel, level), (bf16(*slots.shape), jax.Shap...]
    all_to_all x1 -> x2, starting transfers between devices: 7.26 us -> 11.3 us  [the longest x1 7.26 us: body(): parts = lax.all_to_all(parts, 'fsdp', 0, 0, axis_index_groups=same_core)]
    pallas_call x1, Pallas kernels: 3.51 us -> 1.48 us  [current_attention(): call(current_kernel, (bf16(rows, QW // 2), bf16(rows, QW // 2), jax.Shape...]
    pallas_call x6 -> x4, Pallas kernels: 10.8 us -> 12.8 us  [the longest x1 9.52 us: outputs(): call(functools.partial(outputs_kernel, level), (bf16(*qkv.shape), bf16(ro...]
  transfers between devices with their start and end apart: 12 -> 11, of which waited for: 7 -> 4; matrix products, arithmetic and copies ran while one was open for 0% -> 0% of each run, Pallas kernels for 13% -> 21%
where the time goes in v3:
time: 137 us; the launch traced here: 135 us
  starting transfers between devices  56.8 us (41%)
  Pallas kernels  31 us (23%)
  waiting for transfers between devices  28.7 us (21%)
  between operations  14.9 us (11%)
  local copies, waits for them, and re-layouts  3.32 us (2%)
    ppermute x5, starting transfers between devices, swap(): return lax.ppermute(a, ('dp', 'fsdp'), all_pairs(dp_flip, fsdp_flip))  33.1 us
    all_to_all x1, waiting for transfers between devices, body(): shares = lax.all_to_all(shares, 'dp', 0, 0, axis_index_groups=far)  13.9 us
    all_to_all x1, waiting for transfers between devices, body(): parts = lax.all_to_all(parts, 'fsdp', 0, 0, axis_index_groups=same_core)  12.1 us
    all_to_all x2, starting transfers between devices, body(): shares = lax.all_to_all(shares, 'dp', 0, 0, axis_index_groups=near)  10.4 us
    pallas_call x4, Pallas kernels, move_step(): call(functools.partial(move_kernel, level), (bf16(*slots.shape), jax.Shap...  9.83 us
    pallas_call x1, Pallas kernels, outputs(): call(functools.partial(outputs_kernel, level), (bf16(*qkv.shape), bf16(ro...  9.52 us
    all_to_all x1, starting transfers between devices, body(): parts = lax.all_to_all(parts, 'fsdp', 0, 0, axis_index_groups=same_core)  7.26 us
    all_to_all x1, starting transfers between devices, body(): shares = lax.all_to_all(shares, 'dp', 0, 0, axis_index_groups=far)  4.02 us
  transfers between devices with their start and end apart: 11, of which 4 were waited for; matrix products, arithmetic and copies ran while one was open for 0% of the time, Pallas kernels for 21%

profile of v3, /device:TPU:24, one launch (start us, length us, event | category | flops | bytes accessed | tf_op | source)
XLA Modules:
  0.0 134.9 jit_solution(18250765860002809469)
XLA Ops:
  7.2 0.0 copy-start.1
  7.2 0.0 all-gather.2.cloned.1.call-start
  7.2 1.8 %side_by_side.1 = bf16[40,5120]{1,0:T(8,128)(2,1)} custom-call(bf16[40,2560]{1,0:T(8,128)(2,1)} %left.1, bf16[40,2560]{1,0:T(8,128)(2,1)} %right.1), custom_call_target="tpu_custom_call" | custom-call | flops 100000000 | bytes 1000000 | tf_op jit(solution)/shard_map/side_by_side/pallas_call | solution.py:320
  9.1 0.0 all-gather.2.cloned.1.call-update
  9.8 2.8 %next_attention.1 = (bf16[256,640]{1,0:T(8,128)(2,1)}, bf16[128,640]{1,0:T(8,128)(2,1)}) custom-call(s32[1,1]{1,0:T(1,128)S(6)} %copy.12.live_ref, s32[1,1,5]{2,1,0:T(1,128)} %plan_ref.11, bf16[256,896]{1,0:T(8,128)(2,1)} %x_ref, s32[2,128]{1,0:T(2,128)} %bitcast.3), custom_call_target="tpu_custom_call" | custom-call | flops 100000000 | bytes 1000000 | tf_op jit(solution)/shard_map/next_attention/pallas_call | solution.py:115
  12.6 3.8 %collective-permute-start = (bf16[128,640]{1,0:T(8,128)(2,1)}, bf16[128,640]{1,0:T(8,128)(2,1)S(1)}, u32[]{:S(2)}, u32[]{:S(2)}) collective-permute-start(bf16[128,640]{1,0:T(8,128)(2,1)} %get-tuple-element.30), channel_id=1, source_target_pairs={{0,16},{1,17},{2,18},{3,19},{4,20},{5,21},{6,22},{7,23},{8,24},{9,... | collective-permute-start | bytes 491528 | tf_op jit(solution)/shard_map/ppermute | solution.py:338
  16.4 0.2 fusion.order_ref
  16.6 0.0 copy-done.1
  16.6 0.0 copy-done.2
  16.7 1.5 %current_attention.1 = (bf16[256,320]{1,0:T(8,128)(2,1)S(1)}, bf16[256,320]{1,0:T(8,128)(2,1)S(1)}, f32[2,640,128]{2,1,0:T(8,128)S(1)}) custom-call(bf16[256,896]{1,0:T(8,128)(2,1)S(1)} %copy-done.1, s32[2,128]{1,0:T(2,128)S(1)} %bitcast.2, bf16[640,640]{1,0:T(8,128)(2,1)S(1)} %fusion.order_ref), custom_call_target="tpu_custom_call" | custom-call | flops 100000000 | bytes 1000000 | tf_op jit(solution)/shard_map/current_attention/pallas_call | solution.py:149
  18.1 0.0 copy-start
  18.2 2.6 %collective-permute-done.arrived_ref = bf16[128,640]{1,0:T(8,128)(2,1)S(1)} collective-permute-done((bf16[128,640]{1,0:T(8,128)(2,1)}, bf16[128,640]{1,0:T(8,128)(2,1)S(1)}, u32[]{:S(2)}, u32[]{:S(2)}) %collective-permute-start) | collective-permute-done | bytes 163872 | tf_op jit(solution)/shard_map/ppermute | solution.py:338
  20.8 0.7 copy-done.6
  21.5 2.0 %move_step_1.1 = (bf16[256,640]{1,0:T(8,128)(2,1)}, s32[1,1]{1,0:T(1,128)}, bf16[128,640]{1,0:T(8,128)(2,1)}) custom-call(s32[1,1]{1,0:T(1,128)S(6)} %copy.12.live_ref, s32[1,1,5]{2,1,0:T(1,128)} %plan_ref.11, bf16[256,640]{1,0:T(8,128)(2,1)} %get-tuple-element.29.slots_ref, bf16[128,640]{1,0:T(8,128)(2,1)} %copy-done.6), custom_call_target="tpu_custom_call" | custom-call | flops 4000000000 | tf_op jit(solution)/shard_map/move_step_1/pallas_call | solution.py:131
  23.5 0.6 terms_to_send.1
  24.1 1.9 %collective-permute-start.5 = (bf16[320,2560]{1,0:T(8,128)(2,1)S(1)}, bf16[320,2560]{1,0:T(8,128)(2,1)S(1)}, u32[]{:S(2)}, u32[]{:S(2)}) collective-permute-start(bf16[320,2560]{1,0:T(8,128)(2,1)S(1)} %terms_to_send.1), channel_id=1, source_target_pairs={{0,1},{1,0},{2,3},{3,2},{4,5},{5,4},{6,7},{7,6},{8,9},{9,8},{10,11... | collective-permute-start | bytes 4915208 | tf_op jit(solution)/shard_map/ppermute | solution.py:384
  26.0 0.0 copy-done.5
  26.0 5.2 %collective-permute-start.1 = (bf16[128,640]{1,0:T(8,128)(2,1)S(1)}, bf16[128,640]{1,0:T(8,128)(2,1)S(1)}, u32[]{:S(2)}, u32[]{:S(2)}) collective-permute-start(bf16[128,640]{1,0:T(8,128)(2,1)S(1)} %copy-done.5), channel_id=1, source_target_pairs={{0,32},{1,33},{2,34},{3,35},{4,36},{5,37},{6,38},{7,39},{8,40},{9,... | collective-permute-start | bytes 491528 | tf_op jit(solution)/shard_map/ppermute | solution.py:338
  31.2 0.0 collective-permute-done.5.other_ref
  31.2 1.9 %terms_with_other_core.1 = bf16[8,40,2560]{2,1,0:T(8,128)(2,1)} custom-call(bf16[256,320]{1,0:T(8,128)(2,1)S(1)} %get-tuple-element.46.a_ref, bf16[256,2560]{1,0:T(8,128)(2,1)S(1)} %copy-done, bf16[320,2560]{1,0:T(8,128)(2,1)S(1)} %collective-permute-done.5.other_ref), custom_call_target="tpu_custom_call" | custom-call | flops 100000000 | bytes 1000000 | tf_op jit(solution)/shard_map/terms_with_other_core/pallas_call | solution.py:259
  33.1 7.3 %all-to-all-start = ((bf16[8,40,2560]{2,1,0:T(8,128)(2,1)}), bf16[8,40,2560]{2,1,0:T(8,128)(2,1)S(1)}, u32[]{:S(2)}, u32[]{:S(2)}) async-start(bf16[8,40,2560]{2,1,0:T(8,128)(2,1)} %terms_with_other_core.1), calls=%async_computation | async-start | bytes 3276800 | tf_op jit(solution)/shard_map/all_to_all | solution.py:386
  40.4 0.0 collective-permute-done.1.arrived_ref
  40.4 0.7 copy-done.7
  41.0 2.7 %move_step_2.1 = (bf16[256,640]{1,0:T(8,128)(2,1)}, s32[1,1]{1,0:T(1,128)}, bf16[128,640]{1,0:T(8,128)(2,1)}) custom-call(s32[1,1]{1,0:T(1,128)} %get-tuple-element.31.live_ref, s32[1,1,5]{2,1,0:T(1,128)} %plan_ref.11, bf16[256,640]{1,0:T(8,128)(2,1)} %get-tuple-element.32.slots_ref, bf16[128,640]{1,0:T(8,128)(2,1)} %copy-done.7), custom_call_target="tpu_custom_call" | custom-call | flops 14000000000 | tf_op jit(solution)/shard_map/move_step_2/pallas_call | solution.py:131
  43.7 9.1 %collective-permute-start.2 = (bf16[128,640]{1,0:T(8,128)(2,1)}, bf16[128,640]{1,0:T(8,128)(2,1)S(1)}, u32[]{:S(2)}, u32[]{:S(2)}) collective-permute-start(bf16[128,640]{1,0:T(8,128)(2,1)} %get-tuple-element.36), channel_id=1, source_target_pairs={{0,64},{1,65},{2,66},{3,67},{4,68},{5,69},{6,70},{7,71},{8,72},{9,... | collective-permute-start | bytes 491528 | tf_op jit(solution)/shard_map/ppermute | solution.py:338
  52.8 12.1 %all-to-all-done.parts_ref = bf16[8,40,2560]{2,1,0:T(8,128)(2,1)S(1)} async-done(((bf16[8,40,2560]{2,1,0:T(8,128)(2,1)}), bf16[8,40,2560]{2,1,0:T(8,128)(2,1)S(1)}, u32[]{:S(2)}, u32[]{:S(2)}) %all-to-all-start) | async-done | bytes 1638432 | tf_op jit(solution)/shard_map/all_to_all | solution.py:386
  64.9 0.9 group_sum.1
  65.8 5.6 %all-to-all-start.1 = ((bf16[8,112,128]{2,1,0:T(8,128)(2,1)}), bf16[8,112,128]{2,1,0:T(8,128)(2,1)S(1)}, u32[]{:S(2)}, u32[]{:S(2)}) async-start(bf16[8,112,128]{2,1,0:T(8,128)(2,1)} %group_sum.1), calls=%async_computation.1 | async-start | bytes 458752 | tf_op jit(solution)/shard_map/all_to_all | solution.py:389
  71.4 0.0 collective-permute-done.2.arrived_ref
  71.4 0.7 copy-done.8
  72.1 2.6 %move_step_3.1 = (bf16[256,640]{1,0:T(8,128)(2,1)}, s32[1,1]{1,0:T(1,128)}, bf16[128,640]{1,0:T(8,128)(2,1)}) custom-call(s32[1,1]{1,0:T(1,128)} %get-tuple-element.34.live_ref, s32[1,1,5]{2,1,0:T(1,128)} %plan_ref.11, bf16[256,640]{1,0:T(8,128)(2,1)} %get-tuple-element.35.slots_ref, bf16[128,640]{1,0:T(8,128)(2,1)} %copy-done.8), custom_call_target="tpu_custom_call" | custom-call | flops 20000000000 | tf_op jit(solution)/shard_map/move_step_3/pallas_call | solution.py:131
  74.6 11.7 %collective-permute-start.3 = (bf16[128,640]{1,0:T(8,128)(2,1)}, bf16[128,640]{1,0:T(8,128)(2,1)S(1)}, u32[]{:S(2)}, u32[]{:S(2)}) collective-permute-start(bf16[128,640]{1,0:T(8,128)(2,1)} %get-tuple-element.39), channel_id=1, source_target_pairs={{0,128},{1,129},{2,130},{3,131},{4,132},{5,133},{6,134},{7,135},{8... | collective-permute-start | bytes 491528 | tf_op jit(solution)/shard_map/ppermute | solution.py:338
  86.3 0.0 all-to-all-done.1.parts_ref
  86.4 0.7 near_sum.1
  87.0 4.0 %all-to-all-start.2 = ((bf16[4,112,128]{2,1,0:T(8,128)(2,1)}), bf16[4,112,128]{2,1,0:T(8,128)(2,1)S(1)}, u32[]{:S(2)}, u32[]{:S(2)}) async-start(bf16[4,112,128]{2,1,0:T(8,128)(2,1)} %near_sum.1), calls=%async_computation.2 | async-start | bytes 229376 | tf_op jit(solution)/shard_map/all_to_all | solution.py:392
  91.0 0.1 collective-permute-done.3.arrived_ref
  91.1 0.7 copy-done.9
  91.8 2.6 %move_step_4.1 = (bf16[256,640]{1,0:T(8,128)(2,1)}, s32[1,1]{1,0:T(1,128)}, bf16[128,640]{1,0:T(8,128)(2,1)}) custom-call(s32[1,1]{1,0:T(1,128)} %get-tuple-element.37.live_ref, s32[1,1,5]{2,1,0:T(1,128)} %plan_ref.11, bf16[256,640]{1,0:T(8,128)(2,1)} %get-tuple-element.38.slots_ref, bf16[128,640]{1,0:T(8,128)(2,1)} %copy-done.9), custom_call_target="tpu_custom_call" | custom-call | flops 16000000000 | tf_op jit(solution)/shard_map/move_step_4/pallas_call | solution.py:131
  94.4 3.3 %collective-permute-start.4 = (bf16[128,640]{1,0:T(8,128)(2,1)}, bf16[128,640]{1,0:T(8,128)(2,1)S(1)}, u32[]{:S(2)}, u32[]{:S(2)}) collective-permute-start(bf16[128,640]{1,0:T(8,128)(2,1)} %get-tuple-element.44), channel_id=1, source_target_pairs={{0,256},{1,257},{2,258},{3,259},{4,260},{5,261},{6,262},{7,263},{8... | collective-permute-start | bytes 491528 | tf_op jit(solution)/shard_map/ppermute | solution.py:338
  97.8 13.9 %all-to-all-done.2.parts_ref = bf16[4,112,128]{2,1,0:T(8,128)(2,1)S(1)} async-done(((bf16[4,112,128]{2,1,0:T(8,128)(2,1)}), bf16[4,112,128]{2,1,0:T(8,128)(2,1)S(1)}, u32[]{:S(2)}, u32[]{:S(2)}) %all-to-all-start.2) | async-done | bytes 114720 | tf_op jit(solution)/shard_map/all_to_all | solution.py:392
  111.7 0.7 mean.1
  112.4 4.8 %all-to-all-start.3 = ((bf16[8,112,128]{2,1,0:T(8,128)(2,1)}), bf16[8,112,128]{2,1,0:T(8,128)(2,1)S(1)}, u32[]{:S(2)}, u32[]{:S(2)}) async-start(bf16[8,112,128]{2,1,0:T(8,128)(2,1)} %mean.1), calls=%async_computation.3 | async-start | bytes 458752 | tf_op jit(solution)/shard_map/all_to_all | solution.py:394
  117.2 0.0 collective-permute-done.4.arrived_hbm
  117.2 0.0 all-gather.2.cloned.1.call-done.w_hbm
  117.2 0.6 copy-done.4
  117.8 9.5 %outputs.1 = (bf16[256,896]{1,0:T(8,128)(2,1)}, bf16[256,2560]{1,0:T(8,128)(2,1)}) custom-call(s32[1,1]{1,0:T(1,128)} %get-tuple-element.40.live_ref, s32[1,1,5]{2,1,0:T(1,128)} %plan_ref.11, bf16[256,896]{1,0:T(8,128)(2,1)} %x_hbm.1, f32[2,640,128]{2,1,0:T(8,128)} %copy-done.3, bf16[256,2560]{1,0:T(8,128)(2,1)} %g_ref.3, ...), custom_call_target="tpu_custom_call" | custom-call | flops 20000000000 | tf_op jit(solution)/shard_map/outputs/pallas_call | solution.py:225
  127.4 0.0 all-to-all-done.3.shares_ref
  127.4 0.7 join.1
  (11 shorter events, 0.0 us)
Async XLA Ops:
  7.2 9.5 %copy-start.1 = (bf16[256,896]{1,0:T(8,128)(2,1)S(1)}, bf16[256,896]{1,0:T(8,128)(2,1)}, u32[]{:S(2)}) copy-start(bf16[256,896]{1,0:T(8,128)(2,1)} %x_hbm.1) | copy-start | bytes 1376260
  7.2 9.5 %copy-start.2 = (s32[256]{0:T(256)S(1)}, s32[256]{0:T(256)}, u32[]{:S(2)}) copy-start(s32[256]{0:T(256)} %param.12) | copy-start | bytes 3076
  7.2 110.0 %all-gather.2.cloned.1.call-start = ((), (), s32[]{:S(2)}) async-start(), calls=%async_computation.4 | async-start | bytes 6963200 | tf_op jit(solution)/shard_map/all_gather | solution.py:375
  12.6 8.2 %collective-permute-start = (bf16[128,640]{1,0:T(8,128)(2,1)}, bf16[128,640]{1,0:T(8,128)(2,1)S(1)}, u32[]{:S(2)}, u32[]{:S(2)}) collective-permute-start(bf16[128,640]{1,0:T(8,128)(2,1)} %get-tuple-element.30), channel_id=1, source_target_pairs={{0,16},{1,17},{2,18},{3,19},{4,20},{5,21},{6,22},{7,23},{8,24},{9,... | collective-permute-start | bytes 491528 | tf_op jit(solution)/shard_map/ppermute | solution.py:338
  18.1 5.3 %copy-start.3 = (f32[2,640,128]{2,1,0:T(8,128)}, f32[2,640,128]{2,1,0:T(8,128)S(1)}, u32[]{:S(2)}) copy-start(f32[2,640,128]{2,1,0:T(8,128)S(1)} %get-tuple-element.42.prob_hbm) | copy-start | bytes 1966084
  18.1 5.3 %copy-start = (bf16[256,2560]{1,0:T(8,128)(2,1)S(1)}, bf16[256,2560]{1,0:T(8,128)(2,1)}, u32[]{:S(2)}) copy-start(bf16[256,2560]{1,0:T(8,128)(2,1)} %g_ref.3) | copy-start | bytes 3932164
  20.8 0.7 copy-start.6
  23.5 2.6 %copy-start.5 = (bf16[128,640]{1,0:T(8,128)(2,1)S(1)}, bf16[128,640]{1,0:T(8,128)(2,1)}, u32[]{:S(2)}) copy-start(bf16[128,640]{1,0:T(8,128)(2,1)} %get-tuple-element.33) | copy-start | bytes 491524
  24.1 7.1 %collective-permute-start.5 = (bf16[320,2560]{1,0:T(8,128)(2,1)S(1)}, bf16[320,2560]{1,0:T(8,128)(2,1)S(1)}, u32[]{:S(2)}, u32[]{:S(2)}) collective-permute-start(bf16[320,2560]{1,0:T(8,128)(2,1)S(1)} %terms_to_send.1), channel_id=1, source_target_pairs={{0,1},{1,0},{2,3},{3,2},{4,5},{5,4},{6,7},{7,6},{8,9},{9,8},{10,11... | collective-permute-start | bytes 4915208 | tf_op jit(solution)/shard_map/ppermute | solution.py:384
  26.0 14.3 %collective-permute-start.1 = (bf16[128,640]{1,0:T(8,128)(2,1)S(1)}, bf16[128,640]{1,0:T(8,128)(2,1)S(1)}, u32[]{:S(2)}, u32[]{:S(2)}) collective-permute-start(bf16[128,640]{1,0:T(8,128)(2,1)S(1)} %copy-done.5), channel_id=1, source_target_pairs={{0,32},{1,33},{2,34},{3,35},{4,36},{5,37},{6,38},{7,39},{8,40},{9,... | collective-permute-start | bytes 491528 | tf_op jit(solution)/shard_map/ppermute | solution.py:338
  33.1 31.8 %all-to-all-start = ((bf16[8,40,2560]{2,1,0:T(8,128)(2,1)}), bf16[8,40,2560]{2,1,0:T(8,128)(2,1)S(1)}, u32[]{:S(2)}, u32[]{:S(2)}) async-start(bf16[8,40,2560]{2,1,0:T(8,128)(2,1)} %terms_with_other_core.1), calls=%async_computation | async-start | bytes 3276800 | tf_op jit(solution)/shard_map/all_to_all | solution.py:386
  40.4 0.7 copy-start.7
  43.7 27.7 %collective-permute-start.2 = (bf16[128,640]{1,0:T(8,128)(2,1)}, bf16[128,640]{1,0:T(8,128)(2,1)S(1)}, u32[]{:S(2)}, u32[]{:S(2)}) collective-permute-start(bf16[128,640]{1,0:T(8,128)(2,1)} %get-tuple-element.36), channel_id=1, source_target_pairs={{0,64},{1,65},{2,66},{3,67},{4,68},{5,69},{6,70},{7,71},{8,72},{9,... | collective-permute-start | bytes 491528 | tf_op jit(solution)/shard_map/ppermute | solution.py:338
  65.8 20.6 %all-to-all-start.1 = ((bf16[8,112,128]{2,1,0:T(8,128)(2,1)}), bf16[8,112,128]{2,1,0:T(8,128)(2,1)S(1)}, u32[]{:S(2)}, u32[]{:S(2)}) async-start(bf16[8,112,128]{2,1,0:T(8,128)(2,1)} %group_sum.1), calls=%async_computation.1 | async-start | bytes 458752 | tf_op jit(solution)/shard_map/all_to_all | solution.py:389
  71.4 0.7 copy-start.8
  74.6 16.5 %collective-permute-start.3 = (bf16[128,640]{1,0:T(8,128)(2,1)}, bf16[128,640]{1,0:T(8,128)(2,1)S(1)}, u32[]{:S(2)}, u32[]{:S(2)}) collective-permute-start(bf16[128,640]{1,0:T(8,128)(2,1)} %get-tuple-element.39), channel_id=1, source_target_pairs={{0,128},{1,129},{2,130},{3,131},{4,132},{5,133},{6,134},{7,135},{8... | collective-permute-start | bytes 491528 | tf_op jit(solution)/shard_map/ppermute | solution.py:338
  87.0 24.6 %all-to-all-start.2 = ((bf16[4,112,128]{2,1,0:T(8,128)(2,1)}), bf16[4,112,128]{2,1,0:T(8,128)(2,1)S(1)}, u32[]{:S(2)}, u32[]{:S(2)}) async-start(bf16[4,112,128]{2,1,0:T(8,128)(2,1)} %near_sum.1), calls=%async_computation.2 | async-start | bytes 229376 | tf_op jit(solution)/shard_map/all_to_all | solution.py:392
  91.1 0.7 copy-start.9
  94.4 22.7 %collective-permute-start.4 = (bf16[128,640]{1,0:T(8,128)(2,1)}, bf16[128,640]{1,0:T(8,128)(2,1)S(1)}, u32[]{:S(2)}, u32[]{:S(2)}) collective-permute-start(bf16[128,640]{1,0:T(8,128)(2,1)} %get-tuple-element.44), channel_id=1, source_target_pairs={{0,256},{1,257},{2,258},{3,259},{4,260},{5,261},{6,262},{7,263},{8... | collective-permute-start | bytes 491528 | tf_op jit(solution)/shard_map/ppermute | solution.py:338
  112.4 15.0 %all-to-all-start.3 = ((bf16[8,112,128]{2,1,0:T(8,128)(2,1)}), bf16[8,112,128]{2,1,0:T(8,128)(2,1)S(1)}, u32[]{:S(2)}, u32[]{:S(2)}) async-start(bf16[8,112,128]{2,1,0:T(8,128)(2,1)} %mean.1), calls=%async_computation.3 | async-start | bytes 458752 | tf_op jit(solution)/shard_map/all_to_all | solution.py:394
  117.2 0.7 copy-start.4
Sparse Core Ops, SparseCore 0:
  11.9 94.2 all-gather.1

commit v4 on v3

--- a/solution.py
+++ b/solution.py
@@ -20,13 +20,13 @@
 ABSENT = 1024.0
 COSTS = {
     name: (flops * 10**9, 0)
-    for name, flops in (("move_step_1", 4), ("move_step_2", 14), ("move_step_3", 20), ("move_step_4", 16), ("outputs", 20))
+    for name, flops in (("move_step_1", 16), ("move_step_2", 10), ("move_step_3", 10), ("move_step_4", 10), ("outputs", 8))
 }
 N_DP = 32
 N_FSDP = 16
 VMEM = 20 * 1024 * 1024
 VMEM_FROM_HBM = 58 * 1024 * 1024
-FROM_HBM = ("outputs", "side_by_side", "next_attention", "move_step_1", "move_step_2", "move_step_3", "move_step_4")
+FROM_HBM = ("outputs", "side_by_side", "next_attention")
 
 NN = (((1,), (0,)), ((), ()))
 NT = (((1,), (1,)), ((), ()))
@@ -77,6 +77,10 @@
 ANY = pl.BlockSpec(memory_space=pl.ANY)
 
 
+def column_blocks(ref):
+    return [slice(i, i + HD) for i in range(0, ref.shape[-1], HD)]
+
+
 def attend(x_ref, seg_ref, out_ref, prob_ref=None):
     for b in range(2):
         rows = slice(b * ALIGNED_ROWS, (b + 1) * ALIGNED_ROWS)
@@ -88,53 +92,60 @@
             out_ref[rows, h * HD : (h + 1) * HD] = out[h * ALIGNED_ROWS : (h + 1) * ALIGNED_ROWS]
 
 
-def with_arrived(live, count, slots_ref, arrived_ref, slots_out):
-    top = live - count
-    present = (jnp.max(arrived_ref[0:16, 0:HD].astype(jnp.float32)) < ABSENT / 2).astype(jnp.int32)
-    place = jnp.where(present == 1, top, -1)
-    arrived = arrived_ref[...]
-    for s in range(SLOT_NUMBER):
-        rows = slice(s * ALIGNED_ROWS, (s + 1) * ALIGNED_ROWS)
-        slots_out[rows, :] = jnp.where(place == s, arrived, slots_ref[rows, :])
-    return top + present
-
-
-def leaving_block(live, count, slots_ref):
-    first, second = slots_ref[:ALIGNED_ROWS, :], slots_ref[ALIGNED_ROWS:, :]
-    block = jnp.where(live - count >= 1, second, first)
-    return jnp.where(count > 0, block, jnp.full_like(block, ABSENT))
-
-
-def next_kernel(live_ref, plan_ref, x_ref, seg_ref, out_ref, block_ref):
+def move(level, live, table_ref, slots_ref, block_ref, arrived_ref=None, slots_out=None):
+    square = (ALIGNED_ROWS, HD)
+    slot_rows = slice(0, ALIGNED_ROWS), slice(ALIGNED_ROWS, 2 * ALIGNED_ROWS)
+    if arrived_ref is not None:
+        top = live - table_ref[level : level + 1, :]
+        present = (arrived_ref[0:1, 0:HD].astype(jnp.float32) < ABSENT / 2).astype(jnp.int32)
+        live = top + present
+        place = jnp.where(present == 1, top, -1)
+    if block_ref is not None:
+        count = table_ref[level + 1 : level + 2, :]
+        leaving = jnp.broadcast_to(jnp.where(count > 0, jnp.maximum(live - count, 0), -1), square)
+    for columns in column_blocks(slots_ref):
+        slots = [slots_ref[rows, columns] for rows in slot_rows]
+        if arrived_ref is not None:
+            arrived = arrived_ref[:, columns]
+            for s in range(SLOT_NUMBER):
+                slots[s] = jnp.where(jnp.broadcast_to(place, square) == s, arrived, slots[s])
+                slots_out[slot_rows[s], columns] = slots[s]
+        if block_ref is not None:
+            block = jnp.where(leaving == 0, slots[0], jnp.full(square, ABSENT, jnp.bfloat16))
+            block_ref[:, columns] = jnp.where(leaving == 1, slots[1], block)
+    return live
+
+
+def next_kernel(live_ref, plan_ref, x_ref, seg_ref, out_ref, block_ref, table_ref):
     attend(x_ref, seg_ref, out_ref)
-    block_ref[...] = leaving_block(live_ref[0, 0], plan_ref[0, 0, 0], out_ref)
+    numbers = [live_ref[0, 0]] + [plan_ref[0, 0, level] for level in range(5)]
+    for row, number in enumerate(numbers):
+        table_ref[row : row + 1, :] = jnp.full((1, HD), number, jnp.int32)
+    table_ref[6:8, :] = jnp.zeros((2, HD), jnp.int32)
+    move(0, table_ref[0:1, :], table_ref, out_ref, block_ref)
 
 
 def next_attention(live, plan, qkv, segments):
     rows = qkv.shape[0]
     return call(
         next_kernel,
-        (bf16(rows, QW), bf16(ALIGNED_ROWS, QW)),
+        (bf16(rows, QW), bf16(ALIGNED_ROWS, QW), jax.ShapeDtypeStruct((8, HD), jnp.int32)),
         name="next_attention",
         in_specs=[SMEM, SMEM, WHOLE, WHOLE],
     )(live, plan, qkv, segments)
 
 
-def move_kernel(level, live_ref, plan_ref, slots_ref, arrived_ref, slots_out, live_out, block_ref):
-    live = with_arrived(live_ref[0, 0], plan_ref[0, 0, level - 1], slots_ref, arrived_ref, slots_out)
-    live_out[0, 0] = live
-    block_ref[...] = leaving_block(live, plan_ref[0, 0, level], slots_out)
-
-
-def move_step(level, plan, live, slots, block):
+def move_kernel(level, table_ref, live_ref, slots_ref, arrived_ref, slots_out, live_out, block_ref):
+    live_out[...] = move(level, live_ref[0:1, :], table_ref, slots_ref, block_ref, arrived_ref, slots_out)
+
+
+def move_step(level, table, live, slots, block):
     arrived = swap(block, 1 << (level - 1))
     return call(
         functools.partial(move_kernel, level),
-        (bf16(*slots.shape), jax.ShapeDtypeStruct(live.shape, jnp.int32), bf16(*block.shape)),
+        (bf16(*slots.shape), jax.ShapeDtypeStruct((1, HD), jnp.int32), bf16(*block.shape)),
         name=f"move_step_{level}",
-        in_specs=[SMEM, SMEM, WHOLE, WHOLE],
-        out_specs=(WHOLE, SMEM, WHOLE),
-    )(live, plan, slots, arrived)
+    )(table, live, slots, arrived)
 
 
 def current_kernel(x_ref, seg_ref, order_ref, keep_ref, send_ref, prob_ref, attn_ref):
@@ -159,7 +170,7 @@
 
 
 def outputs_kernel(
-    level, live_ref, plan_ref, x_hbm, prob_hbm, g_hbm, slots_hbm, arrived_hbm, w_hbm, grad_hbm, frozen_hbm,
+    level, table_ref, live_ref, x_hbm, prob_hbm, g_hbm, slots_hbm, arrived_hbm, w_hbm, grad_hbm, frozen_hbm,
     x_ref, prob_ref, g_ref, slots_ref, arrived_ref, w_ref, ga_ref, grad_ref, moved_ref, frozen_ref, sems, out_sems,
 ):
     g_copy, x_copy, prob_copy, slots_copy, arrived_copy = (
@@ -202,11 +213,13 @@
     grad_copy.start()
     slots_copy.wait()
     arrived_copy.wait()
-    live = with_arrived(live_ref[0, 0], plan_ref[0, 0, level], slots_ref, arrived_ref, moved_ref)
-    for s in range(SLOT_NUMBER):
-        rows = slice(s * ALIGNED_ROWS, (s + 1) * ALIGNED_ROWS)
-        block = moved_ref[rows, :]
-        moved_ref[rows, :] = jnp.where(live > s, block, jnp.zeros_like(block))
+    live = move(level, live_ref[0:1, :], table_ref, slots_ref, None, arrived_ref, moved_ref)
+    for columns in column_blocks(moved_ref):
+        for s in range(SLOT_NUMBER):
+            rows = slice(s * ALIGNED_ROWS, (s + 1) * ALIGNED_ROWS)
+            block = moved_ref[rows, columns]
+            alive = jnp.broadcast_to(live, block.shape) > s
+            moved_ref[rows, columns] = jnp.where(alive, block, jnp.zeros_like(block))
     out_copies = []
     for n, (copy, (i, j)) in enumerate(zip(frozen_copies, FROZEN_PARTS)):
         copy.wait()
@@ -219,7 +232,7 @@
         copy.wait()
 
 
-def outputs(level, live, plan, qkv, probs, grad_output, slots, arrived, weights):
+def outputs(level, table, live, qkv, probs, grad_output, slots, arrived, weights):
     rows = qkv.shape[0]
     inputs = (qkv, probs, grad_output, slots, arrived, weights)
     return call(
@@ -231,9 +244,9 @@
         + [pltpu.SemaphoreType.DMA((10,)), pltpu.SemaphoreType.DMA((3,))],
         (3 * 10**9, 10**7),
         "outputs",
-        in_specs=[SMEM, SMEM] + [ANY] * len(inputs),
+        in_specs=[WHOLE, WHOLE] + [ANY] * len(inputs),
         out_specs=(ANY, ANY),
-    )(live, plan, *inputs)
+    )(table, live, *inputs)
 
 
 def terms_kernel(a_ref, g_ref, out_ref):
@@ -373,29 +386,29 @@
 
     own = side_by_side(policy_out, frozen_out)
     weights = lax.all_gather(own, "fsdp", axis=0, tiled=True)
-    live, plan = block_counts, move_plan
-    slots, block = next_attention(
-        live, plan, after(query_key_value_next, own), document_next.reshape(SLOT_NUMBER, ALIGNED_ROWS)
-    )
+    slots, block, table = next_attention(
+        block_counts, move_plan, after(query_key_value_next, own), document_next.reshape(SLOT_NUMBER, ALIGNED_ROWS)
+    )
+    live = table
     keep_half, send_half, probs = current_attention(
         after(qkv_current, slots), segment_current.reshape(2, ALIGNED_ROWS), sum_order(me)
     )
-    slots, live, block = move_step(1, plan, live, slots, block)
-    other = lax.ppermute(terms_to_send(after(send_half, live), grad_output), "fsdp", fsdp_pairs(1, 0))
-    parts = terms_with_other_core(keep_half, grad_output, other)
+    slots, live, block = move_step(1, table, live, slots, block)
+    other = lax.ppermute(terms_to_send(send_half, grad_output), "fsdp", fsdp_pairs(1, 0))
+    parts = terms_with_other_core(keep_half, grad_output, after(other, live))
+    slots, live, block = move_step(2, table, live, slots, block)
     parts = lax.all_to_all(parts, "fsdp", 0, 0, axis_index_groups=same_core)
-    slots, live, block = move_step(2, plan, live, slots, block)
+    slots, live, block = move_step(3, table, live, slots, block)
     shares = group_sum(after(parts, live))
     shares = lax.all_to_all(shares, "dp", 0, 0, axis_index_groups=near)
-    slots, live, block = move_step(3, plan, live, slots, block)
+    slots, live, block = move_step(4, table, live, slots, block)
     shares = spread_sum(after(shares, live), len(far[0]), 1.0, "near_sum")
+    block = swap(block, 16)
     shares = lax.all_to_all(shares, "dp", 0, 0, axis_index_groups=far)
     shares = spread_sum(shares, PEERS, 1.0 / (N_DP * N_FSDP), "mean")
     shares = lax.all_to_all(shares, "dp", 0, 0, axis_index_groups=near)
-    slots, live, block = move_step(4, plan, live, slots, block)
-    block = swap(block, 16)
     qkv_gradient, frozen_layer_output = outputs(
-        4, live, plan, qkv_current, probs, grad_output, slots, block, weights
+        5, table, live, qkv_current, probs, grad_output, slots, block, weights
     )
     weight_grad = join(after(shares, qkv_gradient))
     return (qkv_gradient, weight_grad, frozen_layer_output)

time: 137 us -> 136 us (level)
  the two profiles are of different devices: /device:TPU:24 before, /device:TPU:33 now
where the time goes in v4:
time: 136 us; the launch traced here: 135 us
  starting transfers between devices  60.5 us (44%)
  waiting for transfers between devices  36.1 us (27%)
  Pallas kernels  20.9 us (15%)
  between operations  15 us (11%)
  local copies, waits for them, and re-layouts  2.4 us (2%)
    ppermute x5, starting transfers between devices, swap(): return lax.ppermute(a, ('dp', 'fsdp'), all_pairs(dp_flip, fsdp_flip))  26.5 us
    ppermute x5, waiting for transfers between devices, swap(): return lax.ppermute(a, ('dp', 'fsdp'), all_pairs(dp_flip, fsdp_flip))  15.2 us
    all_to_all x2, starting transfers between devices, body(): shares = lax.all_to_all(shares, 'dp', 0, 0, axis_index_groups=near)  14.7 us
    all_to_all x1, waiting for transfers between devices, body(): shares = lax.all_to_all(shares, 'dp', 0, 0, axis_index_groups=far)  9.62 us
    pallas_call x1, Pallas kernels, outputs(): call(functools.partial(outputs_kernel, level), (bf16(*qkv.shape), bf16(ro...  8.87 us
    ppermute x1, starting transfers between devices, body(): lax.ppermute(terms_to_send(send_half, grad_output), 'fsdp', fsdp_pairs(1,...  8.05 us
    all_to_all x1, starting transfers between devices, body(): shares = lax.all_to_all(shares, 'dp', 0, 0, axis_index_groups=far)  7.17 us
    all_gather x1, waiting for transfers between devices, body(): weights = lax.all_gather(own, 'fsdp', axis=0, tiled=True)  5.97 us
  transfers between devices with their start and end apart: 11, of which 7 were waited for; matrix products, arithmetic and copies ran while one was open for 0% of the time, Pallas kernels for 14%

profile of v4, /device:TPU:33, one launch (start us, length us, event | category | flops | bytes accessed | tf_op | source)
XLA Modules:
  0.0 135.2 jit_solution(171329539081542904)
XLA Ops:
  7.2 0.0 copy-start.1
  7.2 0.0 copy-start.2
  7.2 0.0 all-gather.2.cloned.1.call-start
  7.2 1.8 %side_by_side.1 = bf16[40,5120]{1,0:T(8,128)(2,1)} custom-call(bf16[40,2560]{1,0:T(8,128)(2,1)} %left.1, bf16[40,2560]{1,0:T(8,128)(2,1)} %right.1), custom_call_target="tpu_custom_call" | custom-call | flops 100000000 | bytes 1000000 | tf_op jit(solution)/shard_map/side_by_side/pallas_call | solution.py:333
  9.1 0.0 all-gather.2.cloned.1.call-update
  9.9 2.8 %next_attention.1 = (bf16[256,640]{1,0:T(8,128)(2,1)}, bf16[128,640]{1,0:T(8,128)(2,1)}, s32[8,128]{1,0:T(8,128)}) custom-call(s32[1,1]{1,0:T(1,128)S(6)} %copy.12.live_ref, s32[1,1,5]{2,1,0:T(1,128)} %plan_ref.1, bf16[256,896]{1,0:T(8,128)(2,1)} %x_ref, s32[2,128]{1,0:T(2,128)} %bitcast.3), custom_call_target="tpu_custom_call" | custom-call | flops 100000000 | bytes 1000000 | tf_op jit(solution)/shard_map/next_attention/pallas_call | solution.py:130
  12.7 1.9 %collective-permute-start = (bf16[128,640]{1,0:T(8,128)(2,1)}, bf16[128,640]{1,0:T(8,128)(2,1)S(1)}, u32[]{:S(2)}, u32[]{:S(2)}) collective-permute-start(bf16[128,640]{1,0:T(8,128)(2,1)} %get-tuple-element.32), channel_id=1, source_target_pairs={{0,16},{1,17},{2,18},{3,19},{4,20},{5,21},{6,22},{7,23},{8,24},{9,... | collective-permute-start | bytes 491528 | tf_op jit(solution)/shard_map/ppermute | solution.py:351
  14.6 0.2 fusion.order_ref
  14.8 0.0 copy-done.1
  14.8 0.0 copy-done.2
  14.9 1.5 %current_attention.1 = (bf16[256,320]{1,0:T(8,128)(2,1)S(1)}, bf16[256,320]{1,0:T(8,128)(2,1)S(1)}, f32[2,640,128]{2,1,0:T(8,128)S(1)}) custom-call(bf16[256,896]{1,0:T(8,128)(2,1)S(1)} %copy-done.1, s32[2,128]{1,0:T(2,128)S(1)} %bitcast.2, bf16[640,640]{1,0:T(8,128)(2,1)S(1)} %fusion.order_ref), custom_call_target="tpu_custom_call" | custom-call | flops 100000000 | bytes 1000000 | tf_op jit(solution)/shard_map/current_attention/pallas_call | solution.py:160
  16.3 0.0 copy-start.3
  16.4 0.9 copy-done.3
  17.3 0.0 copy-done
  17.3 0.6 terms_to_send.1
  17.9 8.1 %collective-permute-start.5 = (bf16[320,2560]{1,0:T(8,128)(2,1)S(1)}, bf16[320,2560]{1,0:T(8,128)(2,1)S(1)}, u32[]{:S(2)}, u32[]{:S(2)}) collective-permute-start(bf16[320,2560]{1,0:T(8,128)(2,1)S(1)} %terms_to_send.1), channel_id=1, source_target_pairs={{0,1},{1,0},{2,3},{3,2},{4,5},{5,4},{6,7},{7,6},{8,9},{9,8},{10,11... | collective-permute-start | bytes 4915208 | tf_op jit(solution)/shard_map/ppermute | solution.py:397
  26.0 0.0 collective-permute-done.arrived_ref
  26.0 0.1 move_step_1.1
  26.1 0.0 copy-start.7
  26.1 0.7 copy-done.7
  26.8 1.9 %collective-permute-start.1 = (bf16[128,640]{1,0:T(8,128)(2,1)S(1)}, bf16[128,640]{1,0:T(8,128)(2,1)S(1)}, u32[]{:S(2)}, u32[]{:S(2)}) collective-permute-start(bf16[128,640]{1,0:T(8,128)(2,1)S(1)} %get-tuple-element.35), channel_id=1, source_target_pairs={{0,32},{1,33},{2,34},{3,35},{4,36},{5,37},{6,38},{7,39},{8,40},{9,... | collective-permute-start | bytes 491528 | tf_op jit(solution)/shard_map/ppermute | solution.py:351
  28.8 0.3 collective-permute-done.5.other_ref
  29.1 1.9 %terms_with_other_core.1 = bf16[8,40,2560]{2,1,0:T(8,128)(2,1)} custom-call(bf16[256,320]{1,0:T(8,128)(2,1)S(1)} %get-tuple-element.48.a_ref, bf16[256,2560]{1,0:T(8,128)(2,1)S(1)} %copy-done, bf16[320,2560]{1,0:T(8,128)(2,1)S(1)} %collective-permute-done.5.other_ref), custom_call_target="tpu_custom_call" | custom-call | flops 100000000 | bytes 1000000 | tf_op jit(solution)/shard_map/terms_with_other_core/pallas_call | solution.py:272
  30.9 4.1 %all-to-all-start = ((bf16[8,40,2560]{2,1,0:T(8,128)(2,1)}), bf16[8,40,2560]{2,1,0:T(8,128)(2,1)S(1)}, u32[]{:S(2)}, u32[]{:S(2)}) async-start(bf16[8,40,2560]{2,1,0:T(8,128)(2,1)} %terms_with_other_core.1), calls=%async_computation | async-start | bytes 3276800 | tf_op jit(solution)/shard_map/all_to_all | solution.py:400
  35.0 0.7 collective-permute-done.1.arrived_ref
  35.7 0.1 move_step_2.1
  35.8 8.2 %collective-permute-start.2 = (bf16[128,640]{1,0:T(8,128)(2,1)S(1)}, bf16[128,640]{1,0:T(8,128)(2,1)S(1)}, u32[]{:S(2)}, u32[]{:S(2)}) collective-permute-start(bf16[128,640]{1,0:T(8,128)(2,1)S(1)} %get-tuple-element.38), channel_id=1, source_target_pairs={{0,64},{1,65},{2,66},{3,67},{4,68},{5,69},{6,70},{7,71},{8,72},{9,... | collective-permute-start | bytes 491528 | tf_op jit(solution)/shard_map/ppermute | solution.py:351
  44.0 11.1 %collective-permute-done.2.arrived_ref = bf16[128,640]{1,0:T(8,128)(2,1)S(1)} collective-permute-done((bf16[128,640]{1,0:T(8,128)(2,1)S(1)}, bf16[128,640]{1,0:T(8,128)(2,1)S(1)}, u32[]{:S(2)}, u32[]{:S(2)}) %collective-permute-start.2) | collective-permute-done | bytes 163872 | tf_op jit(solution)/shard_map/ppermute | solution.py:351
  55.1 0.1 move_step_3.1
  55.2 12.2 %collective-permute-start.3 = (bf16[128,640]{1,0:T(8,128)(2,1)S(1)}, bf16[128,640]{1,0:T(8,128)(2,1)S(1)}, u32[]{:S(2)}, u32[]{:S(2)}) collective-permute-start(bf16[128,640]{1,0:T(8,128)(2,1)S(1)} %get-tuple-element.41), channel_id=1, source_target_pairs={{0,128},{1,129},{2,130},{3,131},{4,132},{5,133},{6,134},{7,135},{8... | collective-permute-start | bytes 491528 | tf_op jit(solution)/shard_map/ppermute | solution.py:351
  67.4 0.0 all-to-all-done.parts_ref
  67.4 0.9 group_sum.1
  68.3 8.2 %all-to-all-start.1 = ((bf16[8,112,128]{2,1,0:T(8,128)(2,1)}), bf16[8,112,128]{2,1,0:T(8,128)(2,1)S(1)}, u32[]{:S(2)}, u32[]{:S(2)}) async-start(bf16[8,112,128]{2,1,0:T(8,128)(2,1)} %group_sum.1), calls=%async_computation.1 | async-start | bytes 458752 | tf_op jit(solution)/shard_map/all_to_all | solution.py:403
  76.6 3.4 %collective-permute-done.3.arrived_ref = bf16[128,640]{1,0:T(8,128)(2,1)S(1)} collective-permute-done((bf16[128,640]{1,0:T(8,128)(2,1)S(1)}, bf16[128,640]{1,0:T(8,128)(2,1)S(1)}, u32[]{:S(2)}, u32[]{:S(2)}) %collective-permute-start.3) | collective-permute-done | bytes 163872 | tf_op jit(solution)/shard_map/ppermute | solution.py:351
  80.0 0.1 move_step_4.1
  80.1 0.7 copy-done.6
  80.8 4.9 %all-to-all-done.1.parts_ref = bf16[8,112,128]{2,1,0:T(8,128)(2,1)S(1)} async-done(((bf16[8,112,128]{2,1,0:T(8,128)(2,1)}), bf16[8,112,128]{2,1,0:T(8,128)(2,1)S(1)}, u32[]{:S(2)}, u32[]{:S(2)}) %all-to-all-start.1) | async-done | bytes 229408 | tf_op jit(solution)/shard_map/all_to_all | solution.py:403
  85.7 0.7 near_sum.1
  86.4 7.2 %all-to-all-start.2 = ((bf16[4,112,128]{2,1,0:T(8,128)(2,1)}), bf16[4,112,128]{2,1,0:T(8,128)(2,1)S(1)}, u32[]{:S(2)}, u32[]{:S(2)}) async-start(bf16[4,112,128]{2,1,0:T(8,128)(2,1)} %near_sum.1), calls=%async_computation.2 | async-start | bytes 229376 | tf_op jit(solution)/shard_map/all_to_all | solution.py:407
  93.6 2.3 %collective-permute-start.4 = (bf16[128,640]{1,0:T(8,128)(2,1)S(1)}, bf16[128,640]{1,0:T(8,128)(2,1)S(1)}, u32[]{:S(2)}, u32[]{:S(2)}) collective-permute-start(bf16[128,640]{1,0:T(8,128)(2,1)S(1)} %get-tuple-element.46), channel_id=1, source_target_pairs={{0,256},{1,257},{2,258},{3,259},{4,260},{5,261},{6,262},{7,263},{8... | collective-permute-start | bytes 491528 | tf_op jit(solution)/shard_map/ppermute | solution.py:351
  95.9 9.6 %all-to-all-done.2.parts_ref = bf16[4,112,128]{2,1,0:T(8,128)(2,1)S(1)} async-done(((bf16[4,112,128]{2,1,0:T(8,128)(2,1)}), bf16[4,112,128]{2,1,0:T(8,128)(2,1)S(1)}, u32[]{:S(2)}, u32[]{:S(2)}) %all-to-all-start.2) | async-done | bytes 114720 | tf_op jit(solution)/shard_map/all_to_all | solution.py:407
  105.5 0.7 mean.1
  106.3 6.5 %all-to-all-start.3 = ((bf16[8,112,128]{2,1,0:T(8,128)(2,1)}), bf16[8,112,128]{2,1,0:T(8,128)(2,1)S(1)}, u32[]{:S(2)}, u32[]{:S(2)}) async-start(bf16[8,112,128]{2,1,0:T(8,128)(2,1)} %mean.1), calls=%async_computation.3 | async-start | bytes 458752 | tf_op jit(solution)/shard_map/all_to_all | solution.py:409
  112.7 0.0 collective-permute-done.4.arrived_hbm
  112.7 6.0 %all-gather.2.cloned.1.call-done.w_hbm = bf16[640,5120]{1,0:T(8,128)(2,1)} async-done(((bf16[40,5120]{1,0:T(8,128)(2,1)}), bf16[640,5120]{1,0:T(8,128)(2,1)}) %all-gather.2.cloned.1.call-update) | async-done | bytes 6553616 | tf_op jit(solution)/shard_map/all_gather | solution.py:388
  118.7 8.9 %outputs.1 = (bf16[256,896]{1,0:T(8,128)(2,1)}, bf16[256,2560]{1,0:T(8,128)(2,1)}) custom-call(s32[8,128]{1,0:T(8,128)} %get-tuple-element.30.table_ref.live_ref, s32[1,128]{1,0:T(1,128)} %copy-done.9, bf16[256,896]{1,0:T(8,128)(2,1)} %x_hbm.1, f32[2,640,128]{2,1,0:T(8,128)} %copy-done.3, bf16[256,2560]{1,0:T(8,128)(2,1)} %g_ref.3, ...), custom_call_target="tpu_custom_call" | custom-call | flops 8000000000 | tf_op jit(solution)/shard_map/outputs/pallas_call | solution.py:238
  127.6 0.0 all-to-all-done.3.shares_ref
  127.6 0.7 join.1
  (13 shorter events, 0.0 us)
Async XLA Ops:
  7.2 7.7 %copy-start.1 = (bf16[256,896]{1,0:T(8,128)(2,1)S(1)}, bf16[256,896]{1,0:T(8,128)(2,1)}, u32[]{:S(2)}) copy-start(bf16[256,896]{1,0:T(8,128)(2,1)} %x_hbm.1) | copy-start | bytes 1376260
  7.2 7.7 %copy-start.2 = (s32[256]{0:T(256)S(1)}, s32[256]{0:T(256)}, u32[]{:S(2)}) copy-start(s32[256]{0:T(256)} %param.12) | copy-start | bytes 3076
  7.2 111.5 %all-gather.2.cloned.1.call-start = ((), (), s32[]{:S(2)}) async-start(), calls=%async_computation.4 | async-start | bytes 6963200 | tf_op jit(solution)/shard_map/all_gather | solution.py:388
  9.1 8.2 %copy-start = (bf16[256,2560]{1,0:T(8,128)(2,1)S(1)}, bf16[256,2560]{1,0:T(8,128)(2,1)}, u32[]{:S(2)}) copy-start(bf16[256,2560]{1,0:T(8,128)(2,1)} %g_ref.3) | copy-start | bytes 3932164
  12.7 13.3 %collective-permute-start = (bf16[128,640]{1,0:T(8,128)(2,1)}, bf16[128,640]{1,0:T(8,128)(2,1)S(1)}, u32[]{:S(2)}, u32[]{:S(2)}) collective-permute-start(bf16[128,640]{1,0:T(8,128)(2,1)} %get-tuple-element.32), channel_id=1, source_target_pairs={{0,16},{1,17},{2,18},{3,19},{4,20},{5,21},{6,22},{7,23},{8,24},{9,... | collective-permute-start | bytes 491528 | tf_op jit(solution)/shard_map/ppermute | solution.py:351
  16.3 0.9 copy-start.3
  17.3 8.7 %copy-start.4 = (bf16[256,640]{1,0:T(8,128)(2,1)S(1)}, bf16[256,640]{1,0:T(8,128)(2,1)}, u32[]{:S(2)}) copy-start(bf16[256,640]{1,0:T(8,128)(2,1)} %get-tuple-element.31.slots_ref) | copy-start | bytes 983044
  17.3 8.7 %copy-start.5 = (s32[8,128]{1,0:T(8,128)S(1)}, s32[8,128]{1,0:T(8,128)}, u32[]{:S(2)}) copy-start(s32[8,128]{1,0:T(8,128)} %get-tuple-element.30.table_ref.live_ref) | copy-start | bytes 12292
  17.9 11.2 %collective-permute-start.5 = (bf16[320,2560]{1,0:T(8,128)(2,1)S(1)}, bf16[320,2560]{1,0:T(8,128)(2,1)S(1)}, u32[]{:S(2)}, u32[]{:S(2)}) collective-permute-start(bf16[320,2560]{1,0:T(8,128)(2,1)S(1)} %terms_to_send.1), channel_id=1, source_target_pairs={{0,1},{1,0},{2,3},{3,2},{4,5},{5,4},{6,7},{7,6},{8,9},{9,8},{10,11... | collective-permute-start | bytes 4915208 | tf_op jit(solution)/shard_map/ppermute | solution.py:397
  26.1 0.7 copy-start.7
  26.8 8.9 %collective-permute-start.1 = (bf16[128,640]{1,0:T(8,128)(2,1)S(1)}, bf16[128,640]{1,0:T(8,128)(2,1)S(1)}, u32[]{:S(2)}, u32[]{:S(2)}) collective-permute-start(bf16[128,640]{1,0:T(8,128)(2,1)S(1)} %get-tuple-element.35), channel_id=1, source_target_pairs={{0,32},{1,33},{2,34},{3,35},{4,36},{5,37},{6,38},{7,39},{8,40},{9,... | collective-permute-start | bytes 491528 | tf_op jit(solution)/shard_map/ppermute | solution.py:351
  30.9 4.8 %copy-start.8 = (bf16[256,640]{1,0:T(8,128)(2,1)S(1)}, bf16[256,640]{1,0:T(8,128)(2,1)}, u32[]{:S(2)}) copy-start(bf16[256,640]{1,0:T(8,128)(2,1)} %copy-done.7) | copy-start | bytes 983044
  30.9 36.5 %all-to-all-start = ((bf16[8,40,2560]{2,1,0:T(8,128)(2,1)}), bf16[8,40,2560]{2,1,0:T(8,128)(2,1)S(1)}, u32[]{:S(2)}, u32[]{:S(2)}) async-start(bf16[8,40,2560]{2,1,0:T(8,128)(2,1)} %terms_with_other_core.1), calls=%async_computation | async-start | bytes 3276800 | tf_op jit(solution)/shard_map/all_to_all | solution.py:400
  35.8 19.3 %collective-permute-start.2 = (bf16[128,640]{1,0:T(8,128)(2,1)S(1)}, bf16[128,640]{1,0:T(8,128)(2,1)S(1)}, u32[]{:S(2)}, u32[]{:S(2)}) collective-permute-start(bf16[128,640]{1,0:T(8,128)(2,1)S(1)} %get-tuple-element.38), channel_id=1, source_target_pairs={{0,64},{1,65},{2,66},{3,67},{4,68},{5,69},{6,70},{7,71},{8,72},{9,... | collective-permute-start | bytes 491528 | tf_op jit(solution)/shard_map/ppermute | solution.py:351
  55.2 24.8 %collective-permute-start.3 = (bf16[128,640]{1,0:T(8,128)(2,1)S(1)}, bf16[128,640]{1,0:T(8,128)(2,1)S(1)}, u32[]{:S(2)}, u32[]{:S(2)}) collective-permute-start(bf16[128,640]{1,0:T(8,128)(2,1)S(1)} %get-tuple-element.41), channel_id=1, source_target_pairs={{0,128},{1,129},{2,130},{3,131},{4,132},{5,133},{6,134},{7,135},{8... | collective-permute-start | bytes 491528 | tf_op jit(solution)/shard_map/ppermute | solution.py:351
  68.3 17.4 %all-to-all-start.1 = ((bf16[8,112,128]{2,1,0:T(8,128)(2,1)}), bf16[8,112,128]{2,1,0:T(8,128)(2,1)S(1)}, u32[]{:S(2)}, u32[]{:S(2)}) async-start(bf16[8,112,128]{2,1,0:T(8,128)(2,1)} %group_sum.1), calls=%async_computation.1 | async-start | bytes 458752 | tf_op jit(solution)/shard_map/all_to_all | solution.py:403
  80.1 0.7 copy-start.6
  80.8 37.9 %copy-start.9 = (s32[1,128]{1,0:T(1,128)}, s32[1,128]{1,0:T(1,128)S(1)}, u32[]{:S(2)}) copy-start(s32[1,128]{1,0:T(1,128)S(1)} %get-tuple-element.42.live_ref) | copy-start | bytes 1540
  86.4 19.1 %all-to-all-start.2 = ((bf16[4,112,128]{2,1,0:T(8,128)(2,1)}), bf16[4,112,128]{2,1,0:T(8,128)(2,1)S(1)}, u32[]{:S(2)}, u32[]{:S(2)}) async-start(bf16[4,112,128]{2,1,0:T(8,128)(2,1)} %near_sum.1), calls=%async_computation.2 | async-start | bytes 229376 | tf_op jit(solution)/shard_map/all_to_all | solution.py:407
  93.6 19.1 %collective-permute-start.4 = (bf16[128,640]{1,0:T(8,128)(2,1)S(1)}, bf16[128,640]{1,0:T(8,128)(2,1)S(1)}, u32[]{:S(2)}, u32[]{:S(2)}) collective-permute-start(bf16[128,640]{1,0:T(8,128)(2,1)S(1)} %get-tuple-element.46), channel_id=1, source_target_pairs={{0,256},{1,257},{2,258},{3,259},{4,260},{5,261},{6,262},{7,263},{8... | collective-permute-start | bytes 491528 | tf_op jit(solution)/shard_map/ppermute | solution.py:351
  106.3 21.3 %all-to-all-start.3 = ((bf16[8,112,128]{2,1,0:T(8,128)(2,1)}), bf16[8,112,128]{2,1,0:T(8,128)(2,1)S(1)}, u32[]{:S(2)}, u32[]{:S(2)}) async-start(bf16[8,112,128]{2,1,0:T(8,128)(2,1)} %mean.1), calls=%async_computation.3 | async-start | bytes 458752 | tf_op jit(solution)/shard_map/all_to_all | solution.py:409
  112.7 6.0 %copy-start.10 = (bf16[128,640]{1,0:T(8,128)(2,1)}, bf16[128,640]{1,0:T(8,128)(2,1)S(1)}, u32[]{:S(2)}) copy-start(bf16[128,640]{1,0:T(8,128)(2,1)S(1)} %collective-permute-done.4.arrived_hbm) | copy-start | bytes 491524
Sparse Core Ops, SparseCore 0:
  11.9 106.7 all-gather.1

commit v5 on v4

--- a/solution.py
+++ b/solution.py
@@ -165,7 +165,7 @@
     )(qkv, segments, order)
 
 
-POLICY_PARTS = (0, 256), (256, 512), (512, QW)
+POLICY_PARTS = ((0, QW),)
 FROZEN_PARTS = (0, D // 2), (D // 2, D)
 
 
@@ -184,7 +184,7 @@
         for n, (i, j) in enumerate(POLICY_PARTS)
     ]
     frozen_copies = [
-        pltpu.make_async_copy(w_hbm.at[:, pl.ds(D + i, j - i)], w_ref.at[:, pl.ds(D + i, j - i)], sems.at[8 + n])
+        pltpu.make_async_copy(w_hbm.at[:, pl.ds(D + i, j - i)], w_ref.at[:, pl.ds(D + i, j - i)], sems.at[6 + n])
         for n, (i, j) in enumerate(FROZEN_PARTS)
     ]
     for copy in (g_copy, *policy_copies, x_copy, prob_copy, slots_copy, arrived_copy, *frozen_copies):
@@ -202,12 +202,11 @@
         p = prob_ref[b]
         dp = dot(ga, v, NT)
         ds = p * (dp - jnp.sum(p * dp, axis=-1, keepdims=True))
-        high = ds.astype(jnp.bfloat16)
-        low = (ds - high.astype(jnp.float32)).astype(jnp.bfloat16)
-        dq = ((dot(high, k, NN) + dot(low, k, NN)) * SCALE).astype(jnp.bfloat16)
+        ds = ds.astype(jnp.bfloat16)
+        dq = (dot(ds, k, NN) * SCALE).astype(jnp.bfloat16)
         for h in range(HQ):
             grad_ref[rows, h * HD : (h + 1) * HD] = dq[h * ALIGNED_ROWS : (h + 1) * ALIGNED_ROWS]
-        grad_ref[rows, QW : QW + HD] = ((dot(high, q, TN) + dot(low, q, TN)) * SCALE).astype(jnp.bfloat16)
+        grad_ref[rows, QW : QW + HD] = (dot(ds, q, TN) * SCALE).astype(jnp.bfloat16)
         grad_ref[rows, QW + HD :] = dot(p.astype(jnp.bfloat16), ga, TN).astype(jnp.bfloat16)
     grad_copy = pltpu.make_async_copy(grad_ref, grad_hbm, out_sems.at[0])
     grad_copy.start()
@@ -241,7 +240,7 @@
         [pltpu.VMEM(a.shape, a.dtype) for a in inputs]
         + [pltpu.VMEM((rows, QW), jnp.bfloat16), pltpu.VMEM(qkv.shape, jnp.bfloat16)]
         + [pltpu.VMEM((rows, QW), jnp.bfloat16), pltpu.VMEM((rows, D), jnp.bfloat16)]
-        + [pltpu.SemaphoreType.DMA((10,)), pltpu.SemaphoreType.DMA((3,))],
+        + [pltpu.SemaphoreType.DMA((8,)), pltpu.SemaphoreType.DMA((3,))],
         (3 * 10**9, 10**7),
         "outputs",
         in_specs=[WHOLE, WHOLE] + [ANY] * len(inputs),

time: 136 us -> 135 us (level)
  transfers between devices with their start and end apart: 11 -> 11, of which waited for: 7 -> 7; matrix products, arithmetic and copies ran while one was open for 0% -> 0% of each run, Pallas kernels for 14% -> 13%
where the time goes in v5:
time: 135 us
  starting transfers between devices  60.5 us (45%)
  waiting for transfers between devices  36.1 us (27%)
  Pallas kernels  20.3 us (15%)
  between operations  15 us (11%)
  local copies, waits for them, and re-layouts  2.4 us (2%)
    ppermute x5, starting transfers between devices, swap(): return lax.ppermute(a, ('dp', 'fsdp'), all_pairs(dp_flip, fsdp_flip))  26.5 us
    ppermute x5, waiting for transfers between devices, swap(): return lax.ppermute(a, ('dp', 'fsdp'), all_pairs(dp_flip, fsdp_flip))  15.2 us
    all_to_all x2, starting transfers between devices, body(): shares = lax.all_to_all(shares, 'dp', 0, 0, axis_index_groups=near)  14.7 us
    all_to_all x1, waiting for transfers between devices, body(): shares = lax.all_to_all(shares, 'dp', 0, 0, axis_index_groups=far)  9.62 us
    pallas_call x1, Pallas kernels, outputs(): call(functools.partial(outputs_kernel, level), (bf16(*qkv.shape), bf16(ro...  8.26 us
    ppermute x1, starting transfers between devices, body(): lax.ppermute(terms_to_send(send_half, grad_output), 'fsdp', fsdp_pairs(1,...  8.05 us
    all_to_all x1, starting transfers between devices, body(): shares = lax.all_to_all(shares, 'dp', 0, 0, axis_index_groups=far)  7.17 us
    all_gather x1, waiting for transfers between devices, body(): weights = lax.all_gather(own, 'fsdp', axis=0, tiled=True)  5.97 us
  transfers between devices with their start and end apart: 11, of which 7 were waited for; matrix products, arithmetic and copies ran while one was open for 0% of the time, Pallas kernels for 13%

profile of v5, /device:TPU:33, one launch (start us, length us, event | category | flops | bytes accessed | tf_op | source)
XLA Modules:
  0.0 134.5 jit_solution(10405849298870690880)
XLA Ops:
  7.2 0.0 copy-start.1
  7.2 0.0 copy-start.2
  7.2 0.0 all-gather.2.cloned.1.call-start
  7.2 1.8 %side_by_side.1 = bf16[40,5120]{1,0:T(8,128)(2,1)} custom-call(bf16[40,2560]{1,0:T(8,128)(2,1)} %left.1, bf16[40,2560]{1,0:T(8,128)(2,1)} %right.1), custom_call_target="tpu_custom_call" | custom-call | flops 100000000 | bytes 1000000 | tf_op jit(solution)/shard_map/side_by_side/pallas_call | solution.py:332
  9.1 0.0 all-gather.2.cloned.1.call-update
  9.9 2.8 %next_attention.1 = (bf16[256,640]{1,0:T(8,128)(2,1)}, bf16[128,640]{1,0:T(8,128)(2,1)}, s32[8,128]{1,0:T(8,128)}) custom-call(s32[1,1]{1,0:T(1,128)S(6)} %copy.12.live_ref, s32[1,1,5]{2,1,0:T(1,128)} %plan_ref.1, bf16[256,896]{1,0:T(8,128)(2,1)} %x_ref, s32[2,128]{1,0:T(2,128)} %bitcast.3), custom_call_target="tpu_custom_call" | custom-call | flops 100000000 | bytes 1000000 | tf_op jit(solution)/shard_map/next_attention/pallas_call | solution.py:130
  12.7 1.9 %collective-permute-start = (bf16[128,640]{1,0:T(8,128)(2,1)}, bf16[128,640]{1,0:T(8,128)(2,1)S(1)}, u32[]{:S(2)}, u32[]{:S(2)}) collective-permute-start(bf16[128,640]{1,0:T(8,128)(2,1)} %get-tuple-element.32), channel_id=1, source_target_pairs={{0,16},{1,17},{2,18},{3,19},{4,20},{5,21},{6,22},{7,23},{8,24},{9,... | collective-permute-start | bytes 491528 | tf_op jit(solution)/shard_map/ppermute | solution.py:350
  14.6 0.2 fusion.order_ref
  14.8 0.0 copy-done.1
  14.9 1.5 %current_attention.1 = (bf16[256,320]{1,0:T(8,128)(2,1)S(1)}, bf16[256,320]{1,0:T(8,128)(2,1)S(1)}, f32[2,640,128]{2,1,0:T(8,128)S(1)}) custom-call(bf16[256,896]{1,0:T(8,128)(2,1)S(1)} %copy-done.1, s32[2,128]{1,0:T(2,128)S(1)} %bitcast.2, bf16[640,640]{1,0:T(8,128)(2,1)S(1)} %fusion.order_ref), custom_call_target="tpu_custom_call" | custom-call | flops 100000000 | bytes 1000000 | tf_op jit(solution)/shard_map/current_attention/pallas_call | solution.py:160
  16.3 0.0 copy-start.3
  16.4 0.9 copy-done.3
  17.3 0.0 copy-done
  17.3 0.6 terms_to_send.1
  17.9 8.1 %collective-permute-start.5 = (bf16[320,2560]{1,0:T(8,128)(2,1)S(1)}, bf16[320,2560]{1,0:T(8,128)(2,1)S(1)}, u32[]{:S(2)}, u32[]{:S(2)}) collective-permute-start(bf16[320,2560]{1,0:T(8,128)(2,1)S(1)} %terms_to_send.1), channel_id=1, source_target_pairs={{0,1},{1,0},{2,3},{3,2},{4,5},{5,4},{6,7},{7,6},{8,9},{9,8},{10,11... | collective-permute-start | bytes 4915208 | tf_op jit(solution)/shard_map/ppermute | solution.py:396
  26.0 0.0 collective-permute-done.arrived_ref
  26.0 0.1 move_step_1.1
  26.1 0.0 copy-start.7
  26.1 0.7 copy-done.7
  26.8 1.9 %collective-permute-start.1 = (bf16[128,640]{1,0:T(8,128)(2,1)S(1)}, bf16[128,640]{1,0:T(8,128)(2,1)S(1)}, u32[]{:S(2)}, u32[]{:S(2)}) collective-permute-start(bf16[128,640]{1,0:T(8,128)(2,1)S(1)} %get-tuple-element.35), channel_id=1, source_target_pairs={{0,32},{1,33},{2,34},{3,35},{4,36},{5,37},{6,38},{7,39},{8,40},{9,... | collective-permute-start | bytes 491528 | tf_op jit(solution)/shard_map/ppermute | solution.py:350
  28.8 0.3 collective-permute-done.5.other_ref
  29.1 1.9 %terms_with_other_core.1 = bf16[8,40,2560]{2,1,0:T(8,128)(2,1)} custom-call(bf16[256,320]{1,0:T(8,128)(2,1)S(1)} %get-tuple-element.48.a_ref, bf16[256,2560]{1,0:T(8,128)(2,1)S(1)} %copy-done, bf16[320,2560]{1,0:T(8,128)(2,1)S(1)} %collective-permute-done.5.other_ref), custom_call_target="tpu_custom_call" | custom-call | flops 100000000 | bytes 1000000 | tf_op jit(solution)/shard_map/terms_with_other_core/pallas_call | solution.py:271
  30.9 4.1 %all-to-all-start = ((bf16[8,40,2560]{2,1,0:T(8,128)(2,1)}), bf16[8,40,2560]{2,1,0:T(8,128)(2,1)S(1)}, u32[]{:S(2)}, u32[]{:S(2)}) async-start(bf16[8,40,2560]{2,1,0:T(8,128)(2,1)} %terms_with_other_core.1), calls=%async_computation | async-start | bytes 3276800 | tf_op jit(solution)/shard_map/all_to_all | solution.py:399
  35.0 0.7 collective-permute-done.1.arrived_ref
  35.7 0.1 move_step_2.1
  35.8 8.2 %collective-permute-start.2 = (bf16[128,640]{1,0:T(8,128)(2,1)S(1)}, bf16[128,640]{1,0:T(8,128)(2,1)S(1)}, u32[]{:S(2)}, u32[]{:S(2)}) collective-permute-start(bf16[128,640]{1,0:T(8,128)(2,1)S(1)} %get-tuple-element.38), channel_id=1, source_target_pairs={{0,64},{1,65},{2,66},{3,67},{4,68},{5,69},{6,70},{7,71},{8,72},{9,... | collective-permute-start | bytes 491528 | tf_op jit(solution)/shard_map/ppermute | solution.py:350
  44.0 11.1 %collective-permute-done.2.arrived_ref = bf16[128,640]{1,0:T(8,128)(2,1)S(1)} collective-permute-done((bf16[128,640]{1,0:T(8,128)(2,1)S(1)}, bf16[128,640]{1,0:T(8,128)(2,1)S(1)}, u32[]{:S(2)}, u32[]{:S(2)}) %collective-permute-start.2) | collective-permute-done | bytes 163872 | tf_op jit(solution)/shard_map/ppermute | solution.py:350
  55.1 0.1 move_step_3.1
  55.2 12.2 %collective-permute-start.3 = (bf16[128,640]{1,0:T(8,128)(2,1)S(1)}, bf16[128,640]{1,0:T(8,128)(2,1)S(1)}, u32[]{:S(2)}, u32[]{:S(2)}) collective-permute-start(bf16[128,640]{1,0:T(8,128)(2,1)S(1)} %get-tuple-element.41), channel_id=1, source_target_pairs={{0,128},{1,129},{2,130},{3,131},{4,132},{5,133},{6,134},{7,135},{8... | collective-permute-start | bytes 491528 | tf_op jit(solution)/shard_map/ppermute | solution.py:350
  67.4 0.0 all-to-all-done.parts_ref
  67.4 0.9 group_sum.1
  68.3 8.2 %all-to-all-start.1 = ((bf16[8,112,128]{2,1,0:T(8,128)(2,1)}), bf16[8,112,128]{2,1,0:T(8,128)(2,1)S(1)}, u32[]{:S(2)}, u32[]{:S(2)}) async-start(bf16[8,112,128]{2,1,0:T(8,128)(2,1)} %group_sum.1), calls=%async_computation.1 | async-start | bytes 458752 | tf_op jit(solution)/shard_map/all_to_all | solution.py:402
  76.6 3.4 %collective-permute-done.3.arrived_ref = bf16[128,640]{1,0:T(8,128)(2,1)S(1)} collective-permute-done((bf16[128,640]{1,0:T(8,128)(2,1)S(1)}, bf16[128,640]{1,0:T(8,128)(2,1)S(1)}, u32[]{:S(2)}, u32[]{:S(2)}) %collective-permute-start.3) | collective-permute-done | bytes 163872 | tf_op jit(solution)/shard_map/ppermute | solution.py:350
  80.0 0.1 move_step_4.1
  80.1 0.0 copy-start.6
  80.1 0.7 copy-done.6
  80.8 4.9 %all-to-all-done.1.parts_ref = bf16[8,112,128]{2,1,0:T(8,128)(2,1)S(1)} async-done(((bf16[8,112,128]{2,1,0:T(8,128)(2,1)}), bf16[8,112,128]{2,1,0:T(8,128)(2,1)S(1)}, u32[]{:S(2)}, u32[]{:S(2)}) %all-to-all-start.1) | async-done | bytes 229408 | tf_op jit(solution)/shard_map/all_to_all | solution.py:402
  85.7 0.7 near_sum.1
  86.4 7.2 %all-to-all-start.2 = ((bf16[4,112,128]{2,1,0:T(8,128)(2,1)}), bf16[4,112,128]{2,1,0:T(8,128)(2,1)S(1)}, u32[]{:S(2)}, u32[]{:S(2)}) async-start(bf16[4,112,128]{2,1,0:T(8,128)(2,1)} %near_sum.1), calls=%async_computation.2 | async-start | bytes 229376 | tf_op jit(solution)/shard_map/all_to_all | solution.py:406
  93.6 2.3 %collective-permute-start.4 = (bf16[128,640]{1,0:T(8,128)(2,1)S(1)}, bf16[128,640]{1,0:T(8,128)(2,1)S(1)}, u32[]{:S(2)}, u32[]{:S(2)}) collective-permute-start(bf16[128,640]{1,0:T(8,128)(2,1)S(1)} %get-tuple-element.46), channel_id=1, source_target_pairs={{0,256},{1,257},{2,258},{3,259},{4,260},{5,261},{6,262},{7,263},{8... | collective-permute-start | bytes 491528 | tf_op jit(solution)/shard_map/ppermute | solution.py:350
  95.9 9.6 %all-to-all-done.2.parts_ref = bf16[4,112,128]{2,1,0:T(8,128)(2,1)S(1)} async-done(((bf16[4,112,128]{2,1,0:T(8,128)(2,1)}), bf16[4,112,128]{2,1,0:T(8,128)(2,1)S(1)}, u32[]{:S(2)}, u32[]{:S(2)}) %all-to-all-start.2) | async-done | bytes 114720 | tf_op jit(solution)/shard_map/all_to_all | solution.py:406
  105.5 0.7 mean.1
  106.3 6.5 %all-to-all-start.3 = ((bf16[8,112,128]{2,1,0:T(8,128)(2,1)}), bf16[8,112,128]{2,1,0:T(8,128)(2,1)S(1)}, u32[]{:S(2)}, u32[]{:S(2)}) async-start(bf16[8,112,128]{2,1,0:T(8,128)(2,1)} %mean.1), calls=%async_computation.3 | async-start | bytes 458752 | tf_op jit(solution)/shard_map/all_to_all | solution.py:408
  112.7 0.0 collective-permute-done.4.arrived_hbm
  112.7 6.0 %all-gather.2.cloned.1.call-done.w_hbm = bf16[640,5120]{1,0:T(8,128)(2,1)} async-done(((bf16[40,5120]{1,0:T(8,128)(2,1)}), bf16[640,5120]{1,0:T(8,128)(2,1)}) %all-gather.2.cloned.1.call-update) | async-done | bytes 6553616 | tf_op jit(solution)/shard_map/all_gather | solution.py:387
  118.7 8.3 %outputs.1 = (bf16[256,896]{1,0:T(8,128)(2,1)}, bf16[256,2560]{1,0:T(8,128)(2,1)}) custom-call(s32[8,128]{1,0:T(8,128)} %get-tuple-element.30.table_ref.live_ref, s32[1,128]{1,0:T(1,128)} %copy-done.9, bf16[256,896]{1,0:T(8,128)(2,1)} %x_hbm.1, f32[2,640,128]{2,1,0:T(8,128)} %copy-done.3, bf16[256,2560]{1,0:T(8,128)(2,1)} %g_ref.3, ...), custom_call_target="tpu_custom_call" | custom-call | flops 8000000000 | tf_op jit(solution)/shard_map/outputs/pallas_call | solution.py:237
  127.0 0.0 all-to-all-done.3.shares_ref
  127.0 0.7 join.1
  (13 shorter events, 0.0 us)
Async XLA Ops:
  7.2 7.7 %copy-start.1 = (bf16[256,896]{1,0:T(8,128)(2,1)S(1)}, bf16[256,896]{1,0:T(8,128)(2,1)}, u32[]{:S(2)}) copy-start(bf16[256,896]{1,0:T(8,128)(2,1)} %x_hbm.1) | copy-start | bytes 1376260
  7.2 7.7 %copy-start.2 = (s32[256]{0:T(256)S(1)}, s32[256]{0:T(256)}, u32[]{:S(2)}) copy-start(s32[256]{0:T(256)} %param.12) | copy-start | bytes 3076
  7.2 111.5 %all-gather.2.cloned.1.call-start = ((), (), s32[]{:S(2)}) async-start(), calls=%async_computation.4 | async-start | bytes 6963200 | tf_op jit(solution)/shard_map/all_gather | solution.py:387
  9.1 8.2 %copy-start = (bf16[256,2560]{1,0:T(8,128)(2,1)S(1)}, bf16[256,2560]{1,0:T(8,128)(2,1)}, u32[]{:S(2)}) copy-start(bf16[256,2560]{1,0:T(8,128)(2,1)} %g_ref.3) | copy-start | bytes 3932164
  12.7 13.3 %collective-permute-start = (bf16[128,640]{1,0:T(8,128)(2,1)}, bf16[128,640]{1,0:T(8,128)(2,1)S(1)}, u32[]{:S(2)}, u32[]{:S(2)}) collective-permute-start(bf16[128,640]{1,0:T(8,128)(2,1)} %get-tuple-element.32), channel_id=1, source_target_pairs={{0,16},{1,17},{2,18},{3,19},{4,20},{5,21},{6,22},{7,23},{8,24},{9,... | collective-permute-start | bytes 491528 | tf_op jit(solution)/shard_map/ppermute | solution.py:350
  16.3 0.9 copy-start.3
  17.3 8.7 %copy-start.4 = (bf16[256,640]{1,0:T(8,128)(2,1)S(1)}, bf16[256,640]{1,0:T(8,128)(2,1)}, u32[]{:S(2)}) copy-start(bf16[256,640]{1,0:T(8,128)(2,1)} %get-tuple-element.31.slots_ref) | copy-start | bytes 983044
  17.3 8.7 %copy-start.5 = (s32[8,128]{1,0:T(8,128)S(1)}, s32[8,128]{1,0:T(8,128)}, u32[]{:S(2)}) copy-start(s32[8,128]{1,0:T(8,128)} %get-tuple-element.30.table_ref.live_ref) | copy-start | bytes 12292
  17.9 11.2 %collective-permute-start.5 = (bf16[320,2560]{1,0:T(8,128)(2,1)S(1)}, bf16[320,2560]{1,0:T(8,128)(2,1)S(1)}, u32[]{:S(2)}, u32[]{:S(2)}) collective-permute-start(bf16[320,2560]{1,0:T(8,128)(2,1)S(1)} %terms_to_send.1), channel_id=1, source_target_pairs={{0,1},{1,0},{2,3},{3,2},{4,5},{5,4},{6,7},{7,6},{8,9},{9,8},{10,11... | collective-permute-start | bytes 4915208 | tf_op jit(solution)/shard_map/ppermute | solution.py:396
  26.1 0.7 copy-start.7
  26.8 8.9 %collective-permute-start.1 = (bf16[128,640]{1,0:T(8,128)(2,1)S(1)}, bf16[128,640]{1,0:T(8,128)(2,1)S(1)}, u32[]{:S(2)}, u32[]{:S(2)}) collective-permute-start(bf16[128,640]{1,0:T(8,128)(2,1)S(1)} %get-tuple-element.35), channel_id=1, source_target_pairs={{0,32},{1,33},{2,34},{3,35},{4,36},{5,37},{6,38},{7,39},{8,40},{9,... | collective-permute-start | bytes 491528 | tf_op jit(solution)/shard_map/ppermute | solution.py:350
  30.9 4.8 %copy-start.8 = (bf16[256,640]{1,0:T(8,128)(2,1)S(1)}, bf16[256,640]{1,0:T(8,128)(2,1)}, u32[]{:S(2)}) copy-start(bf16[256,640]{1,0:T(8,128)(2,1)} %copy-done.7) | copy-start | bytes 983044
  30.9 36.5 %all-to-all-start = ((bf16[8,40,2560]{2,1,0:T(8,128)(2,1)}), bf16[8,40,2560]{2,1,0:T(8,128)(2,1)S(1)}, u32[]{:S(2)}, u32[]{:S(2)}) async-start(bf16[8,40,2560]{2,1,0:T(8,128)(2,1)} %terms_with_other_core.1), calls=%async_computation | async-start | bytes 3276800 | tf_op jit(solution)/shard_map/all_to_all | solution.py:399
  35.8 19.3 %collective-permute-start.2 = (bf16[128,640]{1,0:T(8,128)(2,1)S(1)}, bf16[128,640]{1,0:T(8,128)(2,1)S(1)}, u32[]{:S(2)}, u32[]{:S(2)}) collective-permute-start(bf16[128,640]{1,0:T(8,128)(2,1)S(1)} %get-tuple-element.38), channel_id=1, source_target_pairs={{0,64},{1,65},{2,66},{3,67},{4,68},{5,69},{6,70},{7,71},{8,72},{9,... | collective-permute-start | bytes 491528 | tf_op jit(solution)/shard_map/ppermute | solution.py:350
  55.2 24.8 %collective-permute-start.3 = (bf16[128,640]{1,0:T(8,128)(2,1)S(1)}, bf16[128,640]{1,0:T(8,128)(2,1)S(1)}, u32[]{:S(2)}, u32[]{:S(2)}) collective-permute-start(bf16[128,640]{1,0:T(8,128)(2,1)S(1)} %get-tuple-element.41), channel_id=1, source_target_pairs={{0,128},{1,129},{2,130},{3,131},{4,132},{5,133},{6,134},{7,135},{8... | collective-permute-start | bytes 491528 | tf_op jit(solution)/shard_map/ppermute | solution.py:350
  68.3 17.4 %all-to-all-start.1 = ((bf16[8,112,128]{2,1,0:T(8,128)(2,1)}), bf16[8,112,128]{2,1,0:T(8,128)(2,1)S(1)}, u32[]{:S(2)}, u32[]{:S(2)}) async-start(bf16[8,112,128]{2,1,0:T(8,128)(2,1)} %group_sum.1), calls=%async_computation.1 | async-start | bytes 458752 | tf_op jit(solution)/shard_map/all_to_all | solution.py:402
  80.1 0.7 copy-start.6
  80.8 37.9 %copy-start.9 = (s32[1,128]{1,0:T(1,128)}, s32[1,128]{1,0:T(1,128)S(1)}, u32[]{:S(2)}) copy-start(s32[1,128]{1,0:T(1,128)S(1)} %get-tuple-element.42.live_ref) | copy-start | bytes 1540
  86.4 19.1 %all-to-all-start.2 = ((bf16[4,112,128]{2,1,0:T(8,128)(2,1)}), bf16[4,112,128]{2,1,0:T(8,128)(2,1)S(1)}, u32[]{:S(2)}, u32[]{:S(2)}) async-start(bf16[4,112,128]{2,1,0:T(8,128)(2,1)} %near_sum.1), calls=%async_computation.2 | async-start | bytes 229376 | tf_op jit(solution)/shard_map/all_to_all | solution.py:406
  93.6 19.1 %collective-permute-start.4 = (bf16[128,640]{1,0:T(8,128)(2,1)S(1)}, bf16[128,640]{1,0:T(8,128)(2,1)S(1)}, u32[]{:S(2)}, u32[]{:S(2)}) collective-permute-start(bf16[128,640]{1,0:T(8,128)(2,1)S(1)} %get-tuple-element.46), channel_id=1, source_target_pairs={{0,256},{1,257},{2,258},{3,259},{4,260},{5,261},{6,262},{7,263},{8... | collective-permute-start | bytes 491528 | tf_op jit(solution)/shard_map/ppermute | solution.py:350
  106.3 20.7 %all-to-all-start.3 = ((bf16[8,112,128]{2,1,0:T(8,128)(2,1)}), bf16[8,112,128]{2,1,0:T(8,128)(2,1)S(1)}, u32[]{:S(2)}, u32[]{:S(2)}) async-start(bf16[8,112,128]{2,1,0:T(8,128)(2,1)} %mean.1), calls=%async_computation.3 | async-start | bytes 458752 | tf_op jit(solution)/shard_map/all_to_all | solution.py:408
  112.7 6.0 %copy-start.10 = (bf16[128,640]{1,0:T(8,128)(2,1)}, bf16[128,640]{1,0:T(8,128)(2,1)S(1)}, u32[]{:S(2)}) copy-start(bf16[128,640]{1,0:T(8,128)(2,1)S(1)} %collective-permute-done.4.arrived_hbm) | copy-start | bytes 491524
Sparse Core Ops, SparseCore 0:
  11.9 106.7 all-gather.1

commit v6 on v5

--- a/solution.py
+++ b/solution.py
@@ -193,6 +193,23 @@
     for copy, (i, j) in zip(policy_copies, POLICY_PARTS):
         copy.wait()
         ga_ref[:, i:j] = dot(g_ref[...], w_ref[i:j, :D], NT).astype(jnp.bfloat16)
+    slots_copy.wait()
+    arrived_copy.wait()
+    live = move(level, live_ref[0:1, :], table_ref, slots_ref, None, arrived_ref, moved_ref)
+    for columns in column_blocks(moved_ref):
+        for s in range(SLOT_NUMBER):
+            rows = slice(s * ALIGNED_ROWS, (s + 1) * ALIGNED_ROWS)
+            block = moved_ref[rows, columns]
+            alive = jnp.broadcast_to(live, block.shape) > s
+            moved_ref[rows, columns] = jnp.where(alive, block, jnp.zeros_like(block))
+    out_copies = []
+    for n, (copy, (i, j)) in enumerate(zip(frozen_copies, FROZEN_PARTS)):
+        copy.wait()
+        frozen_ref[:, i:j] = dot(moved_ref[...], w_ref[:, D + i : D + j], NN).astype(jnp.bfloat16)
+        out_copies.append(
+            pltpu.make_async_copy(frozen_ref.at[:, pl.ds(i, j - i)], frozen_hbm.at[:, pl.ds(i, j - i)], out_sems.at[1 + n])
+        )
+        out_copies[-1].start()
     x_copy.wait()
     prob_copy.wait()
     for b in range(2):
@@ -210,23 +227,6 @@
         grad_ref[rows, QW + HD :] = dot(p.astype(jnp.bfloat16), ga, TN).astype(jnp.bfloat16)
     grad_copy = pltpu.make_async_copy(grad_ref, grad_hbm, out_sems.at[0])
     grad_copy.start()
-    slots_copy.wait()
-    arrived_copy.wait()
-    live = move(level, live_ref[0:1, :], table_ref, slots_ref, None, arrived_ref, moved_ref)
-    for columns in column_blocks(moved_ref):
-        for s in range(SLOT_NUMBER):
-            rows = slice(s * ALIGNED_ROWS, (s + 1) * ALIGNED_ROWS)
-            block = moved_ref[rows, columns]
-            alive = jnp.broadcast_to(live, block.shape) > s
-            moved_ref[rows, columns] = jnp.where(alive, block, jnp.zeros_like(block))
-    out_copies = []
-    for n, (copy, (i, j)) in enumerate(zip(frozen_copies, FROZEN_PARTS)):
-        copy.wait()
-        frozen_ref[:, i:j] = dot(moved_ref[...], w_ref[:, D + i : D + j], NN).astype(jnp.bfloat16)
-        out_copies.append(
-            pltpu.make_async_copy(frozen_ref.at[:, pl.ds(i, j - i)], frozen_hbm.at[:, pl.ds(i, j - i)], out_sems.at[1 + n])
-        )
-        out_copies[-1].start()
     for copy in (grad_copy, *out_copies):
         copy.wait()
 

time: 135 us -> 135 us (level)
  no operation moved by 1% of the time
where the time goes in v6:
time: 135 us
  starting transfers between devices  60.5 us (45%)
  waiting for transfers between devices  36.1 us (27%)
  Pallas kernels  20.3 us (15%)
  between operations  15 us (11%)
  local copies, waits for them, and re-layouts  2.4 us (2%)
    ppermute x5, starting transfers between devices, swap(): return lax.ppermute(a, ('dp', 'fsdp'), all_pairs(dp_flip, fsdp_flip))  26.5 us
    ppermute x5, waiting for transfers between devices, swap(): return lax.ppermute(a, ('dp', 'fsdp'), all_pairs(dp_flip, fsdp_flip))  15.2 us
    all_to_all x2, starting transfers between devices, body(): shares = lax.all_to_all(shares, 'dp', 0, 0, axis_index_groups=near)  14.7 us
    all_to_all x1, waiting for transfers between devices, body(): shares = lax.all_to_all(shares, 'dp', 0, 0, axis_index_groups=far)  9.62 us
    pallas_call x1, Pallas kernels, outputs(): call(functools.partial(outputs_kernel, level), (bf16(*qkv.shape), bf16(ro...  8.26 us
    ppermute x1, starting transfers between devices, body(): lax.ppermute(terms_to_send(send_half, grad_output), 'fsdp', fsdp_pairs(1,...  8.05 us
    all_to_all x1, starting transfers between devices, body(): shares = lax.all_to_all(shares, 'dp', 0, 0, axis_index_groups=far)  7.17 us
    all_gather x1, waiting for transfers between devices, body(): weights = lax.all_gather(own, 'fsdp', axis=0, tiled=True)  5.97 us
  transfers between devices with their start and end apart: 11, of which 7 were waited for; matrix products, arithmetic and copies ran while one was open for 0% of the time, Pallas kernels for 13%

profile of v6, /device:TPU:33, one launch (start us, length us, event | category | flops | bytes accessed | tf_op | source)
XLA Modules:
  0.0 134.6 jit_solution(12487362092707091602)
XLA Ops:
  7.2 0.0 copy-start.1
  7.2 0.0 copy-start.2
  7.2 0.0 all-gather.2.cloned.1.call-start
  7.2 1.8 %side_by_side.1 = bf16[40,5120]{1,0:T(8,128)(2,1)} custom-call(bf16[40,2560]{1,0:T(8,128)(2,1)} %left.1, bf16[40,2560]{1,0:T(8,128)(2,1)} %right.1), custom_call_target="tpu_custom_call" | custom-call | flops 100000000 | bytes 1000000 | tf_op jit(solution)/shard_map/side_by_side/pallas_call | solution.py:332
  9.1 0.0 all-gather.2.cloned.1.call-update
  9.9 2.8 %next_attention.1 = (bf16[256,640]{1,0:T(8,128)(2,1)}, bf16[128,640]{1,0:T(8,128)(2,1)}, s32[8,128]{1,0:T(8,128)}) custom-call(s32[1,1]{1,0:T(1,128)S(6)} %copy.12.live_ref, s32[1,1,5]{2,1,0:T(1,128)} %plan_ref.1, bf16[256,896]{1,0:T(8,128)(2,1)} %x_ref, s32[2,128]{1,0:T(2,128)} %bitcast.3), custom_call_target="tpu_custom_call" | custom-call | flops 100000000 | bytes 1000000 | tf_op jit(solution)/shard_map/next_attention/pallas_call | solution.py:130
  12.7 1.9 %collective-permute-start = (bf16[128,640]{1,0:T(8,128)(2,1)}, bf16[128,640]{1,0:T(8,128)(2,1)S(1)}, u32[]{:S(2)}, u32[]{:S(2)}) collective-permute-start(bf16[128,640]{1,0:T(8,128)(2,1)} %get-tuple-element.32), channel_id=1, source_target_pairs={{0,16},{1,17},{2,18},{3,19},{4,20},{5,21},{6,22},{7,23},{8,24},{9,... | collective-permute-start | bytes 491528 | tf_op jit(solution)/shard_map/ppermute | solution.py:350
  14.6 0.2 fusion.order_ref
  14.8 0.0 copy-done.1
  14.8 0.0 copy-done.2
  14.9 1.5 %current_attention.1 = (bf16[256,320]{1,0:T(8,128)(2,1)S(1)}, bf16[256,320]{1,0:T(8,128)(2,1)S(1)}, f32[2,640,128]{2,1,0:T(8,128)S(1)}) custom-call(bf16[256,896]{1,0:T(8,128)(2,1)S(1)} %copy-done.1, s32[2,128]{1,0:T(2,128)S(1)} %bitcast.2, bf16[640,640]{1,0:T(8,128)(2,1)S(1)} %fusion.order_ref), custom_call_target="tpu_custom_call" | custom-call | flops 100000000 | bytes 1000000 | tf_op jit(solution)/shard_map/current_attention/pallas_call | solution.py:160
  16.3 0.0 copy-start.3
  16.4 0.9 copy-done.3
  17.3 0.0 copy-done
  17.3 0.6 terms_to_send.1
  17.9 8.1 %collective-permute-start.5 = (bf16[320,2560]{1,0:T(8,128)(2,1)S(1)}, bf16[320,2560]{1,0:T(8,128)(2,1)S(1)}, u32[]{:S(2)}, u32[]{:S(2)}) collective-permute-start(bf16[320,2560]{1,0:T(8,128)(2,1)S(1)} %terms_to_send.1), channel_id=1, source_target_pairs={{0,1},{1,0},{2,3},{3,2},{4,5},{5,4},{6,7},{7,6},{8,9},{9,8},{10,11... | collective-permute-start | bytes 4915208 | tf_op jit(solution)/shard_map/ppermute | solution.py:396
  26.0 0.0 collective-permute-done.arrived_ref
  26.0 0.1 move_step_1.1
  26.1 0.0 copy-start.7
  26.1 0.7 copy-done.7
  26.8 1.9 %collective-permute-start.1 = (bf16[128,640]{1,0:T(8,128)(2,1)S(1)}, bf16[128,640]{1,0:T(8,128)(2,1)S(1)}, u32[]{:S(2)}, u32[]{:S(2)}) collective-permute-start(bf16[128,640]{1,0:T(8,128)(2,1)S(1)} %get-tuple-element.35), channel_id=1, source_target_pairs={{0,32},{1,33},{2,34},{3,35},{4,36},{5,37},{6,38},{7,39},{8,40},{9,... | collective-permute-start | bytes 491528 | tf_op jit(solution)/shard_map/ppermute | solution.py:350
  28.8 0.3 collective-permute-done.5.other_ref
  29.1 1.9 %terms_with_other_core.1 = bf16[8,40,2560]{2,1,0:T(8,128)(2,1)} custom-call(bf16[256,320]{1,0:T(8,128)(2,1)S(1)} %get-tuple-element.48.a_ref, bf16[256,2560]{1,0:T(8,128)(2,1)S(1)} %copy-done, bf16[320,2560]{1,0:T(8,128)(2,1)S(1)} %collective-permute-done.5.other_ref), custom_call_target="tpu_custom_call" | custom-call | flops 100000000 | bytes 1000000 | tf_op jit(solution)/shard_map/terms_with_other_core/pallas_call | solution.py:271
  30.9 4.1 %all-to-all-start = ((bf16[8,40,2560]{2,1,0:T(8,128)(2,1)}), bf16[8,40,2560]{2,1,0:T(8,128)(2,1)S(1)}, u32[]{:S(2)}, u32[]{:S(2)}) async-start(bf16[8,40,2560]{2,1,0:T(8,128)(2,1)} %terms_with_other_core.1), calls=%async_computation | async-start | bytes 3276800 | tf_op jit(solution)/shard_map/all_to_all | solution.py:399
  35.0 0.7 collective-permute-done.1.arrived_ref
  35.7 0.1 move_step_2.1
  35.8 8.2 %collective-permute-start.2 = (bf16[128,640]{1,0:T(8,128)(2,1)S(1)}, bf16[128,640]{1,0:T(8,128)(2,1)S(1)}, u32[]{:S(2)}, u32[]{:S(2)}) collective-permute-start(bf16[128,640]{1,0:T(8,128)(2,1)S(1)} %get-tuple-element.38), channel_id=1, source_target_pairs={{0,64},{1,65},{2,66},{3,67},{4,68},{5,69},{6,70},{7,71},{8,72},{9,... | collective-permute-start | bytes 491528 | tf_op jit(solution)/shard_map/ppermute | solution.py:350
  44.0 11.1 %collective-permute-done.2.arrived_ref = bf16[128,640]{1,0:T(8,128)(2,1)S(1)} collective-permute-done((bf16[128,640]{1,0:T(8,128)(2,1)S(1)}, bf16[128,640]{1,0:T(8,128)(2,1)S(1)}, u32[]{:S(2)}, u32[]{:S(2)}) %collective-permute-start.2) | collective-permute-done | bytes 163872 | tf_op jit(solution)/shard_map/ppermute | solution.py:350
  55.1 0.1 move_step_3.1
  55.2 12.2 %collective-permute-start.3 = (bf16[128,640]{1,0:T(8,128)(2,1)S(1)}, bf16[128,640]{1,0:T(8,128)(2,1)S(1)}, u32[]{:S(2)}, u32[]{:S(2)}) collective-permute-start(bf16[128,640]{1,0:T(8,128)(2,1)S(1)} %get-tuple-element.41), channel_id=1, source_target_pairs={{0,128},{1,129},{2,130},{3,131},{4,132},{5,133},{6,134},{7,135},{8... | collective-permute-start | bytes 491528 | tf_op jit(solution)/shard_map/ppermute | solution.py:350
  67.4 0.0 all-to-all-done.parts_ref
  67.4 0.9 group_sum.1
  68.3 8.2 %all-to-all-start.1 = ((bf16[8,112,128]{2,1,0:T(8,128)(2,1)}), bf16[8,112,128]{2,1,0:T(8,128)(2,1)S(1)}, u32[]{:S(2)}, u32[]{:S(2)}) async-start(bf16[8,112,128]{2,1,0:T(8,128)(2,1)} %group_sum.1), calls=%async_computation.1 | async-start | bytes 458752 | tf_op jit(solution)/shard_map/all_to_all | solution.py:402
  76.6 3.4 %collective-permute-done.3.arrived_ref = bf16[128,640]{1,0:T(8,128)(2,1)S(1)} collective-permute-done((bf16[128,640]{1,0:T(8,128)(2,1)S(1)}, bf16[128,640]{1,0:T(8,128)(2,1)S(1)}, u32[]{:S(2)}, u32[]{:S(2)}) %collective-permute-start.3) | collective-permute-done | bytes 163872 | tf_op jit(solution)/shard_map/ppermute | solution.py:350
  80.0 0.1 move_step_4.1
  80.1 0.7 copy-done.6
  80.8 4.9 %all-to-all-done.1.parts_ref = bf16[8,112,128]{2,1,0:T(8,128)(2,1)S(1)} async-done(((bf16[8,112,128]{2,1,0:T(8,128)(2,1)}), bf16[8,112,128]{2,1,0:T(8,128)(2,1)S(1)}, u32[]{:S(2)}, u32[]{:S(2)}) %all-to-all-start.1) | async-done | bytes 229408 | tf_op jit(solution)/shard_map/all_to_all | solution.py:402
  85.7 0.7 near_sum.1
  86.4 7.2 %all-to-all-start.2 = ((bf16[4,112,128]{2,1,0:T(8,128)(2,1)}), bf16[4,112,128]{2,1,0:T(8,128)(2,1)S(1)}, u32[]{:S(2)}, u32[]{:S(2)}) async-start(bf16[4,112,128]{2,1,0:T(8,128)(2,1)} %near_sum.1), calls=%async_computation.2 | async-start | bytes 229376 | tf_op jit(solution)/shard_map/all_to_all | solution.py:406
  93.6 2.3 %collective-permute-start.4 = (bf16[128,640]{1,0:T(8,128)(2,1)S(1)}, bf16[128,640]{1,0:T(8,128)(2,1)S(1)}, u32[]{:S(2)}, u32[]{:S(2)}) collective-permute-start(bf16[128,640]{1,0:T(8,128)(2,1)S(1)} %get-tuple-element.46), channel_id=1, source_target_pairs={{0,256},{1,257},{2,258},{3,259},{4,260},{5,261},{6,262},{7,263},{8... | collective-permute-start | bytes 491528 | tf_op jit(solution)/shard_map/ppermute | solution.py:350
  95.9 9.6 %all-to-all-done.2.parts_ref = bf16[4,112,128]{2,1,0:T(8,128)(2,1)S(1)} async-done(((bf16[4,112,128]{2,1,0:T(8,128)(2,1)}), bf16[4,112,128]{2,1,0:T(8,128)(2,1)S(1)}, u32[]{:S(2)}, u32[]{:S(2)}) %all-to-all-start.2) | async-done | bytes 114720 | tf_op jit(solution)/shard_map/all_to_all | solution.py:406
  105.5 0.7 mean.1
  106.3 6.5 %all-to-all-start.3 = ((bf16[8,112,128]{2,1,0:T(8,128)(2,1)}), bf16[8,112,128]{2,1,0:T(8,128)(2,1)S(1)}, u32[]{:S(2)}, u32[]{:S(2)}) async-start(bf16[8,112,128]{2,1,0:T(8,128)(2,1)} %mean.1), calls=%async_computation.3 | async-start | bytes 458752 | tf_op jit(solution)/shard_map/all_to_all | solution.py:408
  112.7 0.0 collective-permute-done.4.arrived_hbm
  112.7 6.0 %all-gather.2.cloned.1.call-done.w_hbm = bf16[640,5120]{1,0:T(8,128)(2,1)} async-done(((bf16[40,5120]{1,0:T(8,128)(2,1)}), bf16[640,5120]{1,0:T(8,128)(2,1)}) %all-gather.2.cloned.1.call-update) | async-done | bytes 6553616 | tf_op jit(solution)/shard_map/all_gather | solution.py:387
  118.7 8.3 %outputs.1 = (bf16[256,896]{1,0:T(8,128)(2,1)}, bf16[256,2560]{1,0:T(8,128)(2,1)}) custom-call(s32[8,128]{1,0:T(8,128)} %get-tuple-element.30.table_ref.live_ref, s32[1,128]{1,0:T(1,128)} %copy-done.9, bf16[256,896]{1,0:T(8,128)(2,1)} %x_hbm.1, f32[2,640,128]{2,1,0:T(8,128)} %copy-done.3, bf16[256,2560]{1,0:T(8,128)(2,1)} %g_ref.3, ...), custom_call_target="tpu_custom_call" | custom-call | flops 8000000000 | tf_op jit(solution)/shard_map/outputs/pallas_call | solution.py:237
  127.0 0.0 all-to-all-done.3.shares_ref
  127.0 0.7 join.1
  (13 shorter events, 0.0 us)
Async XLA Ops:
  7.2 7.7 %copy-start.1 = (bf16[256,896]{1,0:T(8,128)(2,1)S(1)}, bf16[256,896]{1,0:T(8,128)(2,1)}, u32[]{:S(2)}) copy-start(bf16[256,896]{1,0:T(8,128)(2,1)} %x_hbm.1) | copy-start | bytes 1376260
  7.2 7.7 %copy-start.2 = (s32[256]{0:T(256)S(1)}, s32[256]{0:T(256)}, u32[]{:S(2)}) copy-start(s32[256]{0:T(256)} %param.12) | copy-start | bytes 3076
  7.2 111.5 %all-gather.2.cloned.1.call-start = ((), (), s32[]{:S(2)}) async-start(), calls=%async_computation.4 | async-start | bytes 6963200 | tf_op jit(solution)/shard_map/all_gather | solution.py:387
  9.1 8.2 %copy-start = (bf16[256,2560]{1,0:T(8,128)(2,1)S(1)}, bf16[256,2560]{1,0:T(8,128)(2,1)}, u32[]{:S(2)}) copy-start(bf16[256,2560]{1,0:T(8,128)(2,1)} %g_ref.3) | copy-start | bytes 3932164
  12.7 13.3 %collective-permute-start = (bf16[128,640]{1,0:T(8,128)(2,1)}, bf16[128,640]{1,0:T(8,128)(2,1)S(1)}, u32[]{:S(2)}, u32[]{:S(2)}) collective-permute-start(bf16[128,640]{1,0:T(8,128)(2,1)} %get-tuple-element.32), channel_id=1, source_target_pairs={{0,16},{1,17},{2,18},{3,19},{4,20},{5,21},{6,22},{7,23},{8,24},{9,... | collective-permute-start | bytes 491528 | tf_op jit(solution)/shard_map/ppermute | solution.py:350
  16.3 0.9 copy-start.3
  17.3 8.7 %copy-start.4 = (bf16[256,640]{1,0:T(8,128)(2,1)S(1)}, bf16[256,640]{1,0:T(8,128)(2,1)}, u32[]{:S(2)}) copy-start(bf16[256,640]{1,0:T(8,128)(2,1)} %get-tuple-element.31.slots_ref) | copy-start | bytes 983044
  17.3 8.7 %copy-start.5 = (s32[8,128]{1,0:T(8,128)S(1)}, s32[8,128]{1,0:T(8,128)}, u32[]{:S(2)}) copy-start(s32[8,128]{1,0:T(8,128)} %get-tuple-element.30.table_ref.live_ref) | copy-start | bytes 12292
  17.9 11.2 %collective-permute-start.5 = (bf16[320,2560]{1,0:T(8,128)(2,1)S(1)}, bf16[320,2560]{1,0:T(8,128)(2,1)S(1)}, u32[]{:S(2)}, u32[]{:S(2)}) collective-permute-start(bf16[320,2560]{1,0:T(8,128)(2,1)S(1)} %terms_to_send.1), channel_id=1, source_target_pairs={{0,1},{1,0},{2,3},{3,2},{4,5},{5,4},{6,7},{7,6},{8,9},{9,8},{10,11... | collective-permute-start | bytes 4915208 | tf_op jit(solution)/shard_map/ppermute | solution.py:396
  26.1 0.7 copy-start.7
  26.8 8.9 %collective-permute-start.1 = (bf16[128,640]{1,0:T(8,128)(2,1)S(1)}, bf16[128,640]{1,0:T(8,128)(2,1)S(1)}, u32[]{:S(2)}, u32[]{:S(2)}) collective-permute-start(bf16[128,640]{1,0:T(8,128)(2,1)S(1)} %get-tuple-element.35), channel_id=1, source_target_pairs={{0,32},{1,33},{2,34},{3,35},{4,36},{5,37},{6,38},{7,39},{8,40},{9,... | collective-permute-start | bytes 491528 | tf_op jit(solution)/shard_map/ppermute | solution.py:350
  30.9 4.8 %copy-start.8 = (bf16[256,640]{1,0:T(8,128)(2,1)S(1)}, bf16[256,640]{1,0:T(8,128)(2,1)}, u32[]{:S(2)}) copy-start(bf16[256,640]{1,0:T(8,128)(2,1)} %copy-done.7) | copy-start | bytes 983044
  30.9 36.5 %all-to-all-start = ((bf16[8,40,2560]{2,1,0:T(8,128)(2,1)}), bf16[8,40,2560]{2,1,0:T(8,128)(2,1)S(1)}, u32[]{:S(2)}, u32[]{:S(2)}) async-start(bf16[8,40,2560]{2,1,0:T(8,128)(2,1)} %terms_with_other_core.1), calls=%async_computation | async-start | bytes 3276800 | tf_op jit(solution)/shard_map/all_to_all | solution.py:399
  35.8 19.3 %collective-permute-start.2 = (bf16[128,640]{1,0:T(8,128)(2,1)S(1)}, bf16[128,640]{1,0:T(8,128)(2,1)S(1)}, u32[]{:S(2)}, u32[]{:S(2)}) collective-permute-start(bf16[128,640]{1,0:T(8,128)(2,1)S(1)} %get-tuple-element.38), channel_id=1, source_target_pairs={{0,64},{1,65},{2,66},{3,67},{4,68},{5,69},{6,70},{7,71},{8,72},{9,... | collective-permute-start | bytes 491528 | tf_op jit(solution)/shard_map/ppermute | solution.py:350
  55.2 24.8 %collective-permute-start.3 = (bf16[128,640]{1,0:T(8,128)(2,1)S(1)}, bf16[128,640]{1,0:T(8,128)(2,1)S(1)}, u32[]{:S(2)}, u32[]{:S(2)}) collective-permute-start(bf16[128,640]{1,0:T(8,128)(2,1)S(1)} %get-tuple-element.41), channel_id=1, source_target_pairs={{0,128},{1,129},{2,130},{3,131},{4,132},{5,133},{6,134},{7,135},{8... | collective-permute-start | bytes 491528 | tf_op jit(solution)/shard_map/ppermute | solution.py:350
  68.3 17.4 %all-to-all-start.1 = ((bf16[8,112,128]{2,1,0:T(8,128)(2,1)}), bf16[8,112,128]{2,1,0:T(8,128)(2,1)S(1)}, u32[]{:S(2)}, u32[]{:S(2)}) async-start(bf16[8,112,128]{2,1,0:T(8,128)(2,1)} %group_sum.1), calls=%async_computation.1 | async-start | bytes 458752 | tf_op jit(solution)/shard_map/all_to_all | solution.py:402
  80.1 0.7 copy-start.6
  80.8 37.9 %copy-start.9 = (s32[1,128]{1,0:T(1,128)}, s32[1,128]{1,0:T(1,128)S(1)}, u32[]{:S(2)}) copy-start(s32[1,128]{1,0:T(1,128)S(1)} %get-tuple-element.42.live_ref) | copy-start | bytes 1540
  86.4 19.1 %all-to-all-start.2 = ((bf16[4,112,128]{2,1,0:T(8,128)(2,1)}), bf16[4,112,128]{2,1,0:T(8,128)(2,1)S(1)}, u32[]{:S(2)}, u32[]{:S(2)}) async-start(bf16[4,112,128]{2,1,0:T(8,128)(2,1)} %near_sum.1), calls=%async_computation.2 | async-start | bytes 229376 | tf_op jit(solution)/shard_map/all_to_all | solution.py:406
  93.6 19.1 %collective-permute-start.4 = (bf16[128,640]{1,0:T(8,128)(2,1)S(1)}, bf16[128,640]{1,0:T(8,128)(2,1)S(1)}, u32[]{:S(2)}, u32[]{:S(2)}) collective-permute-start(bf16[128,640]{1,0:T(8,128)(2,1)S(1)} %get-tuple-element.46), channel_id=1, source_target_pairs={{0,256},{1,257},{2,258},{3,259},{4,260},{5,261},{6,262},{7,263},{8... | collective-permute-start | bytes 491528 | tf_op jit(solution)/shard_map/ppermute | solution.py:350
  106.3 20.7 %all-to-all-start.3 = ((bf16[8,112,128]{2,1,0:T(8,128)(2,1)}), bf16[8,112,128]{2,1,0:T(8,128)(2,1)S(1)}, u32[]{:S(2)}, u32[]{:S(2)}) async-start(bf16[8,112,128]{2,1,0:T(8,128)(2,1)} %mean.1), calls=%async_computation.3 | async-start | bytes 458752 | tf_op jit(solution)/shard_map/all_to_all | solution.py:408
  112.7 6.0 %copy-start.10 = (bf16[128,640]{1,0:T(8,128)(2,1)}, bf16[128,640]{1,0:T(8,128)(2,1)S(1)}, u32[]{:S(2)}) copy-start(bf16[128,640]{1,0:T(8,128)(2,1)S(1)} %collective-permute-done.4.arrived_hbm) | copy-start | bytes 491524
Sparse Core Ops, SparseCore 0:
  11.9 106.7 all-gather.1
